TPU v7x, 512 devices: a whole 4x8x8 slice. The times are simulated.
512 devices in a mesh: gz: 16 (over y, core), xy: 32 (over x, z).
Axes of the slice: x: 4, y: 8, z: 8, core: 2. Of those that a mesh axis runs over, the one named last changes fastest.
Arguments:
- design: float32 [128, 512, 1024], P('gz', 'xy'), may hold values from 0 to 1
Outputs:
- blueprint: float32 [128, 512, 1024], P('gz', 'xy')
- printed: float32 [128, 512, 1024], P('gz', 'xy')
All inputs are finite; a program needn't handle non-finite values.
Results may differ from a plain program's by a relative error of at most 0.000054.
Values sent between devices are 32-bit elements; how exact they have to be, the bound alone decides.
No kernel may reach another device: no remote copies, remote signals or barrier semaphores. Data moves between devices by JAX's collectives and lax.ppermute only.
A program may use at most 64 MiB of HBM per device.

v0:
```python
import math

import jax
import jax.numpy as jnp
from jax import lax
from jax.sharding import PartitionSpec as P

ITERS = 3


FILTER_R2 = 4.0
PROJ_BETA = 8.0
PROJ_ETA = 0.5
SHARPNESS = 16.0
SMOOTH_EPS = 0.0001


def extended(cells, sides, width):
    for axis, dim in sides:
        count = lax.axis_size(axis)
        ends = count - 1
        head = lax.slice_in_dim(cells, 0, width, axis=dim)
        tail = lax.slice_in_dim(cells, cells.shape[dim] - width, cells.shape[dim], axis=dim)
        cells = jnp.concatenate(
            [
                lax.ppermute(tail, axis, [(i, (i + 1) % count) for i in range(ends)]),
                cells,
                lax.ppermute(head, axis, [((i + 1) % count, i) for i in range(ends)]),
            ],
            axis=dim,
        )
    return cells


def shifted(block, axis, distance):
    devices = range(lax.axis_size(axis))
    route = [(i - distance, i) for i in devices if i - distance in devices]
    return lax.ppermute(block, axis, route)


def neighbour_sum(padded):
    beside = padded[2:, 1:-1, 1:-1] + padded[:-2, 1:-1, 1:-1]
    beside = beside + padded[1:-1, 2:, 1:-1] + padded[1:-1, :-2, 1:-1]
    beside = beside + padded[1:-1, 1:-1, 2:] + padded[1:-1, 1:-1, :-2]
    return beside


def project(field):
    upper = jnp.tanh(PROJ_BETA * PROJ_ETA) + jnp.tanh(PROJ_BETA * (field - PROJ_ETA))
    lower = math.tanh(PROJ_BETA * PROJ_ETA) + math.tanh(PROJ_BETA * (1.0 - PROJ_ETA))
    return upper / lower


def smooth_min(first, second):
    gap = first - second
    return 0.5 * (first + second - jnp.sqrt(gap * gap + SMOOTH_EPS) + math.sqrt(SMOOTH_EPS))


def support_of(below_layer, inside):
    valid = inside > 0.5
    weights = jnp.pad(jnp.where(valid, jnp.exp(SHARPNESS * below_layer), 0.0), 1)
    count_rows = below_layer.shape[0]
    count_cols = below_layer.shape[1]
    total = jnp.zeros(below_layer.shape, jnp.float32)
    for shift_a in range(3):
        for shift_b in range(3):
            total = total + weights[shift_a : shift_a + count_rows, shift_b : shift_b + count_cols]
    safe_total = jnp.where(valid, total, 1.0)
    return jnp.where(valid, (jnp.log(safe_total) - math.log(9.0)) / SHARPNESS, 0.0)


def within(start, count, limit):
    position = start + jnp.arange(count, dtype=jnp.int32)
    return jnp.where((position >= 0) & (position < limit), 1.0, 0.0).astype(jnp.float32)


def local(design):
    layers = design.shape[0]
    tile_rows = design.shape[1]
    slab_count = lax.axis_size("gz")
    tile_count = lax.axis_size("xy")
    slab_index = lax.axis_index("gz")
    tile_index = lax.axis_index("xy")
    scale = 1.0 + 6.0 * FILTER_R2
    field = design
    for sweep_no in range(ITERS):
        padded = extended(field, (("gz", 0), ("xy", 1)), 1)
        padded = jnp.pad(padded, ((0, 0), (0, 0), (1, 1)))
        field = (design + FILTER_R2 * neighbour_sum(padded)) / scale
    blueprint = project(field)
    blue_wide = extended(blueprint, (("xy", 1),), layers)
    inside = within(
        tile_index * tile_rows - layers, tile_rows + 2 * layers, tile_rows * tile_count
    )[:, None]
    valid_rows = inside > 0.5
    baseplate = jnp.where(
        valid_rows, jnp.ones((tile_rows + 2 * layers, design.shape[2]), jnp.float32), 0.0
    )

    def run_slab(support_rows):

        def layer_step(below_layer, blue_layer):
            printed_layer = jnp.where(
                valid_rows, smooth_min(blue_layer, support_of(below_layer, inside)), 0.0
            )
            return (printed_layer, printed_layer)

        unused, stacked = lax.scan(layer_step, support_rows, blue_wide)
        return stacked

    def incoming(top_layer):
        received = shifted(top_layer, "gz", 1)
        widened_top = extended(received, (("xy", 0),), layers)
        widened_top = jnp.where(valid_rows, widened_top, 0.0)
        return jnp.where(slab_index == 0, baseplate, widened_top)

    def chain_round(round_no, support_rows):
        stacked = run_slab(support_rows)
        return incoming(stacked[layers - 1, layers : layers + tile_rows])

    support_rows = lax.fori_loop(0, slab_count - 1, chain_round, baseplate)
    stacked = run_slab(support_rows)
    printed = stacked[:, layers : layers + tile_rows]
    return (blueprint, printed)


def solution(mesh):
    in_specs = (P("gz", "xy", None),)
    out_specs = (P("gz", "xy", None), P("gz", "xy", None))
    return jax.shard_map(local, mesh=mesh, in_specs=in_specs, out_specs=out_specs, check_vma=False)
```

profile of v0, /device:TPU:38, one launch (start us, length us, event | category | flops | bytes accessed | tf_op | source)
XLA Modules:
  0.0 400.8 jit_solution(17487907961195317163)
XLA Ops:
  10.3 11.2 %collective-permute-start.5 = (f32[10,1,1024]{2,1,0:T(1,128)S(1)}, f32[10,1,1024]{2,1,0:T(1,128)S(1)}, u32[]{:S(2)}, u32[]{:S(2)}) collective-permute-start(f32[10,1,1024]{2,1,0:T(1,128)S(1)} %get-tuple-element.382), channel_id=1, source_target_pairs={{1,0},{2,1},{3,2},{4,3},{5,4},{6,5},{7,6},{8,7},{9,8},{10,9},{11,1... | collective-permute-start | bytes 122888 | tf_op jit(solution)/shard_map/ppermute | solution.py:28
  23.4 6.1 %collective-permute-done.6 = f32[10,1,1024]{2,1,0:T(1,128)S(1)} collective-permute-done((f32[10,1,1024]{2,1,0:T(1,128)S(1)}, f32[10,1,1024]{2,1,0:T(1,128)S(1)}, u32[]{:S(2)}, u32[]{:S(2)}) %collective-permute-start.6) | collective-permute-done | bytes 40992 | tf_op jit(solution)/shard_map/ppermute | solution.py:26
  42.8 6.0 %collective-permute-start.9 = (f32[10,1,1024]{2,1,0:T(1,128)S(1)}, f32[10,1,1024]{2,1,0:T(1,128)S(1)}, u32[]{:S(2)}, u32[]{:S(2)}) collective-permute-start(f32[10,1,1024]{2,1,0:T(1,128)S(1)} %get-tuple-element.380), channel_id=1, source_target_pairs={{1,0},{2,1},{3,2},{4,3},{5,4},{6,5},{7,6},{8,7},{9,8},{10,9},{11,1... | collective-permute-start | bytes 122888 | tf_op jit(solution)/shard_map/ppermute | solution.py:28
  60.2 6.3 %collective-permute-start.13 = (f32[10,1,1024]{2,1,0:T(1,128)S(1)}, f32[10,1,1024]{2,1,0:T(1,128)S(1)}, u32[]{:S(2)}, u32[]{:S(2)}) collective-permute-start(f32[10,1,1024]{2,1,0:T(1,128)S(1)} %get-tuple-element.378), channel_id=1, source_target_pairs={{1,0},{2,1},{3,2},{4,3},{5,4},{6,5},{7,6},{8,7},{9,8},{10,9},{11,1... | collective-permute-start | bytes 122888 | tf_op jit(solution)/shard_map/ppermute | solution.py:28
  68.5 6.1 %collective-permute-done.14 = f32[10,1,1024]{2,1,0:T(1,128)S(1)} collective-permute-done((f32[10,1,1024]{2,1,0:T(1,128)S(1)}, f32[10,1,1024]{2,1,0:T(1,128)S(1)}, u32[]{:S(2)}, u32[]{:S(2)}) %collective-permute-start.14) | collective-permute-done | bytes 40992 | tf_op jit(solution)/shard_map/ppermute | solution.py:26
  77.6 6.0 %collective-permute-start.16 = (f32[8,8,1024]{2,1,0:T(8,128)S(1)}, f32[8,8,1024]{2,1,0:T(8,128)S(1)}, u32[]{:S(2)}, u32[]{:S(2)}) collective-permute-start(f32[8,8,1024]{2,1,0:T(8,128)S(1)} %get-tuple-element.384), channel_id=1, source_target_pairs={{1,0},{2,1},{3,2},{4,3},{5,4},{6,5},{7,6},{8,7},{9,8},{10,9},{11,1... | collective-permute-start | bytes 786440 | tf_op jit(solution)/shard_map/ppermute | solution.py:28
  87.7 308.7 %while.54 = (s32[]{:T(128)}, f32[32,1024]{1,0:T(8,128)S(1)}, pred[]{:T(512)}, f32[8,32,1024]{2,1,0:T(8,128)S(1)}, s32[]{:T(128)}, /*index=5*/f32[32]{0:T(128)S(1)}, s32[]{:T(128)}, s32[]{:T(128)}, s32[]{:T(128)}) while((s32[]{:T(128)}, f32[32,1024]{1,0:T(8,128)S(1)}, pred[]{:T(512)}, f32[8,32,1024]{2,1,0:T(8,128)S(1)}, ...), condition=%wide.region_3.4_spmd.clone.clone, body=%wide.region_0.3_spmd.clone.clone.sunk | while | flops 852548 | bytes 1836947 | solution.py:121
  93.2 4.9 %collective-permute-done = f32[16,1024]{1,0:T(8,128)S(1)} collective-permute-done((f32[16,1024]{1,0:T(8,128)S(1)}, f32[16,1024]{1,0:T(8,128)S(1)}, u32[]{:S(2)}, u32[]{:S(2)}) %collective-permute-start) | collective-permute-done | bytes 65568 | tf_op jit(solution)/shard_map/while/body/eval_jaxpr/ppermute | solution.py:38
  98.1 6.5 %collective-permute-start.1 = (f32[8,1024]{1,0:T(8,128)S(1)}, f32[8,1024]{1,0:T(8,128)S(1)}, u32[]{:S(2)}, u32[]{:S(2)}) collective-permute-start(f32[8,1024]{1,0:T(8,128)S(1)} %get-tuple-element.505), channel_id=1, source_target_pairs={{1,0},{2,1},{3,2},{4,3},{5,4},{6,5},{7,6},{8,7},{9,8},{10,9},{11,1... | collective-permute-start | bytes 98312 | tf_op jit(solution)/shard_map/while/body/eval_jaxpr/ppermute | solution.py:28
  106.5 6.0 %collective-permute-done.2 = f32[8,1024]{1,0:T(8,128)S(1)} collective-permute-done((f32[8,1024]{1,0:T(8,128)S(1)}, f32[8,1024]{1,0:T(8,128)S(1)}, u32[]{:S(2)}, u32[]{:S(2)}) %collective-permute-start.2) | collective-permute-done | bytes 32800 | tf_op jit(solution)/shard_map/while/body/eval_jaxpr/ppermute | solution.py:26
  118.1 4.9 %collective-permute-done = f32[16,1024]{1,0:T(8,128)S(1)} collective-permute-done((f32[16,1024]{1,0:T(8,128)S(1)}, f32[16,1024]{1,0:T(8,128)S(1)}, u32[]{:S(2)}, u32[]{:S(2)}) %collective-permute-start) | collective-permute-done | bytes 65568 | tf_op jit(solution)/shard_map/while/body/eval_jaxpr/ppermute | solution.py:38
  138.3 4.9 %collective-permute-done = f32[16,1024]{1,0:T(8,128)S(1)} collective-permute-done((f32[16,1024]{1,0:T(8,128)S(1)}, f32[16,1024]{1,0:T(8,128)S(1)}, u32[]{:S(2)}, u32[]{:S(2)}) %collective-permute-start) | collective-permute-done | bytes 65568 | tf_op jit(solution)/shard_map/while/body/eval_jaxpr/ppermute | solution.py:38
  158.6 4.9 %collective-permute-done = f32[16,1024]{1,0:T(8,128)S(1)} collective-permute-done((f32[16,1024]{1,0:T(8,128)S(1)}, f32[16,1024]{1,0:T(8,128)S(1)}, u32[]{:S(2)}, u32[]{:S(2)}) %collective-permute-start) | collective-permute-done | bytes 65568 | tf_op jit(solution)/shard_map/while/body/eval_jaxpr/ppermute | solution.py:38
  178.9 4.9 %collective-permute-done = f32[16,1024]{1,0:T(8,128)S(1)} collective-permute-done((f32[16,1024]{1,0:T(8,128)S(1)}, f32[16,1024]{1,0:T(8,128)S(1)}, u32[]{:S(2)}, u32[]{:S(2)}) %collective-permute-start) | collective-permute-done | bytes 65568 | tf_op jit(solution)/shard_map/while/body/eval_jaxpr/ppermute | solution.py:38
  199.2 4.9 %collective-permute-done = f32[16,1024]{1,0:T(8,128)S(1)} collective-permute-done((f32[16,1024]{1,0:T(8,128)S(1)}, f32[16,1024]{1,0:T(8,128)S(1)}, u32[]{:S(2)}, u32[]{:S(2)}) %collective-permute-start) | collective-permute-done | bytes 65568 | tf_op jit(solution)/shard_map/while/body/eval_jaxpr/ppermute | solution.py:38
  219.5 4.9 %collective-permute-done = f32[16,1024]{1,0:T(8,128)S(1)} collective-permute-done((f32[16,1024]{1,0:T(8,128)S(1)}, f32[16,1024]{1,0:T(8,128)S(1)}, u32[]{:S(2)}, u32[]{:S(2)}) %collective-permute-start) | collective-permute-done | bytes 65568 | tf_op jit(solution)/shard_map/while/body/eval_jaxpr/ppermute | solution.py:38
  239.7 4.9 %collective-permute-done = f32[16,1024]{1,0:T(8,128)S(1)} collective-permute-done((f32[16,1024]{1,0:T(8,128)S(1)}, f32[16,1024]{1,0:T(8,128)S(1)}, u32[]{:S(2)}, u32[]{:S(2)}) %collective-permute-start) | collective-permute-done | bytes 65568 | tf_op jit(solution)/shard_map/while/body/eval_jaxpr/ppermute | solution.py:38
  260.0 4.9 %collective-permute-done = f32[16,1024]{1,0:T(8,128)S(1)} collective-permute-done((f32[16,1024]{1,0:T(8,128)S(1)}, f32[16,1024]{1,0:T(8,128)S(1)}, u32[]{:S(2)}, u32[]{:S(2)}) %collective-permute-start) | collective-permute-done | bytes 65568 | tf_op jit(solution)/shard_map/while/body/eval_jaxpr/ppermute | solution.py:38
  280.3 4.9 %collective-permute-done = f32[16,1024]{1,0:T(8,128)S(1)} collective-permute-done((f32[16,1024]{1,0:T(8,128)S(1)}, f32[16,1024]{1,0:T(8,128)S(1)}, u32[]{:S(2)}, u32[]{:S(2)}) %collective-permute-start) | collective-permute-done | bytes 65568 | tf_op jit(solution)/shard_map/while/body/eval_jaxpr/ppermute | solution.py:38
  300.6 4.9 %collective-permute-done = f32[16,1024]{1,0:T(8,128)S(1)} collective-permute-done((f32[16,1024]{1,0:T(8,128)S(1)}, f32[16,1024]{1,0:T(8,128)S(1)}, u32[]{:S(2)}, u32[]{:S(2)}) %collective-permute-start) | collective-permute-done | bytes 65568 | tf_op jit(solution)/shard_map/while/body/eval_jaxpr/ppermute | solution.py:38
  320.8 4.9 %collective-permute-done = f32[16,1024]{1,0:T(8,128)S(1)} collective-permute-done((f32[16,1024]{1,0:T(8,128)S(1)}, f32[16,1024]{1,0:T(8,128)S(1)}, u32[]{:S(2)}, u32[]{:S(2)}) %collective-permute-start) | collective-permute-done | bytes 65568 | tf_op jit(solution)/shard_map/while/body/eval_jaxpr/ppermute | solution.py:38
  341.1 4.9 %collective-permute-done = f32[16,1024]{1,0:T(8,128)S(1)} collective-permute-done((f32[16,1024]{1,0:T(8,128)S(1)}, f32[16,1024]{1,0:T(8,128)S(1)}, u32[]{:S(2)}, u32[]{:S(2)}) %collective-permute-start) | collective-permute-done | bytes 65568 | tf_op jit(solution)/shard_map/while/body/eval_jaxpr/ppermute | solution.py:38
  361.4 4.9 %collective-permute-done = f32[16,1024]{1,0:T(8,128)S(1)} collective-permute-done((f32[16,1024]{1,0:T(8,128)S(1)}, f32[16,1024]{1,0:T(8,128)S(1)}, u32[]{:S(2)}, u32[]{:S(2)}) %collective-permute-start) | collective-permute-done | bytes 65568 | tf_op jit(solution)/shard_map/while/body/eval_jaxpr/ppermute | solution.py:38
  381.7 4.9 %collective-permute-done = f32[16,1024]{1,0:T(8,128)S(1)} collective-permute-done((f32[16,1024]{1,0:T(8,128)S(1)}, f32[16,1024]{1,0:T(8,128)S(1)}, u32[]{:S(2)}, u32[]{:S(2)}) %collective-permute-start) | collective-permute-done | bytes 65568 | tf_op jit(solution)/shard_map/while/body/eval_jaxpr/ppermute | solution.py:38
  (625 shorter events, 322.8 us)
Async XLA Ops:
  10.3 13.2 %collective-permute-start.5 = (f32[10,1,1024]{2,1,0:T(1,128)S(1)}, f32[10,1,1024]{2,1,0:T(1,128)S(1)}, u32[]{:S(2)}, u32[]{:S(2)}) collective-permute-start(f32[10,1,1024]{2,1,0:T(1,128)S(1)} %get-tuple-element.382), channel_id=1, source_target_pairs={{1,0},{2,1},{3,2},{4,3},{5,4},{6,5},{7,6},{8,7},{9,8},{10,9},{11,1... | collective-permute-start | bytes 122888 | tf_op jit(solution)/shard_map/ppermute | solution.py:28
  21.5 8.0 %collective-permute-start.6 = (f32[10,1,1024]{2,1,0:T(1,128)S(1)}, f32[10,1,1024]{2,1,0:T(1,128)S(1)}, u32[]{:S(2)}, u32[]{:S(2)}) collective-permute-start(f32[10,1,1024]{2,1,0:T(1,128)S(1)} %get-tuple-element.381), channel_id=1, source_target_pairs={{0,1},{1,2},{2,3},{3,4},{4,5},{5,6},{6,7},{7,8},{8,9},{9,10},{10,1... | collective-permute-start | bytes 122888 | tf_op jit(solution)/shard_map/ppermute | solution.py:26
  40.8 8.0 %collective-permute-start.10 = (f32[10,1,1024]{2,1,0:T(1,128)S(1)}, f32[10,1,1024]{2,1,0:T(1,128)S(1)}, u32[]{:S(2)}, u32[]{:S(2)}) collective-permute-start(f32[10,1,1024]{2,1,0:T(1,128)S(1)} %get-tuple-element.379), channel_id=1, source_target_pairs={{0,1},{1,2},{2,3},{3,4},{4,5},{5,6},{6,7},{7,8},{8,9},{9,10},{10,1... | collective-permute-start | bytes 122888 | tf_op jit(solution)/shard_map/ppermute | solution.py:26
  42.8 7.7 %collective-permute-start.9 = (f32[10,1,1024]{2,1,0:T(1,128)S(1)}, f32[10,1,1024]{2,1,0:T(1,128)S(1)}, u32[]{:S(2)}, u32[]{:S(2)}) collective-permute-start(f32[10,1,1024]{2,1,0:T(1,128)S(1)} %get-tuple-element.380), channel_id=1, source_target_pairs={{1,0},{2,1},{3,2},{4,3},{5,4},{6,5},{7,6},{8,7},{9,8},{10,9},{11,1... | collective-permute-start | bytes 122888 | tf_op jit(solution)/shard_map/ppermute | solution.py:28
  60.2 8.3 %collective-permute-start.13 = (f32[10,1,1024]{2,1,0:T(1,128)S(1)}, f32[10,1,1024]{2,1,0:T(1,128)S(1)}, u32[]{:S(2)}, u32[]{:S(2)}) collective-permute-start(f32[10,1,1024]{2,1,0:T(1,128)S(1)} %get-tuple-element.378), channel_id=1, source_target_pairs={{1,0},{2,1},{3,2},{4,3},{5,4},{6,5},{7,6},{8,7},{9,8},{10,9},{11,1... | collective-permute-start | bytes 122888 | tf_op jit(solution)/shard_map/ppermute | solution.py:28
  66.6 8.0 %collective-permute-start.14 = (f32[10,1,1024]{2,1,0:T(1,128)S(1)}, f32[10,1,1024]{2,1,0:T(1,128)S(1)}, u32[]{:S(2)}, u32[]{:S(2)}) collective-permute-start(f32[10,1,1024]{2,1,0:T(1,128)S(1)} %get-tuple-element.377), channel_id=1, source_target_pairs={{0,1},{1,2},{2,3},{3,4},{4,5},{5,6},{6,7},{7,8},{8,9},{9,10},{10,1... | collective-permute-start | bytes 122888 | tf_op jit(solution)/shard_map/ppermute | solution.py:26
  75.7 10.4 %collective-permute-start.15 = (f32[8,8,1024]{2,1,0:T(8,128)S(1)}, f32[8,8,1024]{2,1,0:T(8,128)S(1)}, u32[]{:S(2)}, u32[]{:S(2)}) collective-permute-start(f32[8,8,1024]{2,1,0:T(8,128)S(1)} %get-tuple-element.383), channel_id=1, source_target_pairs={{0,1},{1,2},{2,3},{3,4},{4,5},{5,6},{6,7},{7,8},{8,9},{9,10},{10,1... | collective-permute-start | bytes 786440 | tf_op jit(solution)/shard_map/ppermute | solution.py:26
  77.6 9.9 %collective-permute-start.16 = (f32[8,8,1024]{2,1,0:T(8,128)S(1)}, f32[8,8,1024]{2,1,0:T(8,128)S(1)}, u32[]{:S(2)}, u32[]{:S(2)}) collective-permute-start(f32[8,8,1024]{2,1,0:T(8,128)S(1)} %get-tuple-element.384), channel_id=1, source_target_pairs={{1,0},{2,1},{3,2},{4,3},{5,4},{6,5},{7,6},{8,7},{9,8},{10,9},{11,1... | collective-permute-start | bytes 786440 | tf_op jit(solution)/shard_map/ppermute | solution.py:28
  98.1 8.4 %collective-permute-start.1 = (f32[8,1024]{1,0:T(8,128)S(1)}, f32[8,1024]{1,0:T(8,128)S(1)}, u32[]{:S(2)}, u32[]{:S(2)}) collective-permute-start(f32[8,1024]{1,0:T(8,128)S(1)} %get-tuple-element.505), channel_id=1, source_target_pairs={{1,0},{2,1},{3,2},{4,3},{5,4},{6,5},{7,6},{8,7},{9,8},{10,9},{11,1... | collective-permute-start | bytes 98312 | tf_op jit(solution)/shard_map/while/body/eval_jaxpr/ppermute | solution.py:28
  104.6 7.9 %collective-permute-start.2 = (f32[8,1024]{1,0:T(8,128)S(1)}, f32[8,1024]{1,0:T(8,128)S(1)}, u32[]{:S(2)}, u32[]{:S(2)}) collective-permute-start(f32[8,1024]{1,0:T(8,128)S(1)} %get-tuple-element.506), channel_id=1, source_target_pairs={{0,1},{1,2},{2,3},{3,4},{4,5},{5,6},{6,7},{7,8},{8,9},{9,10},{10,1... | collective-permute-start | bytes 98312 | tf_op jit(solution)/shard_map/while/body/eval_jaxpr/ppermute | solution.py:26
  124.9 7.9 %collective-permute-start.2 = (f32[8,1024]{1,0:T(8,128)S(1)}, f32[8,1024]{1,0:T(8,128)S(1)}, u32[]{:S(2)}, u32[]{:S(2)}) collective-permute-start(f32[8,1024]{1,0:T(8,128)S(1)} %get-tuple-element.506), channel_id=1, source_target_pairs={{0,1},{1,2},{2,3},{3,4},{4,5},{5,6},{6,7},{7,8},{8,9},{9,10},{10,1... | collective-permute-start | bytes 98312 | tf_op jit(solution)/shard_map/while/body/eval_jaxpr/ppermute | solution.py:26
  145.1 7.9 %collective-permute-start.2 = (f32[8,1024]{1,0:T(8,128)S(1)}, f32[8,1024]{1,0:T(8,128)S(1)}, u32[]{:S(2)}, u32[]{:S(2)}) collective-permute-start(f32[8,1024]{1,0:T(8,128)S(1)} %get-tuple-element.506), channel_id=1, source_target_pairs={{0,1},{1,2},{2,3},{3,4},{4,5},{5,6},{6,7},{7,8},{8,9},{9,10},{10,1... | collective-permute-start | bytes 98312 | tf_op jit(solution)/shard_map/while/body/eval_jaxpr/ppermute | solution.py:26
  165.4 7.9 %collective-permute-start.2 = (f32[8,1024]{1,0:T(8,128)S(1)}, f32[8,1024]{1,0:T(8,128)S(1)}, u32[]{:S(2)}, u32[]{:S(2)}) collective-permute-start(f32[8,1024]{1,0:T(8,128)S(1)} %get-tuple-element.506), channel_id=1, source_target_pairs={{0,1},{1,2},{2,3},{3,4},{4,5},{5,6},{6,7},{7,8},{8,9},{9,10},{10,1... | collective-permute-start | bytes 98312 | tf_op jit(solution)/shard_map/while/body/eval_jaxpr/ppermute | solution.py:26
  185.7 7.9 %collective-permute-start.2 = (f32[8,1024]{1,0:T(8,128)S(1)}, f32[8,1024]{1,0:T(8,128)S(1)}, u32[]{:S(2)}, u32[]{:S(2)}) collective-permute-start(f32[8,1024]{1,0:T(8,128)S(1)} %get-tuple-element.506), channel_id=1, source_target_pairs={{0,1},{1,2},{2,3},{3,4},{4,5},{5,6},{6,7},{7,8},{8,9},{9,10},{10,1... | collective-permute-start | bytes 98312 | tf_op jit(solution)/shard_map/while/body/eval_jaxpr/ppermute | solution.py:26
  206.0 7.9 %collective-permute-start.2 = (f32[8,1024]{1,0:T(8,128)S(1)}, f32[8,1024]{1,0:T(8,128)S(1)}, u32[]{:S(2)}, u32[]{:S(2)}) collective-permute-start(f32[8,1024]{1,0:T(8,128)S(1)} %get-tuple-element.506), channel_id=1, source_target_pairs={{0,1},{1,2},{2,3},{3,4},{4,5},{5,6},{6,7},{7,8},{8,9},{9,10},{10,1... | collective-permute-start | bytes 98312 | tf_op jit(solution)/shard_map/while/body/eval_jaxpr/ppermute | solution.py:26
  226.2 7.9 %collective-permute-start.2 = (f32[8,1024]{1,0:T(8,128)S(1)}, f32[8,1024]{1,0:T(8,128)S(1)}, u32[]{:S(2)}, u32[]{:S(2)}) collective-permute-start(f32[8,1024]{1,0:T(8,128)S(1)} %get-tuple-element.506), channel_id=1, source_target_pairs={{0,1},{1,2},{2,3},{3,4},{4,5},{5,6},{6,7},{7,8},{8,9},{9,10},{10,1... | collective-permute-start | bytes 98312 | tf_op jit(solution)/shard_map/while/body/eval_jaxpr/ppermute | solution.py:26
  246.5 7.9 %collective-permute-start.2 = (f32[8,1024]{1,0:T(8,128)S(1)}, f32[8,1024]{1,0:T(8,128)S(1)}, u32[]{:S(2)}, u32[]{:S(2)}) collective-permute-start(f32[8,1024]{1,0:T(8,128)S(1)} %get-tuple-element.506), channel_id=1, source_target_pairs={{0,1},{1,2},{2,3},{3,4},{4,5},{5,6},{6,7},{7,8},{8,9},{9,10},{10,1... | collective-permute-start | bytes 98312 | tf_op jit(solution)/shard_map/while/body/eval_jaxpr/ppermute | solution.py:26
  266.8 7.9 %collective-permute-start.2 = (f32[8,1024]{1,0:T(8,128)S(1)}, f32[8,1024]{1,0:T(8,128)S(1)}, u32[]{:S(2)}, u32[]{:S(2)}) collective-permute-start(f32[8,1024]{1,0:T(8,128)S(1)} %get-tuple-element.506), channel_id=1, source_target_pairs={{0,1},{1,2},{2,3},{3,4},{4,5},{5,6},{6,7},{7,8},{8,9},{9,10},{10,1... | collective-permute-start | bytes 98312 | tf_op jit(solution)/shard_map/while/body/eval_jaxpr/ppermute | solution.py:26
  287.1 7.9 %collective-permute-start.2 = (f32[8,1024]{1,0:T(8,128)S(1)}, f32[8,1024]{1,0:T(8,128)S(1)}, u32[]{:S(2)}, u32[]{:S(2)}) collective-permute-start(f32[8,1024]{1,0:T(8,128)S(1)} %get-tuple-element.506), channel_id=1, source_target_pairs={{0,1},{1,2},{2,3},{3,4},{4,5},{5,6},{6,7},{7,8},{8,9},{9,10},{10,1... | collective-permute-start | bytes 98312 | tf_op jit(solution)/shard_map/while/body/eval_jaxpr/ppermute | solution.py:26
  307.3 7.9 %collective-permute-start.2 = (f32[8,1024]{1,0:T(8,128)S(1)}, f32[8,1024]{1,0:T(8,128)S(1)}, u32[]{:S(2)}, u32[]{:S(2)}) collective-permute-start(f32[8,1024]{1,0:T(8,128)S(1)} %get-tuple-element.506), channel_id=1, source_target_pairs={{0,1},{1,2},{2,3},{3,4},{4,5},{5,6},{6,7},{7,8},{8,9},{9,10},{10,1... | collective-permute-start | bytes 98312 | tf_op jit(solution)/shard_map/while/body/eval_jaxpr/ppermute | solution.py:26
  327.6 7.9 %collective-permute-start.2 = (f32[8,1024]{1,0:T(8,128)S(1)}, f32[8,1024]{1,0:T(8,128)S(1)}, u32[]{:S(2)}, u32[]{:S(2)}) collective-permute-start(f32[8,1024]{1,0:T(8,128)S(1)} %get-tuple-element.506), channel_id=1, source_target_pairs={{0,1},{1,2},{2,3},{3,4},{4,5},{5,6},{6,7},{7,8},{8,9},{9,10},{10,1... | collective-permute-start | bytes 98312 | tf_op jit(solution)/shard_map/while/body/eval_jaxpr/ppermute | solution.py:26
  347.9 7.9 %collective-permute-start.2 = (f32[8,1024]{1,0:T(8,128)S(1)}, f32[8,1024]{1,0:T(8,128)S(1)}, u32[]{:S(2)}, u32[]{:S(2)}) collective-permute-start(f32[8,1024]{1,0:T(8,128)S(1)} %get-tuple-element.506), channel_id=1, source_target_pairs={{0,1},{1,2},{2,3},{3,4},{4,5},{5,6},{6,7},{7,8},{8,9},{9,10},{10,1... | collective-permute-start | bytes 98312 | tf_op jit(solution)/shard_map/while/body/eval_jaxpr/ppermute | solution.py:26
  368.2 7.9 %collective-permute-start.2 = (f32[8,1024]{1,0:T(8,128)S(1)}, f32[8,1024]{1,0:T(8,128)S(1)}, u32[]{:S(2)}, u32[]{:S(2)}) collective-permute-start(f32[8,1024]{1,0:T(8,128)S(1)} %get-tuple-element.506), channel_id=1, source_target_pairs={{0,1},{1,2},{2,3},{3,4},{4,5},{5,6},{6,7},{7,8},{8,9},{9,10},{10,1... | collective-permute-start | bytes 98312 | tf_op jit(solution)/shard_map/while/body/eval_jaxpr/ppermute | solution.py:26
  388.5 7.9 %collective-permute-start.2 = (f32[8,1024]{1,0:T(8,128)S(1)}, f32[8,1024]{1,0:T(8,128)S(1)}, u32[]{:S(2)}, u32[]{:S(2)}) collective-permute-start(f32[8,1024]{1,0:T(8,128)S(1)} %get-tuple-element.506), channel_id=1, source_target_pairs={{0,1},{1,2},{2,3},{3,4},{4,5},{5,6},{6,7},{7,8},{8,9},{9,10},{10,1... | collective-permute-start | bytes 98312 | tf_op jit(solution)/shard_map/while/body/eval_jaxpr/ppermute | solution.py:26
  (37 other events, 253.6 us)
where the time goes:
time: 405 us; the launch traced here: 401 us
  starting transfers between devices  173 us (43%)
  waiting for transfers between devices  162 us (40%)
  other arithmetic  56.5 us (14%)
  loops' own time  5.42 us (1%)
    ppermute x22, waiting for transfers between devices, extended(): lax.ppermute(tail, axis, [(i, (i + 1) % count) for i in range(ends)])  85.2 us
    ppermute x22, starting transfers between devices, extended(): lax.ppermute(head, axis, [((i + 1) % count, i) for i in range(ends)])  73.1 us
    ppermute x15, waiting for transfers between devices, shifted(): return lax.ppermute(block, axis, route)  73 us
    ppermute x22, starting transfers between devices, extended(): lax.ppermute(tail, axis, [(i, (i + 1) % count) for i in range(ends)])  70.8 us
    dynamic_update_slice x128, other arithmetic, run_slab(): unused, stacked = lax.scan(layer_step, support_rows, blue_wide)  40.5 us
    ppermute x15, starting transfers between devices, shifted(): return lax.ppermute(block, axis, route)  28.8 us
    select_n x128, other arithmetic, support_of(): jnp.where(valid, jnp.exp(SHARPNESS * below_layer), 0.0)  10.3 us
  transfers between devices with their start and end apart: 59, of which 38 were waited for; matrix products, arithmetic and copies ran while one was open for 0% of the time, Pallas kernels for 0%

commit v1 on v0

v1 whole, which is shorter than its diff:
```python
import functools
import math

import jax
import jax.numpy as jnp
from jax import lax
from jax.experimental import pallas as pl
from jax.experimental.pallas import tpu as pltpu
from jax.sharding import PartitionSpec as P

LAYERS = 16
ROWS = 16
FOLDS = 8
LANES = 128
STRIDE = 80
HALO = 24
REACH = 3
PART = 768
AXES = ("gz", "xy")

FILTER_R2 = 4.0
PROJ_BETA = 8.0
PROJ_ETA = 0.5
SHARPNESS = 16.0
SMOOTH_EPS = 0.0001
HALF = 0.5 * SHARPNESS / math.log(2.0)
OUTSIDE = -50.0
TINY = 2.0**-100
MARGIN_AT = [sum(15 - j for j in range(k)) for k in range(16)]
MARGIN = MARGIN_AT[15]
SIDE = 20 + 18 + 16


def place():
    slab = lax.axis_index("gz")
    return lax.div(slab, 2), lax.rem(slab, 2), lax.axis_index("xy")


def lane_of(shape=(FOLDS, LANES)):
    return lax.broadcasted_iota(jnp.int32, shape, len(shape) - 1)


def column_mask(core):
    fold = lax.broadcasted_iota(jnp.int32, (FOLDS, LANES), 0)
    column = 384 * core + STRIDE * fold + lane_of() - HALO
    return (column >= 0) & (column < 1024)


def fold_kernel(own, partner, near, far, out, to_down, to_up):
    unused, core, unused = place()
    lane = lane_of()

    def fold(source, start, base, count):
        def layer(i, carry):
            for group in range(2):
                tiles = []
                for a in range(7):
                    at = jnp.clip(a - 1 + core, 0, 5) * LANES + start
                    tile = source[i, pl.ds(8 * group, 8), pl.ds(pl.multiple_of(at, LANES), LANES)]
                    if a == 0:
                        tile = jnp.where(core == 0, 0.0, tile)
                    if a == 6:
                        tile = jnp.where(core == 1, 0.0, tile)
                    tiles.append(tile)
                for s in range(FOLDS):
                    a, shift = divmod(LANES - HALO + STRIDE * s, LANES)
                    block = tiles[a]
                    if shift:
                        first = pltpu.roll(tiles[a], LANES - shift, 1)
                        second = pltpu.roll(tiles[a + 1], LANES - shift, 1)
                        block = jnp.where(lane < LANES - shift, first, second)
                    row = ((base + i) * ROWS + 8 * group) * FOLDS
                    out[pl.ds(row + s, 8, stride=FOLDS), :] = block
            return carry

        lax.fori_loop(0, count, layer, 0)

    fold(own, 256 * core, REACH + 8 * core, 8)
    fold(partner, 0, REACH + 8 * (1 - core), 8)
    fold(near, 0, 19 * core, REACH)
    fold(far, 0, 19 * (1 - core), REACH)
    at = 0
    for away in range(REACH):
        for i in range(1 + away, 21 - away):
            to_down[at] = out[pl.ds((i * ROWS + 15 - away) * FOLDS, FOLDS), :]
            to_up[at] = out[pl.ds((i * ROWS + away) * FOLDS, FOLDS), :]
            at += 1


def filter_kernel(count_chips, count_tiles, own, up, down, height, to_down, to_up, cells, first, second):
    chip, core, tile = place()
    inside = column_mask(core)
    scale = jnp.where(inside, 1.0 / (1.0 + 6.0 * FILTER_R2), 0.0)
    above = jnp.where(tile > 0, 1.0, 0.0)
    below = jnp.where(tile < count_tiles - 1, 1.0, 0.0)

    def gather(i, carry):
        cells[i, pl.ds(REACH, ROWS)] = own[i]
        return carry

    lax.fori_loop(0, 22, gather, 0)
    at = 0
    for away in range(REACH):
        for i in range(1 + away, 21 - away):
            cells[i, REACH - 1 - away] = up[at]
            cells[i, REACH + ROWS + away] = down[at]
            at += 1

    def sweep(source, step, store):
        rim = REACH - step

        def layer(i, rows):
            held = jnp.where(((chip == 0) & (i < REACH)) | ((chip == count_chips - 1) & (i >= REACH + LAYERS)), 0.0, scale)
            for r in rows:
                middle = source[i, r]
                total = source[i - 1, r] + source[i + 1, r] + source[i, r - 1] + source[i, r + 1]
                total = total + pltpu.roll(middle, 1, 1) + pltpu.roll(middle, LANES - 1, 1)
                factor = held
                if r < REACH:
                    factor = held * above
                if r >= REACH + ROWS:
                    factor = held * below
                store(i, r, (cells[i, r] + FILTER_R2 * total) * factor)

        def body(i, carry):
            layer(i, range(REACH - rim, REACH + ROWS + rim))
            return carry

        for away in range(rim):
            for i in (REACH - rim + away, REACH + LAYERS + rim - 1 - away):
                layer(i, range(REACH - away, REACH + ROWS + away))
        lax.fori_loop(REACH, REACH + LAYERS, body, 0)

    def keep(target):
        def store(i, r, value):
            target[i, r] = value

        return store

    base = math.tanh(PROJ_BETA * PROJ_ETA)
    gain = HALF / (math.tanh(PROJ_BETA * PROJ_ETA) + math.tanh(PROJ_BETA * (1.0 - PROJ_ETA)))

    def project(i, r, field):
        value = gain * (base + jnp.tanh(PROJ_BETA * field - PROJ_BETA * PROJ_ETA))
        height[i - REACH, r - REACH] = jnp.where(inside, value, OUTSIDE)

    sweep(cells, 1, keep(first))
    sweep(first, 2, keep(second))
    sweep(second, 3, project)
    for k in range(15):
        to_down[pl.ds(MARGIN_AT[k], 15 - k)] = height[k, pl.ds(k + 1, 15 - k)]
        to_up[pl.ds(MARGIN_AT[k], 15 - k)] = height[k, pl.ds(0, 15 - k)]


def chain_kernel(turn, count_tiles, *refs):
    if turn:
        up, middle, down, height, height_up, height_down, unused, printed, top, even, odd = refs
    else:
        height, height_up, height_down, unused, printed, top, even, odd = refs
    chip, core, tile = place()

    @pl.when(chip == turn)
    def run():
        inside = column_mask(core)
        lane = lane_of()
        lift_up = jnp.where(tile > 0, 0.0, OUTSIDE)
        lift_down = jnp.where(tile < count_tiles - 1, 0.0, OUTSIDE)
        if turn:
            for r in range(ROWS):
                even[r] = up[r] + TINY
                even[ROWS + r] = middle[r] + TINY
                even[2 * ROWS + r] = down[r] + TINY
        else:
            ones = jnp.where(inside, math.exp(SHARPNESS), TINY)
            ones_up = jnp.where(tile > 0, ones, TINY)
            ones_down = jnp.where(tile < count_tiles - 1, ones, TINY)
            for r in range(ROWS):
                even[r] = ones_up
                even[ROWS + r] = ones
                even[2 * ROWS + r] = ones_down
        level = HALF * math.sqrt(SMOOTH_EPS)
        for k in range(LAYERS):
            source, target = (even, odd) if k % 2 == 0 else (odd, even)
            for j in range(k + 1, 47 - k):
                total = source[j - 1] + source[j] + source[j + 1]
                total = total + pltpu.roll(total, 1, 1) + pltpu.roll(total, LANES - 1, 1)
                support = jnp.log(total) * (0.5 / math.log(2.0)) - 0.5 * math.log2(9.0)
                if j < ROWS:
                    blue = height_up[MARGIN_AT[k] + j - 1 - k] + lift_up
                elif j < 2 * ROWS:
                    blue = height[k, j - ROWS]
                else:
                    blue = height_down[MARGIN_AT[k] + j - 2 * ROWS] + lift_down
                gap = blue - support
                square = gap * gap + level * level
                value = (blue + support + level) - square * lax.rsqrt(square)
                weight = jnp.exp2(value)
                if ROWS <= j < 2 * ROWS:
                    printed[k, j - ROWS] = value
                if k < LAYERS - 1:
                    target[j] = weight
                else:
                    before = pltpu.roll(pltpu.roll(weight, 1, 0), LANES - STRIDE, 1)
                    after = pltpu.roll(pltpu.roll(weight, FOLDS - 1, 0), STRIDE, 1)
                    weight = jnp.where(lane < HALO, before, weight)
                    weight = jnp.where(lane >= HALO + STRIDE, after, weight)
                    top[j - ROWS] = jnp.where(inside, weight, 0.0)


def unfold_kernel(scale, folded, own, partner):
    unused, core, unused = place()
    lane = lane_of()

    def unfold(target, base):
        def layer(i, carry):
            for group in range(2):
                row = ((base + i) * ROWS + 8 * group) * FOLDS
                blocks = [folded[pl.ds(row + s, 8, stride=FOLDS), :] * scale for s in range(FOLDS)]
                for a in range(5):
                    tile = None
                    for s in range(FOLDS):
                        low = max(LANES * a, STRIDE * s)
                        if low >= min(LANES * a + LANES, STRIDE * s + STRIDE):
                            continue
                        piece = pltpu.roll(blocks[s], (STRIDE * s - LANES * a - HALO) % LANES, 1)
                        tile = piece if tile is None else jnp.where(lane >= low - LANES * a, piece, tile)

                    def store(at, tile=tile):
                        target[i, pl.ds(8 * group, 8), pl.ds(at, LANES)] = tile

                    if a == 0:
                        pl.when(core == 0)(functools.partial(store, 0))
                    elif a == 4:
                        pl.when(core == 1)(functools.partial(store, 3 * LANES))
                    else:
                        store(pl.multiple_of(LANES * (a - core), LANES))
            return carry

        lax.fori_loop(0, 8, layer, 0)

    unfold(own, 8 * core)
    unfold(partner, 8 * (1 - core))


def call(kernel, name, outs, operands, scratch=(), aliases=None):
    held = [pltpu.with_memory_space_constraint(x, pltpu.VMEM) for x in operands]
    vmem = pl.BlockSpec(memory_space=pltpu.VMEM)
    return pl.pallas_call(
        kernel,
        name=name,
        out_shape=[pltpu.VMEM(shape, jnp.float32) for shape in outs],
        in_specs=[vmem] * len(held),
        out_specs=[vmem] * len(outs),
        scratch_shapes=[pltpu.VMEM(shape, jnp.float32) for shape in scratch],
        input_output_aliases=aliases or {},
        compiler_params=pltpu.CompilerParams(vmem_limit_bytes=24 * 1024 * 1024),
    )(*held)


def local(design):
    slabs = lax.axis_size("gz")
    tiles = lax.axis_size("xy")
    chips = slabs // 2
    unused, core, unused = place()

    def at(slab, tile):
        return slab * tiles + tile

    def swap(block):
        return lax.ppermute(block, "gz", [(i, i ^ 1) for i in range(slabs)])

    def from_up(block):
        return lax.ppermute(block, "xy", [(i, i + 1) for i in range(tiles - 1)])

    def from_down(block):
        return lax.ppermute(block, "xy", [(i + 1, i) for i in range(tiles - 1)])

    rim = jnp.where(core == 0, design[:REACH], design[8 - REACH :])
    left, right = design[:, :, :PART], design[:, :, 1024 - PART :]
    rim_left, rim_right = rim[:, :, :PART], rim[:, :, 1024 - PART :]
    crossing = [(i, j) for k in range(1, chips) for i, j in ((2 * k - 1, 2 * k), (2 * k, 2 * k - 1))]
    straight = [(i, j) for k in range(1, chips) for i, j in ((2 * k - 1, 2 * k + 1), (2 * k, 2 * k - 2))]
    near = lax.ppermute(jnp.where(core == 0, rim_right, rim_left), "gz", crossing)
    far = lax.ppermute(jnp.where(core == 0, rim_left, rim_right), "gz", straight)
    partner = swap(jnp.where(core == 0, right, left))
    block = (FOLDS, LANES)
    folded, to_down, to_up = call(
        fold_kernel,
        "fold",
        [(22 * ROWS * FOLDS, LANES), (SIDE, *block), (SIDE, *block)],
        [design, partner, near, far],
    )
    height, to_down, to_up = call(
        functools.partial(filter_kernel, chips, tiles),
        "filter",
        [(LAYERS, ROWS, *block), (MARGIN, *block), (MARGIN, *block)],
        [folded.reshape(22, ROWS, *block), from_up(to_down), from_down(to_up)],
        scratch=[(22, ROWS + 2 * REACH, *block)] * 3,
    )
    height_up, height_down = from_up(to_down), from_down(to_up)

    def spread(folded, scale, name):
        own, other = call(
            functools.partial(unfold_kernel, scale),
            name,
            [(8, ROWS, 512), (8, ROWS, 512)],
            [folded.reshape(LAYERS * ROWS * FOLDS, LANES)],
        )
        other = swap(other)
        return jnp.where(
            core == 0, jnp.concatenate([own, other], axis=2), jnp.concatenate([other, own], axis=2)
        )

    printed = jnp.zeros((LAYERS, ROWS, *block), jnp.float32)
    received = []
    for turn in range(chips):
        operands = [*received, height, height_up, height_down, printed]
        printed, top = call(
            functools.partial(chain_kernel, turn, tiles),
            "chain",
            [(LAYERS, ROWS, *block), (ROWS, *block)],
            operands,
            scratch=[(48, *block)] * 2,
            aliases={len(operands) - 1: 0},
        )
        if turn < chips - 1:
            received = [
                lax.ppermute(
                    top,
                    AXES,
                    [
                        (at(2 * turn + c, t), at(2 * turn + 2 + c, t + away))
                        for c in range(2)
                        for t in range(tiles)
                        if 0 <= t + away < tiles
                    ],
                )
                for away in (1, 0, -1)
            ]
        if turn == 0:
            blueprint = spread(height, 1.0 / HALF, "blueprint")
    return blueprint, spread(printed, 0.5 / HALF, "printed")


def solution(mesh):
    spec = P("gz", "xy", None)
    return jax.shard_map(local, mesh=mesh, in_specs=(spec,), out_specs=(spec, spec), check_vma=False)
```

time: 405 us -> 143 us (0.35)
  the two profiles are of different devices: /device:TPU:38 before, /device:TPU:57 now
where the time goes in v1:
time: 143 us
  waiting for transfers between devices  71.4 us (50%)
  starting transfers between devices  45.7 us (32%)
  Pallas kernels  21.4 us (15%)
  other arithmetic  2.98 us (2%)
    ppermute x21, waiting for transfers between devices, local(): lax.ppermute(top, AXES, [(at(2 * turn + c, t), at(2 * turn + 2 + c, t + a...  46.1 us
    pallas_call x12, Pallas kernels, call(): pl.pallas_call(kernel, name=name, out_shape=[pltpu.VMEM(shape, jnp.float3...  21.4 us
    ppermute x3, starting transfers between devices, swap(): return lax.ppermute(block, 'gz', [(i, i ^ 1) for i in range(slabs)])  17.9 us
    ppermute x21, starting transfers between devices, local(): lax.ppermute(top, AXES, [(at(2 * turn + c, t), at(2 * turn + 2 + c, t + a...  15.2 us
    ppermute x2, waiting for transfers between devices, from_down(): return lax.ppermute(block, 'xy', [(i + 1, i) for i in range(tiles - 1)])  10.7 us
    ppermute x2, waiting for transfers between devices, from_up(): return lax.ppermute(block, 'xy', [(i, i + 1) for i in range(tiles - 1)])  8.48 us
    ppermute x2, starting transfers between devices, from_up(): return lax.ppermute(block, 'xy', [(i, i + 1) for i in range(tiles - 1)])  8.04 us
    ppermute x1, waiting for transfers between devices, local(): lax.ppermute(jnp.where(core == 0, rim_left, rim_right), 'gz', straight)  5.72 us
  transfers between devices with their start and end apart: 30, of which 8 were waited for; matrix products, arithmetic and copies ran while one was open for 1% of the time, Pallas kernels for 9%

profile of v1, /device:TPU:57, one launch (start us, length us, event | category | flops | bytes accessed | tf_op | source)
XLA Modules:
  0.0 142.7 jit_solution(5911459140358126102)
XLA Ops:
  0.6 1.2 slice_select_fusion
  1.9 2.6 %collective-permute-start = (f32[8,16,768]{2,1,0:T(8,128)S(1)}, f32[8,16,768]{2,1,0:T(8,128)S(1)}, u32[]{:S(2)}, u32[]{:S(2)}) collective-permute-start(f32[8,16,768]{2,1,0:T(8,128)S(1)} %slice_select_fusion), channel_id=1, source_target_pairs={{0,32},{32,0},{64,96},{96,64},{128,160},{160,128},{192,224},{224,1... | collective-permute-start | bytes 1179656 | tf_op jit(solution)/shard_map/ppermute | solution.py:270
  5.2 1.3 collective-permute-start.2
  6.5 5.7 %collective-permute-done.2.far = f32[3,16,768]{2,1,0:T(8,128)S(1)} collective-permute-done((f32[3,16,768]{2,1,0:T(8,128)S(1)}, f32[3,16,768]{2,1,0:T(8,128)S(1)}, u32[]{:S(2)}, u32[]{:S(2)}) %collective-permute-start.2) | collective-permute-done | bytes 147488 | tf_op jit(solution)/shard_map/ppermute | solution.py:284
  12.3 2.3 %fold.1 = (f32[2816,128]{1,0:T(8,128)S(1)}, f32[54,8,128]{2,1,0:T(8,128)S(1)}, f32[54,8,128]{2,1,0:T(8,128)S(1)}) custom-call(f32[8,16,1024]{2,1,0:T(8,128)S(1)} %copy-done, f32[8,16,768]{2,1,0:T(8,128)S(1)} %collective-permute-done.partner, f32[3,16,768]{2,1,0:T(8,128)S(1)} %collective-permute-done.1.near, f32[3,16,768]{2,1,0:T(8,128)S(1)} %collective-permute-done.2.far), custom_call_target="tpu_custom_call" | custom-call | tf_op jit(solution)/shard_map/fold/pallas_call | solution.py:248
  14.6 4.0 %collective-permute-start.3 = (f32[54,8,128]{2,1,0:T(8,128)S(1)}, f32[54,8,128]{2,1,0:T(8,128)S(1)}, u32[]{:S(2)}, u32[]{:S(2)}) collective-permute-start(f32[54,8,128]{2,1,0:T(8,128)S(1)} %get-tuple-element.28), channel_id=1, source_target_pairs={{0,1},{1,2},{2,3},{3,4},{4,5},{5,6},{6,7},{7,8},{8,9},{9,10},{10,1... | collective-permute-start | bytes 663560 | tf_op jit(solution)/shard_map/ppermute | solution.py:273
  18.6 1.3 collective-permute-start.4
  19.9 1.8 %collective-permute-done.3.up = f32[54,8,128]{2,1,0:T(8,128)S(1)} collective-permute-done((f32[54,8,128]{2,1,0:T(8,128)S(1)}, f32[54,8,128]{2,1,0:T(8,128)S(1)}, u32[]{:S(2)}, u32[]{:S(2)}) %collective-permute-start.3) | collective-permute-done | bytes 221216 | tf_op jit(solution)/shard_map/ppermute | solution.py:273
  21.7 4.8 %collective-permute-done.4.down = f32[54,8,128]{2,1,0:T(8,128)S(1)} collective-permute-done((f32[54,8,128]{2,1,0:T(8,128)S(1)}, f32[54,8,128]{2,1,0:T(8,128)S(1)}, u32[]{:S(2)}, u32[]{:S(2)}) %collective-permute-start.4) | collective-permute-done | bytes 221216 | tf_op jit(solution)/shard_map/ppermute | solution.py:276
  26.4 6.3 %filter.1 = (f32[16,16,8,128]{3,2,1,0:T(8,128)S(1)}, f32[120,8,128]{2,1,0:T(8,128)S(1)}, f32[120,8,128]{2,1,0:T(8,128)S(1)}) custom-call(f32[22,16,8,128]{3,2,1,0:T(8,128)S(1)} %bitcast.5, f32[54,8,128]{2,1,0:T(8,128)S(1)} %collective-permute-done.3.up, f32[54,8,128]{2,1,0:T(8,128)S(1)} %collective-permute-done.4.down), custom_call_target="tpu_custom_call" | custom-call | tf_op jit(solution)/shard_map/filter/pallas_call | solution.py:248
  32.8 4.0 %collective-permute-start.6 = (f32[120,8,128]{2,1,0:T(8,128)S(1)}, f32[120,8,128]{2,1,0:T(8,128)S(1)}, u32[]{:S(2)}, u32[]{:S(2)}) collective-permute-start(f32[120,8,128]{2,1,0:T(8,128)S(1)} %get-tuple-element.33), channel_id=1, source_target_pairs={{0,1},{1,2},{2,3},{3,4},{4,5},{5,6},{6,7},{7,8},{8,9},{9,10},{10,1... | collective-permute-start | bytes 1474568 | tf_op jit(solution)/shard_map/ppermute | solution.py:273
  36.8 1.3 collective-permute-start.7
  38.1 6.7 %collective-permute-done.6.refs_1_.refs_4_ = f32[120,8,128]{2,1,0:T(8,128)S(1)} collective-permute-done((f32[120,8,128]{2,1,0:T(8,128)S(1)}, f32[120,8,128]{2,1,0:T(8,128)S(1)}, u32[]{:S(2)}, u32[]{:S(2)}) %collective-permute-start.6) | collective-permute-done | bytes 491552 | tf_op jit(solution)/shard_map/ppermute | solution.py:273
  44.8 6.0 %collective-permute-done.7.refs_2_.refs_5_ = f32[120,8,128]{2,1,0:T(8,128)S(1)} collective-permute-done((f32[120,8,128]{2,1,0:T(8,128)S(1)}, f32[120,8,128]{2,1,0:T(8,128)S(1)}, u32[]{:S(2)}, u32[]{:S(2)}) %collective-permute-start.7) | collective-permute-done | bytes 491552 | tf_op jit(solution)/shard_map/ppermute | solution.py:276
  63.5 4.7 %blueprint.1 = (f32[8,16,512]{2,1,0:T(8,128)S(1)}, f32[8,16,512]{2,1,0:T(8,128)S(1)}) custom-call(f32[2048,128]{1,0:T(8,128)S(1)} %bitcast.4), custom_call_target="tpu_custom_call" | custom-call | tf_op jit(solution)/shard_map/blueprint/pallas_call | solution.py:248
  68.2 5.3 %collective-permute-start.5 = (f32[8,16,512]{2,1,0:T(8,128)S(1)}, f32[8,16,512]{2,1,0:T(8,128)S(1)}, u32[]{:S(2)}, u32[]{:S(2)}) collective-permute-start(f32[8,16,512]{2,1,0:T(8,128)S(1)} %get-tuple-element.32), channel_id=1, source_target_pairs={{0,32},{32,0},{64,96},{96,64},{128,160},{160,128},{192,224},{224,1... | collective-permute-start | bytes 786440 | tf_op jit(solution)/shard_map/ppermute | solution.py:270
  74.3 1.3 collective-permute-start.27
  75.6 1.3 collective-permute-start.28
  76.9 43.1 %collective-permute-done.27.refs_1_ = f32[16,8,128]{2,1,0:T(8,128)S(1)} collective-permute-done((f32[16,8,128]{2,1,0:T(8,128)S(1)}, f32[16,8,128]{2,1,0:T(8,128)S(1)}, u32[]{:S(2)}, u32[]{:S(2)}) %collective-permute-start.27) | collective-permute-done | bytes 65568 | tf_op jit(solution)/shard_map/ppermute | solution.py:328
  120.0 3.0 %collective-permute-done.28.refs_2_ = f32[16,8,128]{2,1,0:T(8,128)S(1)} collective-permute-done((f32[16,8,128]{2,1,0:T(8,128)S(1)}, f32[16,8,128]{2,1,0:T(8,128)S(1)}, u32[]{:S(2)}, u32[]{:S(2)}) %collective-permute-start.28) | collective-permute-done | bytes 65568 | tf_op jit(solution)/shard_map/ppermute | solution.py:328
  123.0 3.0 %chain.15 = (f32[16,16,8,128]{3,2,1,0:T(8,128)S(1)}, f32[16,8,128]{2,1,0:T(8,128)}) custom-call(f32[16,8,128]{2,1,0:T(8,128)S(1)} %collective-permute-done.26.refs_0_, f32[16,8,128]{2,1,0:T(8,128)S(1)} %collective-permute-done.27.refs_1_, f32[16,8,128]{2,1,0:T(8,128)S(1)} %collective-permute-done.28.refs_2_, ...), custom_call_target="tpu_custom_call", output_to_operand_aliasing={{0}: (6, {})} | custom-call | tf_op jit(solution)/shard_map/chain/pallas_call | solution.py:248
  126.0 4.7 %printed.1 = (f32[8,16,512]{2,1,0:T(8,128)S(1)}, f32[8,16,512]{2,1,0:T(8,128)S(1)}) custom-call(f32[2048,128]{1,0:T(8,128)S(1)} %bitcast.3), custom_call_target="tpu_custom_call" | custom-call | tf_op jit(solution)/shard_map/printed/pallas_call | solution.py:248
  130.7 10.0 %collective-permute-start.29 = (f32[8,16,512]{2,1,0:T(8,128)S(1)}, f32[8,16,512]{2,1,0:T(8,128)S(1)}, u32[]{:S(2)}, u32[]{:S(2)}) collective-permute-start(f32[8,16,512]{2,1,0:T(8,128)S(1)} %get-tuple-element.51), channel_id=1, source_target_pairs={{0,32},{32,0},{64,96},{96,64},{128,160},{160,128},{192,224},{224,1... | collective-permute-start | bytes 786440 | tf_op jit(solution)/shard_map/ppermute | solution.py:270
  140.7 0.8 maximum_select_fusion
  (56 shorter events, 15.0 us)
Async XLA Ops:
  1.9 10.4 %collective-permute-start = (f32[8,16,768]{2,1,0:T(8,128)S(1)}, f32[8,16,768]{2,1,0:T(8,128)S(1)}, u32[]{:S(2)}, u32[]{:S(2)}) collective-permute-start(f32[8,16,768]{2,1,0:T(8,128)S(1)} %slice_select_fusion), channel_id=1, source_target_pairs={{0,32},{32,0},{64,96},{96,64},{128,160},{160,128},{192,224},{224,1... | collective-permute-start | bytes 1179656 | tf_op jit(solution)/shard_map/ppermute | solution.py:270
  4.5 2.0 %collective-permute-start.1 = (f32[3,16,768]{2,1,0:T(8,128)S(1)}, f32[3,16,768]{2,1,0:T(8,128)S(1)}, u32[]{:S(2)}, u32[]{:S(2)}) collective-permute-start(f32[3,16,768]{2,1,0:T(8,128)S(1)} %get-tuple-element.53), channel_id=1, source_target_pairs={{32,64},{64,32},{96,128},{128,96},{160,192},{192,160},{224,256},{2... | collective-permute-start | bytes 442376 | tf_op jit(solution)/shard_map/ppermute | solution.py:283
  5.2 7.0 %collective-permute-start.2 = (f32[3,16,768]{2,1,0:T(8,128)S(1)}, f32[3,16,768]{2,1,0:T(8,128)S(1)}, u32[]{:S(2)}, u32[]{:S(2)}) collective-permute-start(f32[3,16,768]{2,1,0:T(8,128)S(1)} %get-tuple-element.52), channel_id=1, source_target_pairs={{32,96},{64,0},{96,160},{128,64},{160,224},{192,128},{224,288},{25... | collective-permute-start | bytes 442376 | tf_op jit(solution)/shard_map/ppermute | solution.py:284
  14.6 7.1 %collective-permute-start.3 = (f32[54,8,128]{2,1,0:T(8,128)S(1)}, f32[54,8,128]{2,1,0:T(8,128)S(1)}, u32[]{:S(2)}, u32[]{:S(2)}) collective-permute-start(f32[54,8,128]{2,1,0:T(8,128)S(1)} %get-tuple-element.28), channel_id=1, source_target_pairs={{0,1},{1,2},{2,3},{3,4},{4,5},{5,6},{6,7},{7,8},{8,9},{9,10},{10,1... | collective-permute-start | bytes 663560 | tf_op jit(solution)/shard_map/ppermute | solution.py:273
  18.6 7.9 %collective-permute-start.4 = (f32[54,8,128]{2,1,0:T(8,128)S(1)}, f32[54,8,128]{2,1,0:T(8,128)S(1)}, u32[]{:S(2)}, u32[]{:S(2)}) collective-permute-start(f32[54,8,128]{2,1,0:T(8,128)S(1)} %get-tuple-element.29), channel_id=1, source_target_pairs={{1,0},{2,1},{3,2},{4,3},{5,4},{6,5},{7,6},{8,7},{9,8},{10,9},{11,1... | collective-permute-start | bytes 663560 | tf_op jit(solution)/shard_map/ppermute | solution.py:276
  32.8 12.0 %collective-permute-start.6 = (f32[120,8,128]{2,1,0:T(8,128)S(1)}, f32[120,8,128]{2,1,0:T(8,128)S(1)}, u32[]{:S(2)}, u32[]{:S(2)}) collective-permute-start(f32[120,8,128]{2,1,0:T(8,128)S(1)} %get-tuple-element.33), channel_id=1, source_target_pairs={{0,1},{1,2},{2,3},{3,4},{4,5},{5,6},{6,7},{7,8},{8,9},{9,10},{10,1... | collective-permute-start | bytes 1474568 | tf_op jit(solution)/shard_map/ppermute | solution.py:273
  36.8 13.9 %collective-permute-start.7 = (f32[120,8,128]{2,1,0:T(8,128)S(1)}, f32[120,8,128]{2,1,0:T(8,128)S(1)}, u32[]{:S(2)}, u32[]{:S(2)}) collective-permute-start(f32[120,8,128]{2,1,0:T(8,128)S(1)} %get-tuple-element.34), channel_id=1, source_target_pairs={{1,0},{2,1},{3,2},{4,3},{5,4},{6,5},{7,6},{8,7},{9,8},{10,9},{11,1... | collective-permute-start | bytes 1474568 | tf_op jit(solution)/shard_map/ppermute | solution.py:276
  50.9 2.0 %collective-permute-start.10 = (f32[16,8,128]{2,1,0:T(8,128)S(1)}, f32[16,8,128]{2,1,0:T(8,128)S(1)}, u32[]{:S(2)}, u32[]{:S(2)}) collective-permute-start(f32[16,8,128]{2,1,0:T(8,128)S(1)} %get-tuple-element.35), channel_id=1, source_target_pairs={{1,64},{2,65},{3,66},{4,67},{5,68},{6,69},{7,70},{8,71},{9,72},{10... | collective-permute-start | bytes 196616 | tf_op jit(solution)/shard_map/ppermute | solution.py:328
  51.5 1.4 collective-permute-start.8
  52.9 2.0 %collective-permute-start.11 = (f32[16,8,128]{2,1,0:T(8,128)S(1)}, f32[16,8,128]{2,1,0:T(8,128)S(1)}, u32[]{:S(2)}, u32[]{:S(2)}) collective-permute-start(f32[16,8,128]{2,1,0:T(8,128)S(1)} %get-tuple-element.37), channel_id=1, source_target_pairs={{64,129},{65,130},{66,131},{67,132},{68,133},{69,134},{70,135},{71... | collective-permute-start | bytes 196616 | tf_op jit(solution)/shard_map/ppermute | solution.py:328
  53.6 1.4 collective-permute-start.12
  55.0 2.0 %collective-permute-start.14 = (f32[16,8,128]{2,1,0:T(8,128)S(1)}, f32[16,8,128]{2,1,0:T(8,128)S(1)}, u32[]{:S(2)}, u32[]{:S(2)}) collective-permute-start(f32[16,8,128]{2,1,0:T(8,128)S(1)} %get-tuple-element.39), channel_id=1, source_target_pairs={{128,193},{129,194},{130,195},{131,196},{132,197},{133,198},{134,1... | collective-permute-start | bytes 196616 | tf_op jit(solution)/shard_map/ppermute | solution.py:328
  55.7 1.4 collective-permute-start.15
  57.1 2.0 %collective-permute-start.17 = (f32[16,8,128]{2,1,0:T(8,128)S(1)}, f32[16,8,128]{2,1,0:T(8,128)S(1)}, u32[]{:S(2)}, u32[]{:S(2)}) collective-permute-start(f32[16,8,128]{2,1,0:T(8,128)S(1)} %get-tuple-element.41), channel_id=1, source_target_pairs={{192,257},{193,258},{194,259},{195,260},{196,261},{197,262},{198,2... | collective-permute-start | bytes 196616 | tf_op jit(solution)/shard_map/ppermute | solution.py:328
  57.8 1.4 collective-permute-start.18
  59.4 2.0 %collective-permute-start.20 = (f32[16,8,128]{2,1,0:T(8,128)S(1)}, f32[16,8,128]{2,1,0:T(8,128)S(1)}, u32[]{:S(2)}, u32[]{:S(2)}) collective-permute-start(f32[16,8,128]{2,1,0:T(8,128)S(1)} %get-tuple-element.43), channel_id=1, source_target_pairs={{256,321},{257,322},{258,323},{259,324},{260,325},{261,326},{262,3... | collective-permute-start | bytes 196616 | tf_op jit(solution)/shard_map/ppermute | solution.py:328
  61.4 12.1 %collective-permute-start.23 = (f32[16,8,128]{2,1,0:T(8,128)S(1)}, f32[16,8,128]{2,1,0:T(8,128)S(1)}, u32[]{:S(2)}, u32[]{:S(2)}) collective-permute-start(f32[16,8,128]{2,1,0:T(8,128)S(1)} %get-tuple-element.45), channel_id=1, source_target_pairs={{320,385},{321,386},{322,387},{323,388},{324,389},{325,390},{326,3... | collective-permute-start | bytes 196616 | tf_op jit(solution)/shard_map/ppermute | solution.py:328
  62.1 11.4 %collective-permute-start.24 = (f32[16,8,128]{2,1,0:T(8,128)S(1)}, f32[16,8,128]{2,1,0:T(8,128)S(1)}, u32[]{:S(2)}, u32[]{:S(2)}) collective-permute-start(f32[16,8,128]{2,1,0:T(8,128)S(1)} %get-tuple-element.45), channel_id=1, source_target_pairs={{320,384},{321,385},{322,386},{323,387},{324,388},{325,389},{326,3... | collective-permute-start | bytes 196616 | tf_op jit(solution)/shard_map/ppermute | solution.py:328
  62.8 10.8 %collective-permute-start.25 = (f32[16,8,128]{2,1,0:T(8,128)S(1)}, f32[16,8,128]{2,1,0:T(8,128)S(1)}, u32[]{:S(2)}, u32[]{:S(2)}) collective-permute-start(f32[16,8,128]{2,1,0:T(8,128)S(1)} %get-tuple-element.45), channel_id=1, source_target_pairs={{321,384},{322,385},{323,386},{324,387},{325,388},{326,389},{327,3... | collective-permute-start | bytes 196616 | tf_op jit(solution)/shard_map/ppermute | solution.py:328
  68.2 72.5 %collective-permute-start.5 = (f32[8,16,512]{2,1,0:T(8,128)S(1)}, f32[8,16,512]{2,1,0:T(8,128)S(1)}, u32[]{:S(2)}, u32[]{:S(2)}) collective-permute-start(f32[8,16,512]{2,1,0:T(8,128)S(1)} %get-tuple-element.32), channel_id=1, source_target_pairs={{0,32},{32,0},{64,96},{96,64},{128,160},{160,128},{192,224},{224,1... | collective-permute-start | bytes 786440 | tf_op jit(solution)/shard_map/ppermute | solution.py:270
  73.6 3.3 %collective-permute-start.26 = (f32[16,8,128]{2,1,0:T(8,128)S(1)}, f32[16,8,128]{2,1,0:T(8,128)S(1)}, u32[]{:S(2)}, u32[]{:S(2)}) collective-permute-start(f32[16,8,128]{2,1,0:T(8,128)S(1)} %get-tuple-element.47), channel_id=1, source_target_pairs={{384,449},{385,450},{386,451},{387,452},{388,453},{389,454},{390,4... | collective-permute-start | bytes 196616 | tf_op jit(solution)/shard_map/ppermute | solution.py:328
  74.3 45.7 %collective-permute-start.27 = (f32[16,8,128]{2,1,0:T(8,128)S(1)}, f32[16,8,128]{2,1,0:T(8,128)S(1)}, u32[]{:S(2)}, u32[]{:S(2)}) collective-permute-start(f32[16,8,128]{2,1,0:T(8,128)S(1)} %get-tuple-element.47), channel_id=1, source_target_pairs={{384,448},{385,449},{386,450},{387,451},{388,452},{389,453},{390,4... | collective-permute-start | bytes 196616 | tf_op jit(solution)/shard_map/ppermute | solution.py:328
  75.6 47.4 %collective-permute-start.28 = (f32[16,8,128]{2,1,0:T(8,128)S(1)}, f32[16,8,128]{2,1,0:T(8,128)S(1)}, u32[]{:S(2)}, u32[]{:S(2)}) collective-permute-start(f32[16,8,128]{2,1,0:T(8,128)S(1)} %get-tuple-element.47), channel_id=1, source_target_pairs={{385,448},{386,449},{387,450},{388,451},{389,452},{390,453},{391,4... | collective-permute-start | bytes 196616 | tf_op jit(solution)/shard_map/ppermute | solution.py:328
  130.7 11.1 %collective-permute-start.29 = (f32[8,16,512]{2,1,0:T(8,128)S(1)}, f32[8,16,512]{2,1,0:T(8,128)S(1)}, u32[]{:S(2)}, u32[]{:S(2)}) collective-permute-start(f32[8,16,512]{2,1,0:T(8,128)S(1)} %get-tuple-element.51), channel_id=1, source_target_pairs={{0,32},{32,0},{64,96},{96,64},{128,160},{160,128},{192,224},{224,1... | collective-permute-start | bytes 786440 | tf_op jit(solution)/shard_map/ppermute | solution.py:270
  (7 other events, 8.7 us)

commit v2 on v1

--- a/solution.py
+++ b/solution.py
@@ -73,7 +73,7 @@
                     out[pl.ds(row + s, 8, stride=FOLDS), :] = block
             return carry
 
-        lax.fori_loop(0, count, layer, 0)
+        lax.fori_loop(0, count, layer, 0, unroll=count)
 
     fold(own, 256 * core, REACH + 8 * core, 8)
     fold(partner, 0, REACH + 8 * (1 - core), 8)
@@ -98,7 +98,7 @@
         cells[i, pl.ds(REACH, ROWS)] = own[i]
         return carry
 
-    lax.fori_loop(0, 22, gather, 0)
+    lax.fori_loop(0, 22, gather, 0, unroll=22)
     at = 0
     for away in range(REACH):
         for i in range(1 + away, 21 - away):
@@ -129,7 +129,7 @@
         for away in range(rim):
             for i in (REACH - rim + away, REACH + LAYERS + rim - 1 - away):
                 layer(i, range(REACH - away, REACH + ROWS + away))
-        lax.fori_loop(REACH, REACH + LAYERS, body, 0)
+        lax.fori_loop(REACH, REACH + LAYERS, body, 0, unroll=LAYERS)
 
     def keep(target):
         def store(i, r, value):
@@ -216,6 +216,7 @@
             for group in range(2):
                 row = ((base + i) * ROWS + 8 * group) * FOLDS
                 blocks = [folded[pl.ds(row + s, 8, stride=FOLDS), :] * scale for s in range(FOLDS)]
+                tiles = []
                 for a in range(5):
                     tile = None
                     for s in range(FOLDS):
@@ -224,19 +225,12 @@
                             continue
                         piece = pltpu.roll(blocks[s], (STRIDE * s - LANES * a - HALO) % LANES, 1)
                         tile = piece if tile is None else jnp.where(lane >= low - LANES * a, piece, tile)
-
-                    def store(at, tile=tile):
-                        target[i, pl.ds(8 * group, 8), pl.ds(at, LANES)] = tile
-
-                    if a == 0:
-                        pl.when(core == 0)(functools.partial(store, 0))
-                    elif a == 4:
-                        pl.when(core == 1)(functools.partial(store, 3 * LANES))
-                    else:
-                        store(pl.multiple_of(LANES * (a - core), LANES))
+                    tiles.append(tile)
+                for a in range(4):
+                    target[i, pl.ds(8 * group, 8), pl.ds(LANES * a, LANES)] = jnp.where(core == 0, tiles[a], tiles[a + 1])
             return carry
 
-        lax.fori_loop(0, 8, layer, 0)
+        lax.fori_loop(0, 8, layer, 0, unroll=8)
 
     unfold(own, 8 * core)
     unfold(partner, 8 * (1 - core))
@@ -338,7 +332,9 @@
                 for away in (1, 0, -1)
             ]
         if turn == 0:
-            blueprint = spread(height, 1.0 / HALF, "blueprint")
+            shown, unused = lax.optimization_barrier((height, top))
+            blueprint = spread(shown, 1.0 / HALF, "blueprint")
+            printed, blueprint = lax.optimization_barrier((printed, blueprint))
     return blueprint, spread(printed, 0.5 / HALF, "printed")
 
 

time: 143 us -> 138 us (0.965)
  the two profiles are of different devices: /device:TPU:57 before, /device:TPU:125 now
where the time goes in v2:
time: 138 us
  waiting for transfers between devices  84.1 us (61%)
  starting transfers between devices  42.3 us (31%)
  Pallas kernels  7.06 us (5%)
  other arithmetic  2.98 us (2%)
    ppermute x21, waiting for transfers between devices, local(): lax.ppermute(top, AXES, [(at(2 * turn + c, t), at(2 * turn + 2 + c, t + a...  61 us
    ppermute x21, starting transfers between devices, local(): lax.ppermute(top, AXES, [(at(2 * turn + c, t), at(2 * turn + 2 + c, t + a...  15.8 us
    ppermute x3, starting transfers between devices, swap(): return lax.ppermute(block, 'gz', [(i, i ^ 1) for i in range(slabs)])  11.4 us
    ppermute x2, starting transfers between devices, from_up(): return lax.ppermute(block, 'xy', [(i, i + 1) for i in range(tiles - 1)])  9.21 us
    ppermute x2, waiting for transfers between devices, from_up(): return lax.ppermute(block, 'xy', [(i, i + 1) for i in range(tiles - 1)])  8.26 us
    ppermute x2, waiting for transfers between devices, from_down(): return lax.ppermute(block, 'xy', [(i + 1, i) for i in range(tiles - 1)])  7.96 us
    pallas_call x12, Pallas kernels, call(): pl.pallas_call(kernel, name=name, out_shape=[pltpu.VMEM(shape, jnp.float3...  7.06 us
    ppermute x1, waiting for transfers between devices, local(): lax.ppermute(jnp.where(core == 0, rim_left, rim_right), 'gz', straight)  5.72 us
  transfers between devices with their start and end apart: 30, of which 9 were waited for; matrix products, arithmetic and copies ran while one was open for 1% of the time, Pallas kernels for 0%

profile of v2, /device:TPU:125, one launch (start us, length us, event | category | flops | bytes accessed | tf_op | source)
XLA Modules:
  0.0 137.7 jit_solution(11158097804795500743)
XLA Ops:
  0.6 1.2 slice_select_fusion
  1.9 2.6 %collective-permute-start = (f32[8,16,768]{2,1,0:T(8,128)S(1)}, f32[8,16,768]{2,1,0:T(8,128)S(1)}, u32[]{:S(2)}, u32[]{:S(2)}) collective-permute-start(f32[8,16,768]{2,1,0:T(8,128)S(1)} %slice_select_fusion), channel_id=1, source_target_pairs={{0,32},{32,0},{64,96},{96,64},{128,160},{160,128},{192,224},{224,1... | collective-permute-start | bytes 1179656 | tf_op jit(solution)/shard_map/ppermute | solution.py:264
  5.2 1.3 collective-permute-start.2
  6.5 5.7 %collective-permute-done.2.far = f32[3,16,768]{2,1,0:T(8,128)S(1)} collective-permute-done((f32[3,16,768]{2,1,0:T(8,128)S(1)}, f32[3,16,768]{2,1,0:T(8,128)S(1)}, u32[]{:S(2)}, u32[]{:S(2)}) %collective-permute-start.2) | collective-permute-done | bytes 147488 | tf_op jit(solution)/shard_map/ppermute | solution.py:278
  13.1 4.0 %collective-permute-start.3 = (f32[54,8,128]{2,1,0:T(8,128)S(1)}, f32[54,8,128]{2,1,0:T(8,128)S(1)}, u32[]{:S(2)}, u32[]{:S(2)}) collective-permute-start(f32[54,8,128]{2,1,0:T(8,128)S(1)} %get-tuple-element.31), channel_id=1, source_target_pairs={{0,1},{1,2},{2,3},{3,4},{4,5},{5,6},{6,7},{7,8},{8,9},{9,10},{10,1... | collective-permute-start | bytes 663560 | tf_op jit(solution)/shard_map/ppermute | solution.py:267
  17.1 1.9 %collective-permute-start.4 = (f32[54,8,128]{2,1,0:T(8,128)S(1)}, f32[54,8,128]{2,1,0:T(8,128)S(1)}, u32[]{:S(2)}, u32[]{:S(2)}) collective-permute-start(f32[54,8,128]{2,1,0:T(8,128)S(1)} %get-tuple-element.32), channel_id=1, source_target_pairs={{1,0},{2,1},{3,2},{4,3},{5,4},{6,5},{7,6},{8,7},{9,8},{10,9},{11,1... | collective-permute-start | bytes 663560 | tf_op jit(solution)/shard_map/ppermute | solution.py:270
  19.0 1.3 collective-permute-done.3.up
  20.3 4.6 %collective-permute-done.4.down = f32[54,8,128]{2,1,0:T(8,128)S(1)} collective-permute-done((f32[54,8,128]{2,1,0:T(8,128)S(1)}, f32[54,8,128]{2,1,0:T(8,128)S(1)}, u32[]{:S(2)}, u32[]{:S(2)}) %collective-permute-start.4) | collective-permute-done | bytes 221216 | tf_op jit(solution)/shard_map/ppermute | solution.py:270
  25.0 2.2 %filter.1 = (f32[16,16,8,128]{3,2,1,0:T(8,128)S(1)}, f32[120,8,128]{2,1,0:T(8,128)S(1)}, f32[120,8,128]{2,1,0:T(8,128)S(1)}) custom-call(f32[22,16,8,128]{3,2,1,0:T(8,128)S(1)} %bitcast.5, f32[54,8,128]{2,1,0:T(8,128)S(1)} %collective-permute-done.3.up, f32[54,8,128]{2,1,0:T(8,128)S(1)} %collective-permute-done.4.down), custom_call_target="tpu_custom_call" | custom-call | tf_op jit(solution)/shard_map/filter/pallas_call | solution.py:242
  27.2 5.2 %collective-permute-start.5 = (f32[120,8,128]{2,1,0:T(8,128)S(1)}, f32[120,8,128]{2,1,0:T(8,128)S(1)}, u32[]{:S(2)}, u32[]{:S(2)}) collective-permute-start(f32[120,8,128]{2,1,0:T(8,128)S(1)} %get-tuple-element.34), channel_id=1, source_target_pairs={{0,1},{1,2},{2,3},{3,4},{4,5},{5,6},{6,7},{7,8},{8,9},{9,10},{10,1... | collective-permute-start | bytes 1474568 | tf_op jit(solution)/shard_map/ppermute | solution.py:267
  32.4 1.9 %collective-permute-start.6 = (f32[120,8,128]{2,1,0:T(8,128)S(1)}, f32[120,8,128]{2,1,0:T(8,128)S(1)}, u32[]{:S(2)}, u32[]{:S(2)}) collective-permute-start(f32[120,8,128]{2,1,0:T(8,128)S(1)} %get-tuple-element.35), channel_id=1, source_target_pairs={{1,0},{2,1},{3,2},{4,3},{5,4},{6,5},{7,6},{8,7},{9,8},{10,9},{11,1... | collective-permute-start | bytes 1474568 | tf_op jit(solution)/shard_map/ppermute | solution.py:270
  34.3 7.0 %collective-permute-done.5.refs_1_.refs_4_ = f32[120,8,128]{2,1,0:T(8,128)S(1)} collective-permute-done((f32[120,8,128]{2,1,0:T(8,128)S(1)}, f32[120,8,128]{2,1,0:T(8,128)S(1)}, u32[]{:S(2)}, u32[]{:S(2)}) %collective-permute-start.5) | collective-permute-done | bytes 491552 | tf_op jit(solution)/shard_map/ppermute | solution.py:267
  41.3 3.3 %collective-permute-done.6.refs_2_.refs_5_ = f32[120,8,128]{2,1,0:T(8,128)S(1)} collective-permute-done((f32[120,8,128]{2,1,0:T(8,128)S(1)}, f32[120,8,128]{2,1,0:T(8,128)S(1)}, u32[]{:S(2)}, u32[]{:S(2)}) %collective-permute-start.6) | collective-permute-done | bytes 491552 | tf_op jit(solution)/shard_map/ppermute | solution.py:270
  45.1 5.9 %collective-permute-start.7 = (f32[8,16,512]{2,1,0:T(8,128)S(1)}, f32[8,16,512]{2,1,0:T(8,128)S(1)}, u32[]{:S(2)}, u32[]{:S(2)}) collective-permute-start(f32[8,16,512]{2,1,0:T(8,128)S(1)} %get-tuple-element.40), channel_id=1, source_target_pairs={{0,32},{32,0},{64,96},{96,64},{128,160},{160,128},{192,224},{224,1... | collective-permute-start | bytes 786440 | tf_op jit(solution)/shard_map/ppermute | solution.py:264
  53.0 0.8 maximum_select_fusion
  64.5 1.3 collective-permute-start.26
  65.8 1.3 collective-permute-start.27
  67.1 1.3 collective-permute-start.28
  68.4 55.4 %collective-permute-done.26.refs_0_ = f32[16,8,128]{2,1,0:T(8,128)S(1)} collective-permute-done((f32[16,8,128]{2,1,0:T(8,128)S(1)}, f32[16,8,128]{2,1,0:T(8,128)S(1)}, u32[]{:S(2)}, u32[]{:S(2)}) %collective-permute-start.26) | collective-permute-done | bytes 65568 | tf_op jit(solution)/shard_map/ppermute | solution.py:322
  123.8 1.3 collective-permute-done.27.refs_1_
  125.1 4.3 %collective-permute-done.28.refs_2_ = f32[16,8,128]{2,1,0:T(8,128)S(1)} collective-permute-done((f32[16,8,128]{2,1,0:T(8,128)S(1)}, f32[16,8,128]{2,1,0:T(8,128)S(1)}, u32[]{:S(2)}, u32[]{:S(2)}) %collective-permute-start.28) | collective-permute-done | bytes 65568 | tf_op jit(solution)/shard_map/ppermute | solution.py:322
  129.4 3.0 %chain.15 = (f32[16,16,8,128]{3,2,1,0:T(8,128)S(1)}, f32[16,8,128]{2,1,0:T(8,128)}) custom-call(f32[16,8,128]{2,1,0:T(8,128)S(1)} %collective-permute-done.26.refs_0_, f32[16,8,128]{2,1,0:T(8,128)S(1)} %collective-permute-done.27.refs_1_, f32[16,8,128]{2,1,0:T(8,128)S(1)} %collective-permute-done.28.refs_2_, ...), custom_call_target="tpu_custom_call", output_to_operand_aliasing={{0}: (6, {})} | custom-call | tf_op jit(solution)/shard_map/chain/pallas_call | solution.py:242
  132.7 2.9 %collective-permute-start.29 = (f32[8,16,512]{2,1,0:T(8,128)S(1)}, f32[8,16,512]{2,1,0:T(8,128)S(1)}, u32[]{:S(2)}, u32[]{:S(2)}) collective-permute-start(f32[8,16,512]{2,1,0:T(8,128)S(1)} %get-tuple-element.57), channel_id=1, source_target_pairs={{0,32},{32,0},{64,96},{96,64},{128,160},{160,128},{192,224},{224,1... | collective-permute-start | bytes 786440 | tf_op jit(solution)/shard_map/ppermute | solution.py:264
  135.7 1.1 collective-permute-done.29
  (56 shorter events, 15.5 us)
Async XLA Ops:
  1.9 10.4 %collective-permute-start = (f32[8,16,768]{2,1,0:T(8,128)S(1)}, f32[8,16,768]{2,1,0:T(8,128)S(1)}, u32[]{:S(2)}, u32[]{:S(2)}) collective-permute-start(f32[8,16,768]{2,1,0:T(8,128)S(1)} %slice_select_fusion), channel_id=1, source_target_pairs={{0,32},{32,0},{64,96},{96,64},{128,160},{160,128},{192,224},{224,1... | collective-permute-start | bytes 1179656 | tf_op jit(solution)/shard_map/ppermute | solution.py:264
  4.5 2.0 %collective-permute-start.1 = (f32[3,16,768]{2,1,0:T(8,128)S(1)}, f32[3,16,768]{2,1,0:T(8,128)S(1)}, u32[]{:S(2)}, u32[]{:S(2)}) collective-permute-start(f32[3,16,768]{2,1,0:T(8,128)S(1)} %get-tuple-element.59), channel_id=1, source_target_pairs={{32,64},{64,32},{96,128},{128,96},{160,192},{192,160},{224,256},{2... | collective-permute-start | bytes 442376 | tf_op jit(solution)/shard_map/ppermute | solution.py:277
  5.2 7.0 %collective-permute-start.2 = (f32[3,16,768]{2,1,0:T(8,128)S(1)}, f32[3,16,768]{2,1,0:T(8,128)S(1)}, u32[]{:S(2)}, u32[]{:S(2)}) collective-permute-start(f32[3,16,768]{2,1,0:T(8,128)S(1)} %get-tuple-element.58), channel_id=1, source_target_pairs={{32,96},{64,0},{96,160},{128,64},{160,224},{192,128},{224,288},{25... | collective-permute-start | bytes 442376 | tf_op jit(solution)/shard_map/ppermute | solution.py:278
  13.1 7.2 %collective-permute-start.3 = (f32[54,8,128]{2,1,0:T(8,128)S(1)}, f32[54,8,128]{2,1,0:T(8,128)S(1)}, u32[]{:S(2)}, u32[]{:S(2)}) collective-permute-start(f32[54,8,128]{2,1,0:T(8,128)S(1)} %get-tuple-element.31), channel_id=1, source_target_pairs={{0,1},{1,2},{2,3},{3,4},{4,5},{5,6},{6,7},{7,8},{8,9},{9,10},{10,1... | collective-permute-start | bytes 663560 | tf_op jit(solution)/shard_map/ppermute | solution.py:267
  17.1 7.9 %collective-permute-start.4 = (f32[54,8,128]{2,1,0:T(8,128)S(1)}, f32[54,8,128]{2,1,0:T(8,128)S(1)}, u32[]{:S(2)}, u32[]{:S(2)}) collective-permute-start(f32[54,8,128]{2,1,0:T(8,128)S(1)} %get-tuple-element.32), channel_id=1, source_target_pairs={{1,0},{2,1},{3,2},{4,3},{5,4},{6,5},{7,6},{8,7},{9,8},{10,9},{11,1... | collective-permute-start | bytes 663560 | tf_op jit(solution)/shard_map/ppermute | solution.py:270
  27.2 14.1 %collective-permute-start.5 = (f32[120,8,128]{2,1,0:T(8,128)S(1)}, f32[120,8,128]{2,1,0:T(8,128)S(1)}, u32[]{:S(2)}, u32[]{:S(2)}) collective-permute-start(f32[120,8,128]{2,1,0:T(8,128)S(1)} %get-tuple-element.34), channel_id=1, source_target_pairs={{0,1},{1,2},{2,3},{3,4},{4,5},{5,6},{6,7},{7,8},{8,9},{9,10},{10,1... | collective-permute-start | bytes 1474568 | tf_op jit(solution)/shard_map/ppermute | solution.py:267
  32.4 12.2 %collective-permute-start.6 = (f32[120,8,128]{2,1,0:T(8,128)S(1)}, f32[120,8,128]{2,1,0:T(8,128)S(1)}, u32[]{:S(2)}, u32[]{:S(2)}) collective-permute-start(f32[120,8,128]{2,1,0:T(8,128)S(1)} %get-tuple-element.35), channel_id=1, source_target_pairs={{1,0},{2,1},{3,2},{4,3},{5,4},{6,5},{7,6},{8,7},{9,8},{10,9},{11,1... | collective-permute-start | bytes 1474568 | tf_op jit(solution)/shard_map/ppermute | solution.py:270
  45.1 7.9 %collective-permute-start.7 = (f32[8,16,512]{2,1,0:T(8,128)S(1)}, f32[8,16,512]{2,1,0:T(8,128)S(1)}, u32[]{:S(2)}, u32[]{:S(2)}) collective-permute-start(f32[8,16,512]{2,1,0:T(8,128)S(1)} %get-tuple-element.40), channel_id=1, source_target_pairs={{0,32},{32,0},{64,96},{96,64},{128,160},{160,128},{192,224},{224,1... | collective-permute-start | bytes 786440 | tf_op jit(solution)/shard_map/ppermute | solution.py:264
  51.0 2.9 %collective-permute-start.8 = (f32[16,8,128]{2,1,0:T(8,128)S(1)}, f32[16,8,128]{2,1,0:T(8,128)S(1)}, u32[]{:S(2)}, u32[]{:S(2)}) collective-permute-start(f32[16,8,128]{2,1,0:T(8,128)S(1)} %get-tuple-element.37), channel_id=1, source_target_pairs={{0,65},{1,66},{2,67},{3,68},{4,69},{5,70},{6,71},{7,72},{8,73},{9,... | collective-permute-start | bytes 196616 | tf_op jit(solution)/shard_map/ppermute | solution.py:322
  51.7 2.2 %collective-permute-start.9 = (f32[16,8,128]{2,1,0:T(8,128)S(1)}, f32[16,8,128]{2,1,0:T(8,128)S(1)}, u32[]{:S(2)}, u32[]{:S(2)}) collective-permute-start(f32[16,8,128]{2,1,0:T(8,128)S(1)} %get-tuple-element.37), channel_id=1, source_target_pairs={{0,64},{1,65},{2,66},{3,67},{4,68},{5,69},{6,70},{7,71},{8,72},{9,... | collective-permute-start | bytes 196616 | tf_op jit(solution)/shard_map/ppermute | solution.py:322
  52.3 1.5 %collective-permute-start.10 = (f32[16,8,128]{2,1,0:T(8,128)S(1)}, f32[16,8,128]{2,1,0:T(8,128)S(1)}, u32[]{:S(2)}, u32[]{:S(2)}) collective-permute-start(f32[16,8,128]{2,1,0:T(8,128)S(1)} %get-tuple-element.37), channel_id=1, source_target_pairs={{1,64},{2,65},{3,66},{4,67},{5,68},{6,69},{7,70},{8,71},{9,72},{10... | collective-permute-start | bytes 196616 | tf_op jit(solution)/shard_map/ppermute | solution.py:322
  53.9 2.0 %collective-permute-start.11 = (f32[16,8,128]{2,1,0:T(8,128)S(1)}, f32[16,8,128]{2,1,0:T(8,128)S(1)}, u32[]{:S(2)}, u32[]{:S(2)}) collective-permute-start(f32[16,8,128]{2,1,0:T(8,128)S(1)} %get-tuple-element.43), channel_id=1, source_target_pairs={{64,129},{65,130},{66,131},{67,132},{68,133},{69,134},{70,135},{71... | collective-permute-start | bytes 196616 | tf_op jit(solution)/shard_map/ppermute | solution.py:322
  54.6 1.4 collective-permute-start.12
  56.0 2.0 %collective-permute-start.14 = (f32[16,8,128]{2,1,0:T(8,128)S(1)}, f32[16,8,128]{2,1,0:T(8,128)S(1)}, u32[]{:S(2)}, u32[]{:S(2)}) collective-permute-start(f32[16,8,128]{2,1,0:T(8,128)S(1)} %get-tuple-element.45), channel_id=1, source_target_pairs={{128,193},{129,194},{130,195},{131,196},{132,197},{133,198},{134,1... | collective-permute-start | bytes 196616 | tf_op jit(solution)/shard_map/ppermute | solution.py:322
  56.7 1.4 collective-permute-start.15
  58.2 2.0 %collective-permute-start.17 = (f32[16,8,128]{2,1,0:T(8,128)S(1)}, f32[16,8,128]{2,1,0:T(8,128)S(1)}, u32[]{:S(2)}, u32[]{:S(2)}) collective-permute-start(f32[16,8,128]{2,1,0:T(8,128)S(1)} %get-tuple-element.47), channel_id=1, source_target_pairs={{192,257},{193,258},{194,259},{195,260},{196,261},{197,262},{198,2... | collective-permute-start | bytes 196616 | tf_op jit(solution)/shard_map/ppermute | solution.py:322
  58.9 1.4 collective-permute-start.18
  60.3 2.0 %collective-permute-start.20 = (f32[16,8,128]{2,1,0:T(8,128)S(1)}, f32[16,8,128]{2,1,0:T(8,128)S(1)}, u32[]{:S(2)}, u32[]{:S(2)}) collective-permute-start(f32[16,8,128]{2,1,0:T(8,128)S(1)} %get-tuple-element.49), channel_id=1, source_target_pairs={{256,321},{257,322},{258,323},{259,324},{260,325},{261,326},{262,3... | collective-permute-start | bytes 196616 | tf_op jit(solution)/shard_map/ppermute | solution.py:322
  61.0 1.4 collective-permute-start.21
  62.4 2.0 %collective-permute-start.23 = (f32[16,8,128]{2,1,0:T(8,128)S(1)}, f32[16,8,128]{2,1,0:T(8,128)S(1)}, u32[]{:S(2)}, u32[]{:S(2)}) collective-permute-start(f32[16,8,128]{2,1,0:T(8,128)S(1)} %get-tuple-element.51), channel_id=1, source_target_pairs={{320,385},{321,386},{322,387},{323,388},{324,389},{325,390},{326,3... | collective-permute-start | bytes 196616 | tf_op jit(solution)/shard_map/ppermute | solution.py:322
  64.5 59.3 %collective-permute-start.26 = (f32[16,8,128]{2,1,0:T(8,128)S(1)}, f32[16,8,128]{2,1,0:T(8,128)S(1)}, u32[]{:S(2)}, u32[]{:S(2)}) collective-permute-start(f32[16,8,128]{2,1,0:T(8,128)S(1)} %get-tuple-element.53), channel_id=1, source_target_pairs={{384,449},{385,450},{386,451},{387,452},{388,453},{389,454},{390,4... | collective-permute-start | bytes 196616 | tf_op jit(solution)/shard_map/ppermute | solution.py:322
  65.8 59.3 %collective-permute-start.27 = (f32[16,8,128]{2,1,0:T(8,128)S(1)}, f32[16,8,128]{2,1,0:T(8,128)S(1)}, u32[]{:S(2)}, u32[]{:S(2)}) collective-permute-start(f32[16,8,128]{2,1,0:T(8,128)S(1)} %get-tuple-element.53), channel_id=1, source_target_pairs={{384,448},{385,449},{386,450},{387,451},{388,452},{389,453},{390,4... | collective-permute-start | bytes 196616 | tf_op jit(solution)/shard_map/ppermute | solution.py:322
  67.1 62.3 %collective-permute-start.28 = (f32[16,8,128]{2,1,0:T(8,128)S(1)}, f32[16,8,128]{2,1,0:T(8,128)S(1)}, u32[]{:S(2)}, u32[]{:S(2)}) collective-permute-start(f32[16,8,128]{2,1,0:T(8,128)S(1)} %get-tuple-element.53), channel_id=1, source_target_pairs={{385,448},{386,449},{387,450},{388,451},{389,452},{390,453},{391,4... | collective-permute-start | bytes 196616 | tf_op jit(solution)/shard_map/ppermute | solution.py:322
  132.7 4.1 %collective-permute-start.29 = (f32[8,16,512]{2,1,0:T(8,128)S(1)}, f32[8,16,512]{2,1,0:T(8,128)S(1)}, u32[]{:S(2)}, u32[]{:S(2)}) collective-permute-start(f32[8,16,512]{2,1,0:T(8,128)S(1)} %get-tuple-element.57), channel_id=1, source_target_pairs={{0,32},{32,0},{64,96},{96,64},{128,160},{160,128},{192,224},{224,1... | collective-permute-start | bytes 786440 | tf_op jit(solution)/shard_map/ppermute | solution.py:264
  (7 other events, 8.7 us)

commit v3 on v2

--- a/solution.py
+++ b/solution.py
@@ -154,7 +154,7 @@
 
 def chain_kernel(turn, count_tiles, *refs):
     if turn:
-        up, middle, down, height, height_up, height_down, unused, printed, top, even, odd = refs
+        up, down, middle, height, height_up, height_down, unused, printed, top, even, odd = refs
     else:
         height, height_up, height_down, unused, printed, top, even, odd = refs
     chip, core, tile = place()
@@ -300,11 +300,16 @@
             [(8, ROWS, 512), (8, ROWS, 512)],
             [folded.reshape(LAYERS * ROWS * FOLDS, LANES)],
         )
-        other = swap(other)
+        return own, swap(other)
+
+    def assemble(own, other):
         return jnp.where(
             core == 0, jnp.concatenate([own, other], axis=2), jnp.concatenate([other, own], axis=2)
         )
 
+    shown, height_up = lax.optimization_barrier((height, height_up))
+    shown = spread(shown, 1.0 / HALF, "blueprint")
+    height, shown = lax.optimization_barrier((height, shown))
     printed = jnp.zeros((LAYERS, ROWS, *block), jnp.float32)
     received = []
     for turn in range(chips):
@@ -329,13 +334,11 @@
                         if 0 <= t + away < tiles
                     ],
                 )
-                for away in (1, 0, -1)
+                for away in (1, -1, 0)
             ]
         if turn == 0:
-            shown, unused = lax.optimization_barrier((height, top))
-            blueprint = spread(shown, 1.0 / HALF, "blueprint")
-            printed, blueprint = lax.optimization_barrier((printed, blueprint))
-    return blueprint, spread(printed, 0.5 / HALF, "printed")
+            printed, blueprint = lax.optimization_barrier((printed, assemble(*shown)))
+    return blueprint, assemble(*spread(printed, 0.5 / HALF, "printed"))
 
 
 def solution(mesh):

time: 138 us -> 132 us (0.957)
  the two profiles are of different devices: /device:TPU:125 before, /device:TPU:63 now
where the time goes in v3:
time: 132 us
  waiting for transfers between devices  71 us (54%)
  starting transfers between devices  49.3 us (37%)
  Pallas kernels  7.05 us (5%)
  other arithmetic  2.98 us (2%)
    ppermute x21, waiting for transfers between devices, local(): lax.ppermute(top, AXES, [(at(2 * turn + c, t), at(2 * turn + 2 + c, t + a...  52.8 us
    ppermute x21, starting transfers between devices, local(): lax.ppermute(top, AXES, [(at(2 * turn + c, t), at(2 * turn + 2 + c, t + a...  15.8 us
    ppermute x2, starting transfers between devices, from_down(): return lax.ppermute(block, 'xy', [(i + 1, i) for i in range(tiles - 1)])  15.1 us
    ppermute x3, starting transfers between devices, swap(): return lax.ppermute(block, 'gz', [(i, i ^ 1) for i in range(slabs)])  10.6 us
    ppermute x2, waiting for transfers between devices, from_up(): return lax.ppermute(block, 'xy', [(i, i + 1) for i in range(tiles - 1)])  9.29 us
    pallas_call x12, Pallas kernels, call(): pl.pallas_call(kernel, name=name, out_shape=[pltpu.VMEM(shape, jnp.float3...  7.05 us
    ppermute x2, starting transfers between devices, from_up(): return lax.ppermute(block, 'xy', [(i, i + 1) for i in range(tiles - 1)])  5.92 us
    ppermute x1, waiting for transfers between devices, local(): lax.ppermute(jnp.where(core == 0, rim_left, rim_right), 'gz', straight)  5.72 us
  transfers between devices with their start and end apart: 30, of which 9 were waited for; matrix products, arithmetic and copies ran while one was open for 1% of the time, Pallas kernels for 0%

profile of v3, /device:TPU:63, one launch (start us, length us, event | category | flops | bytes accessed | tf_op | source)
XLA Modules:
  0.0 131.6 jit_solution(10481995465874314279)
XLA Ops:
  0.6 1.2 slice_select_fusion
  1.9 2.6 %collective-permute-start = (f32[8,16,768]{2,1,0:T(8,128)S(1)}, f32[8,16,768]{2,1,0:T(8,128)S(1)}, u32[]{:S(2)}, u32[]{:S(2)}) collective-permute-start(f32[8,16,768]{2,1,0:T(8,128)S(1)} %slice_select_fusion), channel_id=1, source_target_pairs={{0,32},{32,0},{64,96},{96,64},{128,160},{160,128},{192,224},{224,1... | collective-permute-start | bytes 1179656 | tf_op jit(solution)/shard_map/ppermute | solution.py:264
  5.2 1.3 collective-permute-start.2
  6.5 5.7 %collective-permute-done.2.far = f32[3,16,768]{2,1,0:T(8,128)S(1)} collective-permute-done((f32[3,16,768]{2,1,0:T(8,128)S(1)}, f32[3,16,768]{2,1,0:T(8,128)S(1)}, u32[]{:S(2)}, u32[]{:S(2)}) %collective-permute-start.2) | collective-permute-done | bytes 147488 | tf_op jit(solution)/shard_map/ppermute | solution.py:278
  13.1 4.0 %collective-permute-start.3 = (f32[54,8,128]{2,1,0:T(8,128)S(1)}, f32[54,8,128]{2,1,0:T(8,128)S(1)}, u32[]{:S(2)}, u32[]{:S(2)}) collective-permute-start(f32[54,8,128]{2,1,0:T(8,128)S(1)} %get-tuple-element.35), channel_id=1, source_target_pairs={{0,1},{1,2},{2,3},{3,4},{4,5},{5,6},{6,7},{7,8},{8,9},{9,10},{10,1... | collective-permute-start | bytes 663560 | tf_op jit(solution)/shard_map/ppermute | solution.py:267
  17.1 8.9 %collective-permute-start.4 = (f32[54,8,128]{2,1,0:T(8,128)S(1)}, f32[54,8,128]{2,1,0:T(8,128)S(1)}, u32[]{:S(2)}, u32[]{:S(2)}) collective-permute-start(f32[54,8,128]{2,1,0:T(8,128)S(1)} %get-tuple-element.36), channel_id=1, source_target_pairs={{1,0},{2,1},{3,2},{4,3},{5,4},{6,5},{7,6},{8,7},{9,8},{10,9},{11,1... | collective-permute-start | bytes 663560 | tf_op jit(solution)/shard_map/ppermute | solution.py:270
  25.9 2.2 %collective-permute-done.3.up = f32[54,8,128]{2,1,0:T(8,128)S(1)} collective-permute-done((f32[54,8,128]{2,1,0:T(8,128)S(1)}, f32[54,8,128]{2,1,0:T(8,128)S(1)}, u32[]{:S(2)}, u32[]{:S(2)}) %collective-permute-start.3) | collective-permute-done | bytes 221216 | tf_op jit(solution)/shard_map/ppermute | solution.py:267
  28.2 0.9 collective-permute-done.4.down
  29.1 2.2 %filter.1 = (f32[16,16,8,128]{3,2,1,0:T(8,128)S(1)}, f32[120,8,128]{2,1,0:T(8,128)S(1)}, f32[120,8,128]{2,1,0:T(8,128)S(1)}) custom-call(f32[22,16,8,128]{3,2,1,0:T(8,128)S(1)} %bitcast.5, f32[54,8,128]{2,1,0:T(8,128)S(1)} %collective-permute-done.3.up, f32[54,8,128]{2,1,0:T(8,128)S(1)} %collective-permute-done.4.down), custom_call_target="tpu_custom_call" | custom-call | tf_op jit(solution)/shard_map/filter/pallas_call | solution.py:242
  31.3 1.9 %collective-permute-start.5 = (f32[120,8,128]{2,1,0:T(8,128)S(1)}, f32[120,8,128]{2,1,0:T(8,128)S(1)}, u32[]{:S(2)}, u32[]{:S(2)}) collective-permute-start(f32[120,8,128]{2,1,0:T(8,128)S(1)} %get-tuple-element.38), channel_id=1, source_target_pairs={{0,1},{1,2},{2,3},{3,4},{4,5},{5,6},{6,7},{7,8},{8,9},{9,10},{10,1... | collective-permute-start | bytes 1474568 | tf_op jit(solution)/shard_map/ppermute | solution.py:267
  33.2 6.2 %collective-permute-start.7 = (f32[120,8,128]{2,1,0:T(8,128)S(1)}, f32[120,8,128]{2,1,0:T(8,128)S(1)}, u32[]{:S(2)}, u32[]{:S(2)}) collective-permute-start(f32[120,8,128]{2,1,0:T(8,128)S(1)} %get-tuple-element.44), channel_id=1, source_target_pairs={{1,0},{2,1},{3,2},{4,3},{5,4},{6,5},{7,6},{8,7},{9,8},{10,9},{11,1... | collective-permute-start | bytes 1474568 | tf_op jit(solution)/shard_map/ppermute | solution.py:270
  39.4 7.1 %collective-permute-done.5.refs_1_.refs_4_ = f32[120,8,128]{2,1,0:T(8,128)S(1)} collective-permute-done((f32[120,8,128]{2,1,0:T(8,128)S(1)}, f32[120,8,128]{2,1,0:T(8,128)S(1)}, u32[]{:S(2)}, u32[]{:S(2)}) %collective-permute-start.5) | collective-permute-done | bytes 491552 | tf_op jit(solution)/shard_map/ppermute | solution.py:267
  46.9 5.1 %collective-permute-start.6 = (f32[8,16,512]{2,1,0:T(8,128)S(1)}, f32[8,16,512]{2,1,0:T(8,128)S(1)}, u32[]{:S(2)}, u32[]{:S(2)}) collective-permute-start(f32[8,16,512]{2,1,0:T(8,128)S(1)} %get-tuple-element.41), channel_id=1, source_target_pairs={{0,32},{32,0},{64,96},{96,64},{128,160},{160,128},{192,224},{224,1... | collective-permute-start | bytes 786440 | tf_op jit(solution)/shard_map/ppermute | solution.py:264
  51.9 1.1 collective-permute-done.6
  55.2 0.8 maximum_select_fusion
  66.7 1.3 collective-permute-start.26
  68.0 1.3 collective-permute-start.27
  69.3 1.3 collective-permute-start.28
  70.6 50.7 %collective-permute-done.26.refs_0_ = f32[16,8,128]{2,1,0:T(8,128)S(1)} collective-permute-done((f32[16,8,128]{2,1,0:T(8,128)S(1)}, f32[16,8,128]{2,1,0:T(8,128)S(1)}, u32[]{:S(2)}, u32[]{:S(2)}) %collective-permute-start.26) | collective-permute-done | bytes 65568 | tf_op jit(solution)/shard_map/ppermute | solution.py:327
  121.4 1.9 %collective-permute-done.28.refs_2_ = f32[16,8,128]{2,1,0:T(8,128)S(1)} collective-permute-done((f32[16,8,128]{2,1,0:T(8,128)S(1)}, f32[16,8,128]{2,1,0:T(8,128)S(1)}, u32[]{:S(2)}, u32[]{:S(2)}) %collective-permute-start.28) | collective-permute-done | bytes 65568 | tf_op jit(solution)/shard_map/ppermute | solution.py:327
  123.3 3.0 %chain.15 = (f32[16,16,8,128]{3,2,1,0:T(8,128)S(1)}, f32[16,8,128]{2,1,0:T(8,128)}) custom-call(f32[16,8,128]{2,1,0:T(8,128)S(1)} %collective-permute-done.26.refs_0_, f32[16,8,128]{2,1,0:T(8,128)S(1)} %collective-permute-done.27.refs_1_, f32[16,8,128]{2,1,0:T(8,128)S(1)} %collective-permute-done.28.refs_2_, ...), custom_call_target="tpu_custom_call", output_to_operand_aliasing={{0}: (6, {})} | custom-call | tf_op jit(solution)/shard_map/chain/pallas_call | solution.py:242
  126.7 2.9 %collective-permute-start.29 = (f32[8,16,512]{2,1,0:T(8,128)S(1)}, f32[8,16,512]{2,1,0:T(8,128)S(1)}, u32[]{:S(2)}, u32[]{:S(2)}) collective-permute-start(f32[8,16,512]{2,1,0:T(8,128)S(1)} %get-tuple-element.65), channel_id=1, source_target_pairs={{0,32},{32,0},{64,96},{96,64},{128,160},{160,128},{192,224},{224,1... | collective-permute-start | bytes 786440 | tf_op jit(solution)/shard_map/ppermute | solution.py:264
  129.6 1.1 collective-permute-done.29
  130.8 0.8 maximum_select_fusion.1
  (56 shorter events, 14.8 us)
Async XLA Ops:
  1.9 10.4 %collective-permute-start = (f32[8,16,768]{2,1,0:T(8,128)S(1)}, f32[8,16,768]{2,1,0:T(8,128)S(1)}, u32[]{:S(2)}, u32[]{:S(2)}) collective-permute-start(f32[8,16,768]{2,1,0:T(8,128)S(1)} %slice_select_fusion), channel_id=1, source_target_pairs={{0,32},{32,0},{64,96},{96,64},{128,160},{160,128},{192,224},{224,1... | collective-permute-start | bytes 1179656 | tf_op jit(solution)/shard_map/ppermute | solution.py:264
  4.5 2.0 %collective-permute-start.1 = (f32[3,16,768]{2,1,0:T(8,128)S(1)}, f32[3,16,768]{2,1,0:T(8,128)S(1)}, u32[]{:S(2)}, u32[]{:S(2)}) collective-permute-start(f32[3,16,768]{2,1,0:T(8,128)S(1)} %get-tuple-element.67), channel_id=1, source_target_pairs={{32,64},{64,32},{96,128},{128,96},{160,192},{192,160},{224,256},{2... | collective-permute-start | bytes 442376 | tf_op jit(solution)/shard_map/ppermute | solution.py:277
  5.2 7.0 %collective-permute-start.2 = (f32[3,16,768]{2,1,0:T(8,128)S(1)}, f32[3,16,768]{2,1,0:T(8,128)S(1)}, u32[]{:S(2)}, u32[]{:S(2)}) collective-permute-start(f32[3,16,768]{2,1,0:T(8,128)S(1)} %get-tuple-element.66), channel_id=1, source_target_pairs={{32,96},{64,0},{96,160},{128,64},{160,224},{192,128},{224,288},{25... | collective-permute-start | bytes 442376 | tf_op jit(solution)/shard_map/ppermute | solution.py:278
  13.1 15.1 %collective-permute-start.3 = (f32[54,8,128]{2,1,0:T(8,128)S(1)}, f32[54,8,128]{2,1,0:T(8,128)S(1)}, u32[]{:S(2)}, u32[]{:S(2)}) collective-permute-start(f32[54,8,128]{2,1,0:T(8,128)S(1)} %get-tuple-element.35), channel_id=1, source_target_pairs={{0,1},{1,2},{2,3},{3,4},{4,5},{5,6},{6,7},{7,8},{8,9},{9,10},{10,1... | collective-permute-start | bytes 663560 | tf_op jit(solution)/shard_map/ppermute | solution.py:267
  17.1 12.0 %collective-permute-start.4 = (f32[54,8,128]{2,1,0:T(8,128)S(1)}, f32[54,8,128]{2,1,0:T(8,128)S(1)}, u32[]{:S(2)}, u32[]{:S(2)}) collective-permute-start(f32[54,8,128]{2,1,0:T(8,128)S(1)} %get-tuple-element.36), channel_id=1, source_target_pairs={{1,0},{2,1},{3,2},{4,3},{5,4},{6,5},{7,6},{8,7},{9,8},{10,9},{11,1... | collective-permute-start | bytes 663560 | tf_op jit(solution)/shard_map/ppermute | solution.py:270
  31.3 15.2 %collective-permute-start.5 = (f32[120,8,128]{2,1,0:T(8,128)S(1)}, f32[120,8,128]{2,1,0:T(8,128)S(1)}, u32[]{:S(2)}, u32[]{:S(2)}) collective-permute-start(f32[120,8,128]{2,1,0:T(8,128)S(1)} %get-tuple-element.38), channel_id=1, source_target_pairs={{0,1},{1,2},{2,3},{3,4},{4,5},{5,6},{6,7},{7,8},{8,9},{9,10},{10,1... | collective-permute-start | bytes 1474568 | tf_op jit(solution)/shard_map/ppermute | solution.py:267
  33.2 19.9 %collective-permute-start.7 = (f32[120,8,128]{2,1,0:T(8,128)S(1)}, f32[120,8,128]{2,1,0:T(8,128)S(1)}, u32[]{:S(2)}, u32[]{:S(2)}) collective-permute-start(f32[120,8,128]{2,1,0:T(8,128)S(1)} %get-tuple-element.44), channel_id=1, source_target_pairs={{1,0},{2,1},{3,2},{4,3},{5,4},{6,5},{7,6},{8,7},{9,8},{10,9},{11,1... | collective-permute-start | bytes 1474568 | tf_op jit(solution)/shard_map/ppermute | solution.py:270
  46.9 6.2 %collective-permute-start.6 = (f32[8,16,512]{2,1,0:T(8,128)S(1)}, f32[8,16,512]{2,1,0:T(8,128)S(1)}, u32[]{:S(2)}, u32[]{:S(2)}) collective-permute-start(f32[8,16,512]{2,1,0:T(8,128)S(1)} %get-tuple-element.41), channel_id=1, source_target_pairs={{0,32},{32,0},{64,96},{96,64},{128,160},{160,128},{192,224},{224,1... | collective-permute-start | bytes 786440 | tf_op jit(solution)/shard_map/ppermute | solution.py:264
  53.2 2.9 %collective-permute-start.8 = (f32[16,8,128]{2,1,0:T(8,128)S(1)}, f32[16,8,128]{2,1,0:T(8,128)S(1)}, u32[]{:S(2)}, u32[]{:S(2)}) collective-permute-start(f32[16,8,128]{2,1,0:T(8,128)S(1)} %get-tuple-element.49), channel_id=1, source_target_pairs={{0,65},{1,66},{2,67},{3,68},{4,69},{5,70},{6,71},{7,72},{8,73},{9,... | collective-permute-start | bytes 196616 | tf_op jit(solution)/shard_map/ppermute | solution.py:327
  53.9 2.2 %collective-permute-start.9 = (f32[16,8,128]{2,1,0:T(8,128)S(1)}, f32[16,8,128]{2,1,0:T(8,128)S(1)}, u32[]{:S(2)}, u32[]{:S(2)}) collective-permute-start(f32[16,8,128]{2,1,0:T(8,128)S(1)} %get-tuple-element.49), channel_id=1, source_target_pairs={{1,64},{2,65},{3,66},{4,67},{5,68},{6,69},{7,70},{8,71},{9,72},{10... | collective-permute-start | bytes 196616 | tf_op jit(solution)/shard_map/ppermute | solution.py:327
  54.5 1.5 %collective-permute-start.10 = (f32[16,8,128]{2,1,0:T(8,128)S(1)}, f32[16,8,128]{2,1,0:T(8,128)S(1)}, u32[]{:S(2)}, u32[]{:S(2)}) collective-permute-start(f32[16,8,128]{2,1,0:T(8,128)S(1)} %get-tuple-element.49), channel_id=1, source_target_pairs={{0,64},{1,65},{2,66},{3,67},{4,68},{5,69},{6,70},{7,71},{8,72},{9,... | collective-permute-start | bytes 196616 | tf_op jit(solution)/shard_map/ppermute | solution.py:327
  56.1 2.0 %collective-permute-start.11 = (f32[16,8,128]{2,1,0:T(8,128)S(1)}, f32[16,8,128]{2,1,0:T(8,128)S(1)}, u32[]{:S(2)}, u32[]{:S(2)}) collective-permute-start(f32[16,8,128]{2,1,0:T(8,128)S(1)} %get-tuple-element.51), channel_id=1, source_target_pairs={{64,129},{65,130},{66,131},{67,132},{68,133},{69,134},{70,135},{71... | collective-permute-start | bytes 196616 | tf_op jit(solution)/shard_map/ppermute | solution.py:327
  56.8 1.4 %collective-permute-start.12 = (f32[16,8,128]{2,1,0:T(8,128)S(1)}, f32[16,8,128]{2,1,0:T(8,128)S(1)}, u32[]{:S(2)}, u32[]{:S(2)}) collective-permute-start(f32[16,8,128]{2,1,0:T(8,128)S(1)} %get-tuple-element.51), channel_id=1, source_target_pairs={{65,128},{66,129},{67,130},{68,131},{69,132},{70,133},{71,134},{72... | collective-permute-start | bytes 196616 | tf_op jit(solution)/shard_map/ppermute | solution.py:327
  58.2 2.0 %collective-permute-start.14 = (f32[16,8,128]{2,1,0:T(8,128)S(1)}, f32[16,8,128]{2,1,0:T(8,128)S(1)}, u32[]{:S(2)}, u32[]{:S(2)}) collective-permute-start(f32[16,8,128]{2,1,0:T(8,128)S(1)} %get-tuple-element.53), channel_id=1, source_target_pairs={{128,193},{129,194},{130,195},{131,196},{132,197},{133,198},{134,1... | collective-permute-start | bytes 196616 | tf_op jit(solution)/shard_map/ppermute | solution.py:327
  58.9 1.4 %collective-permute-start.15 = (f32[16,8,128]{2,1,0:T(8,128)S(1)}, f32[16,8,128]{2,1,0:T(8,128)S(1)}, u32[]{:S(2)}, u32[]{:S(2)}) collective-permute-start(f32[16,8,128]{2,1,0:T(8,128)S(1)} %get-tuple-element.53), channel_id=1, source_target_pairs={{129,192},{130,193},{131,194},{132,195},{133,196},{134,197},{135,1... | collective-permute-start | bytes 196616 | tf_op jit(solution)/shard_map/ppermute | solution.py:327
  60.4 2.0 %collective-permute-start.17 = (f32[16,8,128]{2,1,0:T(8,128)S(1)}, f32[16,8,128]{2,1,0:T(8,128)S(1)}, u32[]{:S(2)}, u32[]{:S(2)}) collective-permute-start(f32[16,8,128]{2,1,0:T(8,128)S(1)} %get-tuple-element.55), channel_id=1, source_target_pairs={{192,257},{193,258},{194,259},{195,260},{196,261},{197,262},{198,2... | collective-permute-start | bytes 196616 | tf_op jit(solution)/shard_map/ppermute | solution.py:327
  61.1 1.4 %collective-permute-start.18 = (f32[16,8,128]{2,1,0:T(8,128)S(1)}, f32[16,8,128]{2,1,0:T(8,128)S(1)}, u32[]{:S(2)}, u32[]{:S(2)}) collective-permute-start(f32[16,8,128]{2,1,0:T(8,128)S(1)} %get-tuple-element.55), channel_id=1, source_target_pairs={{193,256},{194,257},{195,258},{196,259},{197,260},{198,261},{199,2... | collective-permute-start | bytes 196616 | tf_op jit(solution)/shard_map/ppermute | solution.py:327
  62.5 2.0 %collective-permute-start.20 = (f32[16,8,128]{2,1,0:T(8,128)S(1)}, f32[16,8,128]{2,1,0:T(8,128)S(1)}, u32[]{:S(2)}, u32[]{:S(2)}) collective-permute-start(f32[16,8,128]{2,1,0:T(8,128)S(1)} %get-tuple-element.57), channel_id=1, source_target_pairs={{256,321},{257,322},{258,323},{259,324},{260,325},{261,326},{262,3... | collective-permute-start | bytes 196616 | tf_op jit(solution)/shard_map/ppermute | solution.py:327
  63.2 1.4 %collective-permute-start.21 = (f32[16,8,128]{2,1,0:T(8,128)S(1)}, f32[16,8,128]{2,1,0:T(8,128)S(1)}, u32[]{:S(2)}, u32[]{:S(2)}) collective-permute-start(f32[16,8,128]{2,1,0:T(8,128)S(1)} %get-tuple-element.57), channel_id=1, source_target_pairs={{257,320},{258,321},{259,322},{260,323},{261,324},{262,325},{263,3... | collective-permute-start | bytes 196616 | tf_op jit(solution)/shard_map/ppermute | solution.py:327
  64.6 2.0 %collective-permute-start.23 = (f32[16,8,128]{2,1,0:T(8,128)S(1)}, f32[16,8,128]{2,1,0:T(8,128)S(1)}, u32[]{:S(2)}, u32[]{:S(2)}) collective-permute-start(f32[16,8,128]{2,1,0:T(8,128)S(1)} %get-tuple-element.59), channel_id=1, source_target_pairs={{320,385},{321,386},{322,387},{323,388},{324,389},{325,390},{326,3... | collective-permute-start | bytes 196616 | tf_op jit(solution)/shard_map/ppermute | solution.py:327
  66.7 54.6 %collective-permute-start.26 = (f32[16,8,128]{2,1,0:T(8,128)S(1)}, f32[16,8,128]{2,1,0:T(8,128)S(1)}, u32[]{:S(2)}, u32[]{:S(2)}) collective-permute-start(f32[16,8,128]{2,1,0:T(8,128)S(1)} %get-tuple-element.61), channel_id=1, source_target_pairs={{384,449},{385,450},{386,451},{387,452},{388,453},{389,454},{390,4... | collective-permute-start | bytes 196616 | tf_op jit(solution)/shard_map/ppermute | solution.py:327
  68.0 53.4 %collective-permute-start.27 = (f32[16,8,128]{2,1,0:T(8,128)S(1)}, f32[16,8,128]{2,1,0:T(8,128)S(1)}, u32[]{:S(2)}, u32[]{:S(2)}) collective-permute-start(f32[16,8,128]{2,1,0:T(8,128)S(1)} %get-tuple-element.61), channel_id=1, source_target_pairs={{385,448},{386,449},{387,450},{388,451},{389,452},{390,453},{391,4... | collective-permute-start | bytes 196616 | tf_op jit(solution)/shard_map/ppermute | solution.py:327
  69.3 54.1 %collective-permute-start.28 = (f32[16,8,128]{2,1,0:T(8,128)S(1)}, f32[16,8,128]{2,1,0:T(8,128)S(1)}, u32[]{:S(2)}, u32[]{:S(2)}) collective-permute-start(f32[16,8,128]{2,1,0:T(8,128)S(1)} %get-tuple-element.61), channel_id=1, source_target_pairs={{384,448},{385,449},{386,450},{387,451},{388,452},{389,453},{390,4... | collective-permute-start | bytes 196616 | tf_op jit(solution)/shard_map/ppermute | solution.py:327
  126.7 4.1 %collective-permute-start.29 = (f32[8,16,512]{2,1,0:T(8,128)S(1)}, f32[8,16,512]{2,1,0:T(8,128)S(1)}, u32[]{:S(2)}, u32[]{:S(2)}) collective-permute-start(f32[8,16,512]{2,1,0:T(8,128)S(1)} %get-tuple-element.65), channel_id=1, source_target_pairs={{0,32},{32,0},{64,96},{96,64},{128,160},{160,128},{192,224},{224,1... | collective-permute-start | bytes 786440 | tf_op jit(solution)/shard_map/ppermute | solution.py:264
  (7 other events, 8.7 us)

commit v4 on v3

--- a/solution.py
+++ b/solution.py
@@ -44,6 +44,31 @@
     fold = lax.broadcasted_iota(jnp.int32, (FOLDS, LANES), 0)
     column = 384 * core + STRIDE * fold + lane_of() - HALO
     return (column >= 0) & (column < 1024)
+
+
+def fold_rows(tiles, lane, store):
+    for s in range(FOLDS):
+        a, shift = divmod(LANES - HALO + STRIDE * s, LANES)
+        block = tiles[a]
+        if shift:
+            first = pltpu.roll(tiles[a], LANES - shift, 1)
+            second = pltpu.roll(tiles[a + 1], LANES - shift, 1)
+            block = jnp.where(lane < LANES - shift, first, second)
+        store(s, block)
+
+
+def unfold_rows(blocks, lane):
+    tiles = []
+    for a in range(5):
+        tile = None
+        for s in range(FOLDS):
+            low = max(LANES * a, STRIDE * s)
+            if low >= min(LANES * a + LANES, STRIDE * s + STRIDE):
+                continue
+            piece = pltpu.roll(blocks[s], (STRIDE * s - LANES * a - HALO) % LANES, 1)
+            tile = piece if tile is None else jnp.where(lane >= low - LANES * a, piece, tile)
+        tiles.append(tile)
+    return tiles
 
 
 def fold_kernel(own, partner, near, far, out, to_down, to_up):
@@ -62,15 +87,12 @@
                     if a == 6:
                         tile = jnp.where(core == 1, 0.0, tile)
                     tiles.append(tile)
-                for s in range(FOLDS):
-                    a, shift = divmod(LANES - HALO + STRIDE * s, LANES)
-                    block = tiles[a]
-                    if shift:
-                        first = pltpu.roll(tiles[a], LANES - shift, 1)
-                        second = pltpu.roll(tiles[a + 1], LANES - shift, 1)
-                        block = jnp.where(lane < LANES - shift, first, second)
-                    row = ((base + i) * ROWS + 8 * group) * FOLDS
+                row = ((base + i) * ROWS + 8 * group) * FOLDS
+
+                def store(s, block):
                     out[pl.ds(row + s, 8, stride=FOLDS), :] = block
+
+                fold_rows(tiles, lane, store)
             return carry
 
         lax.fori_loop(0, count, layer, 0, unroll=count)
@@ -87,7 +109,7 @@
             at += 1
 
 
-def filter_kernel(count_chips, count_tiles, own, up, down, height, to_down, to_up, cells, first, second):
+def filter_kernel(count_chips, count_tiles, own, up, down, height, to_down, to_up, cells, first, second, packed):
     chip, core, tile = place()
     inside = column_mask(core)
     scale = jnp.where(inside, 1.0 / (1.0 + 6.0 * FILTER_R2), 0.0)
@@ -147,25 +169,45 @@
     sweep(cells, 1, keep(first))
     sweep(first, 2, keep(second))
     sweep(second, 3, project)
-    for k in range(15):
-        to_down[pl.ds(MARGIN_AT[k], 15 - k)] = height[k, pl.ds(k + 1, 15 - k)]
-        to_up[pl.ds(MARGIN_AT[k], 15 - k)] = height[k, pl.ds(0, 15 - k)]
+    lane = lane_of()
+    for target, low in ((to_down, 1), (to_up, 0)):
+        for k in range(15):
+            rows = height[k, pl.ds(low * (k + 1), 15 - k)]
+            packed[pl.ds(MARGIN_AT[k] * FOLDS, (15 - k) * FOLDS), :] = rows.reshape((15 - k) * FOLDS, LANES)
+        for group in range(MARGIN // 8):
+            blocks = [packed[pl.ds(8 * group * FOLDS + s, 8, stride=FOLDS), :] for s in range(FOLDS)]
+            for a, tile in enumerate(unfold_rows(blocks, lane)):
+                target[pl.ds(8 * group, 8), pl.ds(LANES * a, LANES)] = tile
+
+
+def widen_kernel(edge, rows, out):
+    unused, core, tile = place()
+    lane = lane_of()
+    zero = jnp.zeros((8, LANES), jnp.float32)
+    for group in range(MARGIN // 8):
+        tiles = [rows[pl.ds(8 * group, 8), pl.ds(LANES * a, LANES)] for a in range(5)]
+
+        def store(s, block):
+            out[pl.ds(8 * group * FOLDS + s, 8, stride=FOLDS), :] = block
+
+        fold_rows([zero, *tiles, zero], lane, store)
+    inside = column_mask(core) & (tile != edge)
+    for r in range(MARGIN):
+        at = pl.ds(r * FOLDS, FOLDS)
+        out[at, :] = jnp.where(inside, out[at, :], OUTSIDE)
 
 
 def chain_kernel(turn, count_tiles, *refs):
-    if turn:
-        up, down, middle, height, height_up, height_down, unused, printed, top, even, odd = refs
-    else:
-        height, height_up, height_down, unused, printed, top, even, odd = refs
+    received, refs = (refs[:3], refs[3:]) if turn else ((), refs)
+    height, height_up, height_down, unused, printed, *top, even, odd = refs
     chip, core, tile = place()
 
     @pl.when(chip == turn)
     def run():
         inside = column_mask(core)
         lane = lane_of()
-        lift_up = jnp.where(tile > 0, 0.0, OUTSIDE)
-        lift_down = jnp.where(tile < count_tiles - 1, 0.0, OUTSIDE)
         if turn:
+            up, down, middle = received
             for r in range(ROWS):
                 even[r] = up[r] + TINY
                 even[ROWS + r] = middle[r] + TINY
@@ -186,11 +228,11 @@
                 total = total + pltpu.roll(total, 1, 1) + pltpu.roll(total, LANES - 1, 1)
                 support = jnp.log(total) * (0.5 / math.log(2.0)) - 0.5 * math.log2(9.0)
                 if j < ROWS:
-                    blue = height_up[MARGIN_AT[k] + j - 1 - k] + lift_up
+                    blue = height_up[MARGIN_AT[k] + j - 1 - k]
                 elif j < 2 * ROWS:
                     blue = height[k, j - ROWS]
                 else:
-                    blue = height_down[MARGIN_AT[k] + j - 2 * ROWS] + lift_down
+                    blue = height_down[MARGIN_AT[k] + j - 2 * ROWS]
                 gap = blue - support
                 square = gap * gap + level * level
                 value = (blue + support + level) - square * lax.rsqrt(square)
@@ -199,12 +241,12 @@
                     printed[k, j - ROWS] = value
                 if k < LAYERS - 1:
                     target[j] = weight
-                else:
+                elif top:
                     before = pltpu.roll(pltpu.roll(weight, 1, 0), LANES - STRIDE, 1)
                     after = pltpu.roll(pltpu.roll(weight, FOLDS - 1, 0), STRIDE, 1)
                     weight = jnp.where(lane < HALO, before, weight)
                     weight = jnp.where(lane >= HALO + STRIDE, after, weight)
-                    top[j - ROWS] = jnp.where(inside, weight, 0.0)
+                    top[0][j - ROWS] = jnp.where(inside, weight, 0.0)
 
 
 def unfold_kernel(scale, folded, own, partner):
@@ -216,16 +258,7 @@
             for group in range(2):
                 row = ((base + i) * ROWS + 8 * group) * FOLDS
                 blocks = [folded[pl.ds(row + s, 8, stride=FOLDS), :] * scale for s in range(FOLDS)]
-                tiles = []
-                for a in range(5):
-                    tile = None
-                    for s in range(FOLDS):
-                        low = max(LANES * a, STRIDE * s)
-                        if low >= min(LANES * a + LANES, STRIDE * s + STRIDE):
-                            continue
-                        piece = pltpu.roll(blocks[s], (STRIDE * s - LANES * a - HALO) % LANES, 1)
-                        tile = piece if tile is None else jnp.where(lane >= low - LANES * a, piece, tile)
-                    tiles.append(tile)
+                tiles = unfold_rows(blocks, lane)
                 for a in range(4):
                     target[i, pl.ds(8 * group, 8), pl.ds(LANES * a, LANES)] = jnp.where(core == 0, tiles[a], tiles[a + 1])
             return carry
@@ -274,9 +307,16 @@
     rim_left, rim_right = rim[:, :, :PART], rim[:, :, 1024 - PART :]
     crossing = [(i, j) for k in range(1, chips) for i, j in ((2 * k - 1, 2 * k), (2 * k, 2 * k - 1))]
     straight = [(i, j) for k in range(1, chips) for i, j in ((2 * k - 1, 2 * k + 1), (2 * k, 2 * k - 2))]
-    near = lax.ppermute(jnp.where(core == 0, rim_right, rim_left), "gz", crossing)
-    far = lax.ppermute(jnp.where(core == 0, rim_left, rim_right), "gz", straight)
-    partner = swap(jnp.where(core == 0, right, left))
+    near, far, partner = lax.optimization_barrier(
+        (
+            jnp.where(core == 0, rim_right, rim_left),
+            jnp.where(core == 0, rim_left, rim_right),
+            jnp.where(core == 0, right, left),
+        )
+    )
+    far = lax.ppermute(far, "gz", straight)
+    near = lax.ppermute(near, "gz", crossing)
+    partner = swap(partner)
     block = (FOLDS, LANES)
     folded, to_down, to_up = call(
         fold_kernel,
@@ -287,11 +327,17 @@
     height, to_down, to_up = call(
         functools.partial(filter_kernel, chips, tiles),
         "filter",
-        [(LAYERS, ROWS, *block), (MARGIN, *block), (MARGIN, *block)],
+        [(LAYERS, ROWS, *block), (MARGIN, 640), (MARGIN, 640)],
         [folded.reshape(22, ROWS, *block), from_up(to_down), from_down(to_up)],
-        scratch=[(22, ROWS + 2 * REACH, *block)] * 3,
+        scratch=[(22, ROWS + 2 * REACH, *block)] * 3 + [(MARGIN * FOLDS, LANES)],
     )
-    height_up, height_down = from_up(to_down), from_down(to_up)
+
+    def widen(rows, edge, name):
+        (out,) = call(functools.partial(widen_kernel, edge), name, [(MARGIN * FOLDS, LANES)], [rows])
+        return out.reshape(MARGIN, *block)
+
+    height_up = widen(from_up(to_down), 0, "widen_up")
+    height_down = widen(from_down(to_up), tiles - 1, "widen_down")
 
     def spread(folded, scale, name):
         own, other = call(
@@ -314,10 +360,10 @@
     received = []
     for turn in range(chips):
         operands = [*received, height, height_up, height_down, printed]
-        printed, top = call(
+        printed, *top = call(
             functools.partial(chain_kernel, turn, tiles),
             "chain",
-            [(LAYERS, ROWS, *block), (ROWS, *block)],
+            [(LAYERS, ROWS, *block), (ROWS, *block)][: 2 if turn < chips - 1 else 1],
             operands,
             scratch=[(48, *block)] * 2,
             aliases={len(operands) - 1: 0},
@@ -325,7 +371,7 @@
         if turn < chips - 1:
             received = [
                 lax.ppermute(
-                    top,
+                    top[0],
                     AXES,
                     [
                         (at(2 * turn + c, t), at(2 * turn + 2 + c, t + away))

time: 132 us -> 135 us (1.023)
  starting transfers between devices: 49.3 us -> 53.6 us
  waiting for transfers between devices: 71 us -> 68.2 us
    ppermute x3, starting transfers between devices: 10.6 us -> 14.8 us  [swap(): return lax.ppermute(block, 'gz', [(i, i ^ 1) for i in range(slabs)])]
    ppermute x2, waiting for transfers between devices: 9.29 us -> 5.36 us  [from_up(): return lax.ppermute(block, 'xy', [(i, i + 1) for i in range(tiles - 1)])]
    ppermute x23, waiting for transfers between devices: 58.5 us -> 60 us  [the longest x21 54.3 us: local(): lax.ppermute(top[0], AXES, [(at(2 * turn + c, t), at(2 * turn + 2 + c, t...]
    pallas_call x12 -> x14, Pallas kernels: 7.05 us -> 7.37 us  [call(): pl.pallas_call(kernel, name=name, out_shape=[pltpu.VMEM(shape, jnp.float3...]
  transfers between devices with their start and end apart: 30 -> 30, of which waited for: 9 -> 9; matrix products, arithmetic and copies ran while one was open for 1% -> 1% of each run, Pallas kernels for 0% -> 1%
where the time goes in v4:
time: 135 us; the launch traced here: 134 us
  waiting for transfers between devices  68.2 us (51%)
  starting transfers between devices  53.6 us (40%)
  Pallas kernels  7.37 us (5%)
  other arithmetic  3.99 us (3%)
    ppermute x21, waiting for transfers between devices, local(): lax.ppermute(top[0], AXES, [(at(2 * turn + c, t), at(2 * turn + 2 + c, t...  54.3 us
    ppermute x21, starting transfers between devices, local(): lax.ppermute(top[0], AXES, [(at(2 * turn + c, t), at(2 * turn + 2 + c, t...  15.8 us
    ppermute x2, starting transfers between devices, from_down(): return lax.ppermute(block, 'xy', [(i + 1, i) for i in range(tiles - 1)])  15.1 us
    ppermute x3, starting transfers between devices, swap(): return lax.ppermute(block, 'gz', [(i, i ^ 1) for i in range(slabs)])  14.8 us
    pallas_call x14, Pallas kernels, call(): pl.pallas_call(kernel, name=name, out_shape=[pltpu.VMEM(shape, jnp.float3...  7.37 us
    ppermute x2, starting transfers between devices, from_up(): return lax.ppermute(block, 'xy', [(i, i + 1) for i in range(tiles - 1)])  5.92 us
    ppermute x1, waiting for transfers between devices, local(): far = lax.ppermute(far, 'gz', straight)  5.72 us
    ppermute x2, waiting for transfers between devices, from_up(): return lax.ppermute(block, 'xy', [(i, i + 1) for i in range(tiles - 1)])  5.36 us
  transfers between devices with their start and end apart: 30, of which 9 were waited for; matrix products, arithmetic and copies ran while one was open for 1% of the time, Pallas kernels for 1%

profile of v4, /device:TPU:63, one launch (start us, length us, event | category | flops | bytes accessed | tf_op | source)
XLA Modules:
  0.0 134.4 jit_solution(1900732823565312757)
XLA Ops:
  0.6 1.1 slice_select_fusion.1
  1.8 1.2 slice_select_fusion
  3.0 2.6 %collective-permute-start = (f32[8,16,768]{2,1,0:T(8,128)S(1)}, f32[8,16,768]{2,1,0:T(8,128)S(1)}, u32[]{:S(2)}, u32[]{:S(2)}) collective-permute-start(f32[8,16,768]{2,1,0:T(8,128)S(1)} %slice_select_fusion), channel_id=1, source_target_pairs={{0,32},{32,0},{64,96},{96,64},{128,160},{160,128},{192,224},{224,1... | collective-permute-start | bytes 1179656 | tf_op jit(solution)/shard_map/ppermute | solution.py:297
  6.2 1.3 collective-permute-start.2
  7.5 5.7 %collective-permute-done.2.far = f32[3,16,768]{2,1,0:T(8,128)S(1)} collective-permute-done((f32[3,16,768]{2,1,0:T(8,128)S(1)}, f32[3,16,768]{2,1,0:T(8,128)S(1)}, u32[]{:S(2)}, u32[]{:S(2)}) %collective-permute-start.2) | collective-permute-done | bytes 147488 | tf_op jit(solution)/shard_map/ppermute | solution.py:317
  14.1 4.0 %collective-permute-start.3 = (f32[54,8,128]{2,1,0:T(8,128)S(1)}, f32[54,8,128]{2,1,0:T(8,128)S(1)}, u32[]{:S(2)}, u32[]{:S(2)}) collective-permute-start(f32[54,8,128]{2,1,0:T(8,128)S(1)} %get-tuple-element.40), channel_id=1, source_target_pairs={{0,1},{1,2},{2,3},{3,4},{4,5},{5,6},{6,7},{7,8},{8,9},{9,10},{10,1... | collective-permute-start | bytes 663560 | tf_op jit(solution)/shard_map/ppermute | solution.py:300
  18.1 8.9 %collective-permute-start.4 = (f32[54,8,128]{2,1,0:T(8,128)S(1)}, f32[54,8,128]{2,1,0:T(8,128)S(1)}, u32[]{:S(2)}, u32[]{:S(2)}) collective-permute-start(f32[54,8,128]{2,1,0:T(8,128)S(1)} %get-tuple-element.41), channel_id=1, source_target_pairs={{1,0},{2,1},{3,2},{4,3},{5,4},{6,5},{7,6},{8,7},{9,8},{10,9},{11,1... | collective-permute-start | bytes 663560 | tf_op jit(solution)/shard_map/ppermute | solution.py:303
  27.0 2.2 %collective-permute-done.3.up = f32[54,8,128]{2,1,0:T(8,128)S(1)} collective-permute-done((f32[54,8,128]{2,1,0:T(8,128)S(1)}, f32[54,8,128]{2,1,0:T(8,128)S(1)}, u32[]{:S(2)}, u32[]{:S(2)}) %collective-permute-start.3) | collective-permute-done | bytes 221216 | tf_op jit(solution)/shard_map/ppermute | solution.py:300
  29.2 0.9 collective-permute-done.4.down
  30.1 2.6 %filter.1 = (f32[16,16,8,128]{3,2,1,0:T(8,128)S(1)}, f32[120,640]{1,0:T(8,128)S(1)}, f32[120,640]{1,0:T(8,128)S(1)}) custom-call(f32[22,16,8,128]{3,2,1,0:T(8,128)S(1)} %bitcast.23, f32[54,8,128]{2,1,0:T(8,128)S(1)} %collective-permute-done.3.up, f32[54,8,128]{2,1,0:T(8,128)S(1)} %collective-permute-done.4.down), custom_call_target="tpu_custom_call" | custom-call | tf_op jit(solution)/shard_map/filter/pallas_call | solution.py:275
  32.7 1.9 %collective-permute-start.5 = (f32[120,640]{1,0:T(8,128)S(1)}, f32[120,640]{1,0:T(8,128)S(1)}, u32[]{:S(2)}, u32[]{:S(2)}) collective-permute-start(f32[120,640]{1,0:T(8,128)S(1)} %get-tuple-element.43), channel_id=1, source_target_pairs={{0,1},{1,2},{2,3},{3,4},{4,5},{5,6},{6,7},{7,8},{8,9},{9,10},{10,1... | collective-permute-start | bytes 921608 | tf_op jit(solution)/shard_map/ppermute | solution.py:300
  34.6 6.2 %collective-permute-start.7 = (f32[120,640]{1,0:T(8,128)S(1)}, f32[120,640]{1,0:T(8,128)S(1)}, u32[]{:S(2)}, u32[]{:S(2)}) collective-permute-start(f32[120,640]{1,0:T(8,128)S(1)} %get-tuple-element.49), channel_id=1, source_target_pairs={{1,0},{2,1},{3,2},{4,3},{5,4},{6,5},{7,6},{8,7},{9,8},{10,9},{11,1... | collective-permute-start | bytes 921608 | tf_op jit(solution)/shard_map/ppermute | solution.py:303
  40.8 3.1 %collective-permute-done.5.rows = f32[120,640]{1,0:T(8,128)S(1)} collective-permute-done((f32[120,640]{1,0:T(8,128)S(1)}, f32[120,640]{1,0:T(8,128)S(1)}, u32[]{:S(2)}, u32[]{:S(2)}) %collective-permute-start.5) | collective-permute-done | bytes 307232 | tf_op jit(solution)/shard_map/ppermute | solution.py:300
  44.7 5.1 %collective-permute-start.6 = (f32[8,16,512]{2,1,0:T(8,128)S(1)}, f32[8,16,512]{2,1,0:T(8,128)S(1)}, u32[]{:S(2)}, u32[]{:S(2)}) collective-permute-start(f32[8,16,512]{2,1,0:T(8,128)S(1)} %get-tuple-element.46), channel_id=1, source_target_pairs={{0,32},{32,0},{64,96},{96,64},{128,160},{160,128},{192,224},{224,1... | collective-permute-start | bytes 786440 | tf_op jit(solution)/shard_map/ppermute | solution.py:297
  53.0 0.8 maximum_select_fusion
  64.5 1.3 collective-permute-start.28
  65.8 1.3 collective-permute-start.27
  67.1 1.3 collective-permute-start.26
  68.4 48.6 %collective-permute-done.28.refs_2_ = f32[16,8,128]{2,1,0:T(8,128)S(1)} collective-permute-done((f32[16,8,128]{2,1,0:T(8,128)S(1)}, f32[16,8,128]{2,1,0:T(8,128)S(1)}, u32[]{:S(2)}, u32[]{:S(2)}) %collective-permute-start.28) | collective-permute-done | bytes 65568 | tf_op jit(solution)/shard_map/ppermute | solution.py:373
  116.9 2.8 %collective-permute-done.27.refs_1_ = f32[16,8,128]{2,1,0:T(8,128)S(1)} collective-permute-done((f32[16,8,128]{2,1,0:T(8,128)S(1)}, f32[16,8,128]{2,1,0:T(8,128)S(1)}, u32[]{:S(2)}, u32[]{:S(2)}) %collective-permute-start.27) | collective-permute-done | bytes 65568 | tf_op jit(solution)/shard_map/ppermute | solution.py:373
  119.7 2.9 %collective-permute-done.26.refs_0_ = f32[16,8,128]{2,1,0:T(8,128)S(1)} collective-permute-done((f32[16,8,128]{2,1,0:T(8,128)S(1)}, f32[16,8,128]{2,1,0:T(8,128)S(1)}, u32[]{:S(2)}, u32[]{:S(2)}) %collective-permute-start.26) | collective-permute-done | bytes 65568 | tf_op jit(solution)/shard_map/ppermute | solution.py:373
  122.6 2.3 %chain.15 = f32[16,16,8,128]{3,2,1,0:T(8,128)S(1)} custom-call(f32[16,8,128]{2,1,0:T(8,128)S(1)} %collective-permute-done.26.refs_0_, f32[16,8,128]{2,1,0:T(8,128)S(1)} %collective-permute-done.27.refs_1_, f32[16,8,128]{2,1,0:T(8,128)S(1)} %collective-permute-done.28.refs_2_, ...), custom_call_target="tpu_custom_call", output_to_operand_aliasing={{}: (6, {})} | custom-call | tf_op jit(solution)/shard_map/chain/pallas_call | solution.py:275
  125.3 7.2 %collective-permute-start.29 = (f32[8,16,512]{2,1,0:T(8,128)S(1)}, f32[8,16,512]{2,1,0:T(8,128)S(1)}, u32[]{:S(2)}, u32[]{:S(2)}) collective-permute-start(f32[8,16,512]{2,1,0:T(8,128)S(1)} %get-tuple-element.69), channel_id=1, source_target_pairs={{0,32},{32,0},{64,96},{96,64},{128,160},{160,128},{192,224},{224,1... | collective-permute-start | bytes 786440 | tf_op jit(solution)/shard_map/ppermute | solution.py:297
  132.4 1.1 collective-permute-done.29
  (58 shorter events, 17.0 us)
Async XLA Ops:
  3.0 10.3 %collective-permute-start = (f32[8,16,768]{2,1,0:T(8,128)S(1)}, f32[8,16,768]{2,1,0:T(8,128)S(1)}, u32[]{:S(2)}, u32[]{:S(2)}) collective-permute-start(f32[8,16,768]{2,1,0:T(8,128)S(1)} %slice_select_fusion), channel_id=1, source_target_pairs={{0,32},{32,0},{64,96},{96,64},{128,160},{160,128},{192,224},{224,1... | collective-permute-start | bytes 1179656 | tf_op jit(solution)/shard_map/ppermute | solution.py:297
  5.5 2.0 %collective-permute-start.1 = (f32[3,16,768]{2,1,0:T(8,128)S(1)}, f32[3,16,768]{2,1,0:T(8,128)S(1)}, u32[]{:S(2)}, u32[]{:S(2)}) collective-permute-start(f32[3,16,768]{2,1,0:T(8,128)S(1)} %get-tuple-element.37), channel_id=1, source_target_pairs={{32,64},{64,32},{96,128},{128,96},{160,192},{192,160},{224,256},{2... | collective-permute-start | bytes 442376 | tf_op jit(solution)/shard_map/ppermute | solution.py:318
  6.2 7.0 %collective-permute-start.2 = (f32[3,16,768]{2,1,0:T(8,128)S(1)}, f32[3,16,768]{2,1,0:T(8,128)S(1)}, u32[]{:S(2)}, u32[]{:S(2)}) collective-permute-start(f32[3,16,768]{2,1,0:T(8,128)S(1)} %get-tuple-element.38), channel_id=1, source_target_pairs={{32,96},{64,0},{96,160},{128,64},{160,224},{192,128},{224,288},{25... | collective-permute-start | bytes 442376 | tf_op jit(solution)/shard_map/ppermute | solution.py:317
  14.1 15.1 %collective-permute-start.3 = (f32[54,8,128]{2,1,0:T(8,128)S(1)}, f32[54,8,128]{2,1,0:T(8,128)S(1)}, u32[]{:S(2)}, u32[]{:S(2)}) collective-permute-start(f32[54,8,128]{2,1,0:T(8,128)S(1)} %get-tuple-element.40), channel_id=1, source_target_pairs={{0,1},{1,2},{2,3},{3,4},{4,5},{5,6},{6,7},{7,8},{8,9},{9,10},{10,1... | collective-permute-start | bytes 663560 | tf_op jit(solution)/shard_map/ppermute | solution.py:300
  18.1 12.0 %collective-permute-start.4 = (f32[54,8,128]{2,1,0:T(8,128)S(1)}, f32[54,8,128]{2,1,0:T(8,128)S(1)}, u32[]{:S(2)}, u32[]{:S(2)}) collective-permute-start(f32[54,8,128]{2,1,0:T(8,128)S(1)} %get-tuple-element.41), channel_id=1, source_target_pairs={{1,0},{2,1},{3,2},{4,3},{5,4},{6,5},{7,6},{8,7},{9,8},{10,9},{11,1... | collective-permute-start | bytes 663560 | tf_op jit(solution)/shard_map/ppermute | solution.py:303
  32.7 11.3 %collective-permute-start.5 = (f32[120,640]{1,0:T(8,128)S(1)}, f32[120,640]{1,0:T(8,128)S(1)}, u32[]{:S(2)}, u32[]{:S(2)}) collective-permute-start(f32[120,640]{1,0:T(8,128)S(1)} %get-tuple-element.43), channel_id=1, source_target_pairs={{0,1},{1,2},{2,3},{3,4},{4,5},{5,6},{6,7},{7,8},{8,9},{9,10},{10,1... | collective-permute-start | bytes 921608 | tf_op jit(solution)/shard_map/ppermute | solution.py:300
  34.6 15.1 %collective-permute-start.7 = (f32[120,640]{1,0:T(8,128)S(1)}, f32[120,640]{1,0:T(8,128)S(1)}, u32[]{:S(2)}, u32[]{:S(2)}) collective-permute-start(f32[120,640]{1,0:T(8,128)S(1)} %get-tuple-element.49), channel_id=1, source_target_pairs={{1,0},{2,1},{3,2},{4,3},{5,4},{6,5},{7,6},{8,7},{9,8},{10,9},{11,1... | collective-permute-start | bytes 921608 | tf_op jit(solution)/shard_map/ppermute | solution.py:303
  44.7 6.2 %collective-permute-start.6 = (f32[8,16,512]{2,1,0:T(8,128)S(1)}, f32[8,16,512]{2,1,0:T(8,128)S(1)}, u32[]{:S(2)}, u32[]{:S(2)}) collective-permute-start(f32[8,16,512]{2,1,0:T(8,128)S(1)} %get-tuple-element.46), channel_id=1, source_target_pairs={{0,32},{32,0},{64,96},{96,64},{128,160},{160,128},{192,224},{224,1... | collective-permute-start | bytes 786440 | tf_op jit(solution)/shard_map/ppermute | solution.py:297
  51.0 2.9 %collective-permute-start.10 = (f32[16,8,128]{2,1,0:T(8,128)S(1)}, f32[16,8,128]{2,1,0:T(8,128)S(1)}, u32[]{:S(2)}, u32[]{:S(2)}) collective-permute-start(f32[16,8,128]{2,1,0:T(8,128)S(1)} %get-tuple-element.54), channel_id=1, source_target_pairs={{0,64},{1,65},{2,66},{3,67},{4,68},{5,69},{6,70},{7,71},{8,72},{9,... | collective-permute-start | bytes 196616 | tf_op jit(solution)/shard_map/ppermute | solution.py:373
  51.7 2.2 %collective-permute-start.9 = (f32[16,8,128]{2,1,0:T(8,128)S(1)}, f32[16,8,128]{2,1,0:T(8,128)S(1)}, u32[]{:S(2)}, u32[]{:S(2)}) collective-permute-start(f32[16,8,128]{2,1,0:T(8,128)S(1)} %get-tuple-element.54), channel_id=1, source_target_pairs={{1,64},{2,65},{3,66},{4,67},{5,68},{6,69},{7,70},{8,71},{9,72},{10... | collective-permute-start | bytes 196616 | tf_op jit(solution)/shard_map/ppermute | solution.py:373
  52.3 1.5 %collective-permute-start.8 = (f32[16,8,128]{2,1,0:T(8,128)S(1)}, f32[16,8,128]{2,1,0:T(8,128)S(1)}, u32[]{:S(2)}, u32[]{:S(2)}) collective-permute-start(f32[16,8,128]{2,1,0:T(8,128)S(1)} %get-tuple-element.54), channel_id=1, source_target_pairs={{0,65},{1,66},{2,67},{3,68},{4,69},{5,70},{6,71},{7,72},{8,73},{9,... | collective-permute-start | bytes 196616 | tf_op jit(solution)/shard_map/ppermute | solution.py:373
  53.9 2.0 %collective-permute-start.13 = (f32[16,8,128]{2,1,0:T(8,128)S(1)}, f32[16,8,128]{2,1,0:T(8,128)S(1)}, u32[]{:S(2)}, u32[]{:S(2)}) collective-permute-start(f32[16,8,128]{2,1,0:T(8,128)S(1)} %get-tuple-element.56), channel_id=1, source_target_pairs={{64,128},{65,129},{66,130},{67,131},{68,132},{69,133},{70,134},{71... | collective-permute-start | bytes 196616 | tf_op jit(solution)/shard_map/ppermute | solution.py:373
  54.6 1.4 %collective-permute-start.12 = (f32[16,8,128]{2,1,0:T(8,128)S(1)}, f32[16,8,128]{2,1,0:T(8,128)S(1)}, u32[]{:S(2)}, u32[]{:S(2)}) collective-permute-start(f32[16,8,128]{2,1,0:T(8,128)S(1)} %get-tuple-element.56), channel_id=1, source_target_pairs={{65,128},{66,129},{67,130},{68,131},{69,132},{70,133},{71,134},{72... | collective-permute-start | bytes 196616 | tf_op jit(solution)/shard_map/ppermute | solution.py:373
  56.0 2.0 %collective-permute-start.16 = (f32[16,8,128]{2,1,0:T(8,128)S(1)}, f32[16,8,128]{2,1,0:T(8,128)S(1)}, u32[]{:S(2)}, u32[]{:S(2)}) collective-permute-start(f32[16,8,128]{2,1,0:T(8,128)S(1)} %get-tuple-element.58), channel_id=1, source_target_pairs={{128,192},{129,193},{130,194},{131,195},{132,196},{133,197},{134,1... | collective-permute-start | bytes 196616 | tf_op jit(solution)/shard_map/ppermute | solution.py:373
  56.6 1.4 %collective-permute-start.15 = (f32[16,8,128]{2,1,0:T(8,128)S(1)}, f32[16,8,128]{2,1,0:T(8,128)S(1)}, u32[]{:S(2)}, u32[]{:S(2)}) collective-permute-start(f32[16,8,128]{2,1,0:T(8,128)S(1)} %get-tuple-element.58), channel_id=1, source_target_pairs={{129,192},{130,193},{131,194},{132,195},{133,196},{134,197},{135,1... | collective-permute-start | bytes 196616 | tf_op jit(solution)/shard_map/ppermute | solution.py:373
  58.2 2.0 %collective-permute-start.19 = (f32[16,8,128]{2,1,0:T(8,128)S(1)}, f32[16,8,128]{2,1,0:T(8,128)S(1)}, u32[]{:S(2)}, u32[]{:S(2)}) collective-permute-start(f32[16,8,128]{2,1,0:T(8,128)S(1)} %get-tuple-element.60), channel_id=1, source_target_pairs={{192,256},{193,257},{194,258},{195,259},{196,260},{197,261},{198,2... | collective-permute-start | bytes 196616 | tf_op jit(solution)/shard_map/ppermute | solution.py:373
  58.9 1.4 %collective-permute-start.18 = (f32[16,8,128]{2,1,0:T(8,128)S(1)}, f32[16,8,128]{2,1,0:T(8,128)S(1)}, u32[]{:S(2)}, u32[]{:S(2)}) collective-permute-start(f32[16,8,128]{2,1,0:T(8,128)S(1)} %get-tuple-element.60), channel_id=1, source_target_pairs={{193,256},{194,257},{195,258},{196,259},{197,260},{198,261},{199,2... | collective-permute-start | bytes 196616 | tf_op jit(solution)/shard_map/ppermute | solution.py:373
  60.3 2.0 %collective-permute-start.22 = (f32[16,8,128]{2,1,0:T(8,128)S(1)}, f32[16,8,128]{2,1,0:T(8,128)S(1)}, u32[]{:S(2)}, u32[]{:S(2)}) collective-permute-start(f32[16,8,128]{2,1,0:T(8,128)S(1)} %get-tuple-element.62), channel_id=1, source_target_pairs={{256,320},{257,321},{258,322},{259,323},{260,324},{261,325},{262,3... | collective-permute-start | bytes 196616 | tf_op jit(solution)/shard_map/ppermute | solution.py:373
  61.0 1.4 %collective-permute-start.21 = (f32[16,8,128]{2,1,0:T(8,128)S(1)}, f32[16,8,128]{2,1,0:T(8,128)S(1)}, u32[]{:S(2)}, u32[]{:S(2)}) collective-permute-start(f32[16,8,128]{2,1,0:T(8,128)S(1)} %get-tuple-element.62), channel_id=1, source_target_pairs={{257,320},{258,321},{259,322},{260,323},{261,324},{262,325},{263,3... | collective-permute-start | bytes 196616 | tf_op jit(solution)/shard_map/ppermute | solution.py:373
  62.4 2.0 %collective-permute-start.25 = (f32[16,8,128]{2,1,0:T(8,128)S(1)}, f32[16,8,128]{2,1,0:T(8,128)S(1)}, u32[]{:S(2)}, u32[]{:S(2)}) collective-permute-start(f32[16,8,128]{2,1,0:T(8,128)S(1)} %get-tuple-element.64), channel_id=1, source_target_pairs={{320,384},{321,385},{322,386},{323,387},{324,388},{325,389},{326,3... | collective-permute-start | bytes 196616 | tf_op jit(solution)/shard_map/ppermute | solution.py:373
  64.5 52.5 %collective-permute-start.28 = (f32[16,8,128]{2,1,0:T(8,128)S(1)}, f32[16,8,128]{2,1,0:T(8,128)S(1)}, u32[]{:S(2)}, u32[]{:S(2)}) collective-permute-start(f32[16,8,128]{2,1,0:T(8,128)S(1)} %get-tuple-element.66), channel_id=1, source_target_pairs={{384,448},{385,449},{386,450},{387,451},{388,452},{389,453},{390,4... | collective-permute-start | bytes 196616 | tf_op jit(solution)/shard_map/ppermute | solution.py:373
  65.8 53.9 %collective-permute-start.27 = (f32[16,8,128]{2,1,0:T(8,128)S(1)}, f32[16,8,128]{2,1,0:T(8,128)S(1)}, u32[]{:S(2)}, u32[]{:S(2)}) collective-permute-start(f32[16,8,128]{2,1,0:T(8,128)S(1)} %get-tuple-element.66), channel_id=1, source_target_pairs={{385,448},{386,449},{387,450},{388,451},{389,452},{390,453},{391,4... | collective-permute-start | bytes 196616 | tf_op jit(solution)/shard_map/ppermute | solution.py:373
  67.1 55.5 %collective-permute-start.26 = (f32[16,8,128]{2,1,0:T(8,128)S(1)}, f32[16,8,128]{2,1,0:T(8,128)S(1)}, u32[]{:S(2)}, u32[]{:S(2)}) collective-permute-start(f32[16,8,128]{2,1,0:T(8,128)S(1)} %get-tuple-element.66), channel_id=1, source_target_pairs={{384,449},{385,450},{386,451},{387,452},{388,453},{389,454},{390,4... | collective-permute-start | bytes 196616 | tf_op jit(solution)/shard_map/ppermute | solution.py:373
  125.3 8.3 %collective-permute-start.29 = (f32[8,16,512]{2,1,0:T(8,128)S(1)}, f32[8,16,512]{2,1,0:T(8,128)S(1)}, u32[]{:S(2)}, u32[]{:S(2)}) collective-permute-start(f32[8,16,512]{2,1,0:T(8,128)S(1)} %get-tuple-element.69), channel_id=1, source_target_pairs={{0,32},{32,0},{64,96},{96,64},{128,160},{160,128},{192,224},{224,1... | collective-permute-start | bytes 786440 | tf_op jit(solution)/shard_map/ppermute | solution.py:297
  (7 other events, 17.5 us)

commit v5 on v4

--- a/solution.py
+++ b/solution.py
@@ -207,7 +207,7 @@
         inside = column_mask(core)
         lane = lane_of()
         if turn:
-            up, down, middle = received
+            middle, up, down = received
             for r in range(ROWS):
                 even[r] = up[r] + TINY
                 even[ROWS + r] = middle[r] + TINY
@@ -307,16 +307,9 @@
     rim_left, rim_right = rim[:, :, :PART], rim[:, :, 1024 - PART :]
     crossing = [(i, j) for k in range(1, chips) for i, j in ((2 * k - 1, 2 * k), (2 * k, 2 * k - 1))]
     straight = [(i, j) for k in range(1, chips) for i, j in ((2 * k - 1, 2 * k + 1), (2 * k, 2 * k - 2))]
-    near, far, partner = lax.optimization_barrier(
-        (
-            jnp.where(core == 0, rim_right, rim_left),
-            jnp.where(core == 0, rim_left, rim_right),
-            jnp.where(core == 0, right, left),
-        )
-    )
-    far = lax.ppermute(far, "gz", straight)
-    near = lax.ppermute(near, "gz", crossing)
-    partner = swap(partner)
+    partner = swap(jnp.where(core == 0, right, left))
+    near = lax.ppermute(jnp.where(core == 0, rim_right, rim_left), "gz", crossing)
+    far = lax.ppermute(jnp.where(core == 0, rim_left, rim_right), "gz", straight)
     block = (FOLDS, LANES)
     folded, to_down, to_up = call(
         fold_kernel,
@@ -380,7 +373,7 @@
                         if 0 <= t + away < tiles
                     ],
                 )
-                for away in (1, -1, 0)
+                for away in (0, 1, -1)
             ]
         if turn == 0:
             printed, blueprint = lax.optimization_barrier((printed, assemble(*shown)))

time: 135 us -> 130 us (0.963)
  waiting for transfers between devices: 68.2 us -> 65.2 us
    ppermute x2, waiting for transfers between devices: 5.73 us -> 3.91 us  [the longest x1 3.91 us: local(): lax.ppermute(jnp.where(core == 0, rim_left, rim_right), 'gz', straight)]
    ppermute x2, waiting for transfers between devices: 5.36 us -> 3.68 us  [from_up(): return lax.ppermute(block, 'xy', [(i, i + 1) for i in range(tiles - 1)])]
  transfers between devices with their start and end apart: 30 -> 30, of which waited for: 9 -> 8; matrix products, arithmetic and copies ran while one was open for 1% -> 1% of each run, Pallas kernels for 1% -> 1%
where the time goes in v5:
time: 130 us; the launch traced here: 129 us
  waiting for transfers between devices  65.2 us (50%)
  starting transfers between devices  52.4 us (40%)
  Pallas kernels  7.37 us (6%)
  other arithmetic  2.96 us (2%)
    ppermute x21, waiting for transfers between devices, local(): lax.ppermute(top[0], AXES, [(at(2 * turn + c, t), at(2 * turn + 2 + c, t...  54.2 us
    ppermute x21, starting transfers between devices, local(): lax.ppermute(top[0], AXES, [(at(2 * turn + c, t), at(2 * turn + 2 + c, t...  15.8 us
    ppermute x2, starting transfers between devices, from_down(): return lax.ppermute(block, 'xy', [(i + 1, i) for i in range(tiles - 1)])  14.8 us
    ppermute x3, starting transfers between devices, swap(): return lax.ppermute(block, 'gz', [(i, i ^ 1) for i in range(slabs)])  13.9 us
    pallas_call x14, Pallas kernels, call(): pl.pallas_call(kernel, name=name, out_shape=[pltpu.VMEM(shape, jnp.float3...  7.37 us
    ppermute x2, starting transfers between devices, from_up(): return lax.ppermute(block, 'xy', [(i, i + 1) for i in range(tiles - 1)])  5.92 us
    ppermute x1, waiting for transfers between devices, local(): lax.ppermute(jnp.where(core == 0, rim_left, rim_right), 'gz', straight)  3.91 us
    ppermute x2, waiting for transfers between devices, from_up(): return lax.ppermute(block, 'xy', [(i, i + 1) for i in range(tiles - 1)])  3.68 us
  transfers between devices with their start and end apart: 30, of which 8 were waited for; matrix products, arithmetic and copies ran while one was open for 1% of the time, Pallas kernels for 1%

profile of v5, /device:TPU:63, one launch (start us, length us, event | category | flops | bytes accessed | tf_op | source)
XLA Modules:
  0.0 129.1 jit_solution(3225213883635449080)
XLA Ops:
  0.6 1.2 slice_select_fusion
  1.9 2.6 %collective-permute-start = (f32[8,16,768]{2,1,0:T(8,128)S(1)}, f32[8,16,768]{2,1,0:T(8,128)S(1)}, u32[]{:S(2)}, u32[]{:S(2)}) collective-permute-start(f32[8,16,768]{2,1,0:T(8,128)S(1)} %slice_select_fusion), channel_id=1, source_target_pairs={{0,32},{32,0},{64,96},{96,64},{128,160},{160,128},{192,224},{224,1... | collective-permute-start | bytes 1179656 | tf_op jit(solution)/shard_map/ppermute | solution.py:297
  4.5 1.3 %collective-permute-start.2 = (f32[3,16,768]{2,1,0:T(8,128)S(1)}, f32[3,16,768]{2,1,0:T(8,128)S(1)}, u32[]{:S(2)}, u32[]{:S(2)}) collective-permute-start(f32[3,16,768]{2,1,0:T(8,128)S(1)} %get-tuple-element.64), channel_id=1, source_target_pairs={{32,96},{64,0},{96,160},{128,64},{160,224},{192,128},{224,288},{25... | collective-permute-start | bytes 442376 | tf_op jit(solution)/shard_map/ppermute | solution.py:312
  6.5 3.9 %collective-permute-done.2.far = f32[3,16,768]{2,1,0:T(8,128)S(1)} collective-permute-done((f32[3,16,768]{2,1,0:T(8,128)S(1)}, f32[3,16,768]{2,1,0:T(8,128)S(1)}, u32[]{:S(2)}, u32[]{:S(2)}) %collective-permute-start.2) | collective-permute-done | bytes 147488 | tf_op jit(solution)/shard_map/ppermute | solution.py:312
  10.4 0.8 fold.1
  11.2 4.0 %collective-permute-start.3 = (f32[54,8,128]{2,1,0:T(8,128)S(1)}, f32[54,8,128]{2,1,0:T(8,128)S(1)}, u32[]{:S(2)}, u32[]{:S(2)}) collective-permute-start(f32[54,8,128]{2,1,0:T(8,128)S(1)} %get-tuple-element.34), channel_id=1, source_target_pairs={{0,1},{1,2},{2,3},{3,4},{4,5},{5,6},{6,7},{7,8},{8,9},{9,10},{10,1... | collective-permute-start | bytes 663560 | tf_op jit(solution)/shard_map/ppermute | solution.py:300
  15.3 8.9 %collective-permute-start.4 = (f32[54,8,128]{2,1,0:T(8,128)S(1)}, f32[54,8,128]{2,1,0:T(8,128)S(1)}, u32[]{:S(2)}, u32[]{:S(2)}) collective-permute-start(f32[54,8,128]{2,1,0:T(8,128)S(1)} %get-tuple-element.35), channel_id=1, source_target_pairs={{1,0},{2,1},{3,2},{4,3},{5,4},{6,5},{7,6},{8,7},{9,8},{10,9},{11,1... | collective-permute-start | bytes 663560 | tf_op jit(solution)/shard_map/ppermute | solution.py:303
  24.1 1.4 %collective-permute-done.3.up = f32[54,8,128]{2,1,0:T(8,128)S(1)} collective-permute-done((f32[54,8,128]{2,1,0:T(8,128)S(1)}, f32[54,8,128]{2,1,0:T(8,128)S(1)}, u32[]{:S(2)}, u32[]{:S(2)}) %collective-permute-start.3) | collective-permute-done | bytes 221216 | tf_op jit(solution)/shard_map/ppermute | solution.py:300
  25.5 1.5 %collective-permute-done.4.down = f32[54,8,128]{2,1,0:T(8,128)S(1)} collective-permute-done((f32[54,8,128]{2,1,0:T(8,128)S(1)}, f32[54,8,128]{2,1,0:T(8,128)S(1)}, u32[]{:S(2)}, u32[]{:S(2)}) %collective-permute-start.4) | collective-permute-done | bytes 221216 | tf_op jit(solution)/shard_map/ppermute | solution.py:303
  27.0 2.6 %filter.1 = (f32[16,16,8,128]{3,2,1,0:T(8,128)S(1)}, f32[120,640]{1,0:T(8,128)S(1)}, f32[120,640]{1,0:T(8,128)S(1)}) custom-call(f32[22,16,8,128]{3,2,1,0:T(8,128)S(1)} %bitcast.23, f32[54,8,128]{2,1,0:T(8,128)S(1)} %collective-permute-done.3.up, f32[54,8,128]{2,1,0:T(8,128)S(1)} %collective-permute-done.4.down), custom_call_target="tpu_custom_call" | custom-call | tf_op jit(solution)/shard_map/filter/pallas_call | solution.py:275
  29.6 1.9 %collective-permute-start.5 = (f32[120,640]{1,0:T(8,128)S(1)}, f32[120,640]{1,0:T(8,128)S(1)}, u32[]{:S(2)}, u32[]{:S(2)}) collective-permute-start(f32[120,640]{1,0:T(8,128)S(1)} %get-tuple-element.37), channel_id=1, source_target_pairs={{0,1},{1,2},{2,3},{3,4},{4,5},{5,6},{6,7},{7,8},{8,9},{9,10},{10,1... | collective-permute-start | bytes 921608 | tf_op jit(solution)/shard_map/ppermute | solution.py:300
  31.5 5.9 %collective-permute-start.7 = (f32[120,640]{1,0:T(8,128)S(1)}, f32[120,640]{1,0:T(8,128)S(1)}, u32[]{:S(2)}, u32[]{:S(2)}) collective-permute-start(f32[120,640]{1,0:T(8,128)S(1)} %get-tuple-element.43), channel_id=1, source_target_pairs={{1,0},{2,1},{3,2},{4,3},{5,4},{6,5},{7,6},{8,7},{9,8},{10,9},{11,1... | collective-permute-start | bytes 921608 | tf_op jit(solution)/shard_map/ppermute | solution.py:303
  37.4 2.3 %collective-permute-done.5.rows = f32[120,640]{1,0:T(8,128)S(1)} collective-permute-done((f32[120,640]{1,0:T(8,128)S(1)}, f32[120,640]{1,0:T(8,128)S(1)}, u32[]{:S(2)}, u32[]{:S(2)}) %collective-permute-start.5) | collective-permute-done | bytes 307232 | tf_op jit(solution)/shard_map/ppermute | solution.py:300
  40.4 7.8 %collective-permute-start.6 = (f32[8,16,512]{2,1,0:T(8,128)S(1)}, f32[8,16,512]{2,1,0:T(8,128)S(1)}, u32[]{:S(2)}, u32[]{:S(2)}) collective-permute-start(f32[8,16,512]{2,1,0:T(8,128)S(1)} %get-tuple-element.40), channel_id=1, source_target_pairs={{0,32},{32,0},{64,96},{96,64},{128,160},{160,128},{192,224},{224,1... | collective-permute-start | bytes 786440 | tf_op jit(solution)/shard_map/ppermute | solution.py:297
  51.5 0.8 maximum_select_fusion
  63.0 1.3 %collective-permute-start.28 = (f32[16,8,128]{2,1,0:T(8,128)S(1)}, f32[16,8,128]{2,1,0:T(8,128)S(1)}, u32[]{:S(2)}, u32[]{:S(2)}) collective-permute-start(f32[16,8,128]{2,1,0:T(8,128)S(1)} %get-tuple-element.60), channel_id=1, source_target_pairs={{385,448},{386,449},{387,450},{388,451},{389,452},{390,453},{391,4... | collective-permute-start | bytes 196616 | tf_op jit(solution)/shard_map/ppermute | solution.py:366
  64.3 1.3 %collective-permute-start.27 = (f32[16,8,128]{2,1,0:T(8,128)S(1)}, f32[16,8,128]{2,1,0:T(8,128)S(1)}, u32[]{:S(2)}, u32[]{:S(2)}) collective-permute-start(f32[16,8,128]{2,1,0:T(8,128)S(1)} %get-tuple-element.60), channel_id=1, source_target_pairs={{384,449},{385,450},{386,451},{387,452},{388,453},{389,454},{390,4... | collective-permute-start | bytes 196616 | tf_op jit(solution)/shard_map/ppermute | solution.py:366
  65.6 1.3 %collective-permute-start.26 = (f32[16,8,128]{2,1,0:T(8,128)S(1)}, f32[16,8,128]{2,1,0:T(8,128)S(1)}, u32[]{:S(2)}, u32[]{:S(2)}) collective-permute-start(f32[16,8,128]{2,1,0:T(8,128)S(1)} %get-tuple-element.60), channel_id=1, source_target_pairs={{384,448},{385,449},{386,450},{387,451},{388,452},{389,453},{390,4... | collective-permute-start | bytes 196616 | tf_op jit(solution)/shard_map/ppermute | solution.py:366
  66.9 49.2 %collective-permute-done.28.refs_2_ = f32[16,8,128]{2,1,0:T(8,128)S(1)} collective-permute-done((f32[16,8,128]{2,1,0:T(8,128)S(1)}, f32[16,8,128]{2,1,0:T(8,128)S(1)}, u32[]{:S(2)}, u32[]{:S(2)}) %collective-permute-start.28) | collective-permute-done | bytes 65568 | tf_op jit(solution)/shard_map/ppermute | solution.py:366
  116.1 4.9 %collective-permute-done.27.refs_1_ = f32[16,8,128]{2,1,0:T(8,128)S(1)} collective-permute-done((f32[16,8,128]{2,1,0:T(8,128)S(1)}, f32[16,8,128]{2,1,0:T(8,128)S(1)}, u32[]{:S(2)}, u32[]{:S(2)}) %collective-permute-start.27) | collective-permute-done | bytes 65568 | tf_op jit(solution)/shard_map/ppermute | solution.py:366
  121.0 2.3 %chain.15 = f32[16,16,8,128]{3,2,1,0:T(8,128)S(1)} custom-call(f32[16,8,128]{2,1,0:T(8,128)S(1)} %collective-permute-done.26.refs_0_, f32[16,8,128]{2,1,0:T(8,128)S(1)} %collective-permute-done.27.refs_1_, f32[16,8,128]{2,1,0:T(8,128)S(1)} %collective-permute-done.28.refs_2_, ...), custom_call_target="tpu_custom_call", output_to_operand_aliasing={{}: (6, {})} | custom-call | tf_op jit(solution)/shard_map/chain/pallas_call | solution.py:275
  123.6 3.5 %collective-permute-start.29 = (f32[8,16,512]{2,1,0:T(8,128)S(1)}, f32[8,16,512]{2,1,0:T(8,128)S(1)}, u32[]{:S(2)}, u32[]{:S(2)}) collective-permute-start(f32[8,16,512]{2,1,0:T(8,128)S(1)} %get-tuple-element.63), channel_id=1, source_target_pairs={{0,32},{32,0},{64,96},{96,64},{128,160},{160,128},{192,224},{224,1... | collective-permute-start | bytes 786440 | tf_op jit(solution)/shard_map/ppermute | solution.py:297
  127.1 1.1 collective-permute-done.29
  128.3 0.8 maximum_select_fusion.1
  (58 shorter events, 15.3 us)
Async XLA Ops:
  1.9 8.6 %collective-permute-start = (f32[8,16,768]{2,1,0:T(8,128)S(1)}, f32[8,16,768]{2,1,0:T(8,128)S(1)}, u32[]{:S(2)}, u32[]{:S(2)}) collective-permute-start(f32[8,16,768]{2,1,0:T(8,128)S(1)} %slice_select_fusion), channel_id=1, source_target_pairs={{0,32},{32,0},{64,96},{96,64},{128,160},{160,128},{192,224},{224,1... | collective-permute-start | bytes 1179656 | tf_op jit(solution)/shard_map/ppermute | solution.py:297
  4.5 5.9 %collective-permute-start.2 = (f32[3,16,768]{2,1,0:T(8,128)S(1)}, f32[3,16,768]{2,1,0:T(8,128)S(1)}, u32[]{:S(2)}, u32[]{:S(2)}) collective-permute-start(f32[3,16,768]{2,1,0:T(8,128)S(1)} %get-tuple-element.64), channel_id=1, source_target_pairs={{32,96},{64,0},{96,160},{128,64},{160,224},{192,128},{224,288},{25... | collective-permute-start | bytes 442376 | tf_op jit(solution)/shard_map/ppermute | solution.py:312
  5.8 4.6 %collective-permute-start.1 = (f32[3,16,768]{2,1,0:T(8,128)S(1)}, f32[3,16,768]{2,1,0:T(8,128)S(1)}, u32[]{:S(2)}, u32[]{:S(2)}) collective-permute-start(f32[3,16,768]{2,1,0:T(8,128)S(1)} %get-tuple-element.65), channel_id=1, source_target_pairs={{32,64},{64,32},{96,128},{128,96},{160,192},{192,160},{224,256},{2... | collective-permute-start | bytes 442376 | tf_op jit(solution)/shard_map/ppermute | solution.py:311
  11.2 14.2 %collective-permute-start.3 = (f32[54,8,128]{2,1,0:T(8,128)S(1)}, f32[54,8,128]{2,1,0:T(8,128)S(1)}, u32[]{:S(2)}, u32[]{:S(2)}) collective-permute-start(f32[54,8,128]{2,1,0:T(8,128)S(1)} %get-tuple-element.34), channel_id=1, source_target_pairs={{0,1},{1,2},{2,3},{3,4},{4,5},{5,6},{6,7},{7,8},{8,9},{9,10},{10,1... | collective-permute-start | bytes 663560 | tf_op jit(solution)/shard_map/ppermute | solution.py:300
  15.3 11.7 %collective-permute-start.4 = (f32[54,8,128]{2,1,0:T(8,128)S(1)}, f32[54,8,128]{2,1,0:T(8,128)S(1)}, u32[]{:S(2)}, u32[]{:S(2)}) collective-permute-start(f32[54,8,128]{2,1,0:T(8,128)S(1)} %get-tuple-element.35), channel_id=1, source_target_pairs={{1,0},{2,1},{3,2},{4,3},{5,4},{6,5},{7,6},{8,7},{9,8},{10,9},{11,1... | collective-permute-start | bytes 663560 | tf_op jit(solution)/shard_map/ppermute | solution.py:303
  29.6 10.2 %collective-permute-start.5 = (f32[120,640]{1,0:T(8,128)S(1)}, f32[120,640]{1,0:T(8,128)S(1)}, u32[]{:S(2)}, u32[]{:S(2)}) collective-permute-start(f32[120,640]{1,0:T(8,128)S(1)} %get-tuple-element.37), channel_id=1, source_target_pairs={{0,1},{1,2},{2,3},{3,4},{4,5},{5,6},{6,7},{7,8},{8,9},{9,10},{10,1... | collective-permute-start | bytes 921608 | tf_op jit(solution)/shard_map/ppermute | solution.py:300
  31.5 16.7 %collective-permute-start.7 = (f32[120,640]{1,0:T(8,128)S(1)}, f32[120,640]{1,0:T(8,128)S(1)}, u32[]{:S(2)}, u32[]{:S(2)}) collective-permute-start(f32[120,640]{1,0:T(8,128)S(1)} %get-tuple-element.43), channel_id=1, source_target_pairs={{1,0},{2,1},{3,2},{4,3},{5,4},{6,5},{7,6},{8,7},{9,8},{10,9},{11,1... | collective-permute-start | bytes 921608 | tf_op jit(solution)/shard_map/ppermute | solution.py:303
  40.4 8.9 %collective-permute-start.6 = (f32[8,16,512]{2,1,0:T(8,128)S(1)}, f32[8,16,512]{2,1,0:T(8,128)S(1)}, u32[]{:S(2)}, u32[]{:S(2)}) collective-permute-start(f32[8,16,512]{2,1,0:T(8,128)S(1)} %get-tuple-element.40), channel_id=1, source_target_pairs={{0,32},{32,0},{64,96},{96,64},{128,160},{160,128},{192,224},{224,1... | collective-permute-start | bytes 786440 | tf_op jit(solution)/shard_map/ppermute | solution.py:297
  49.5 2.9 %collective-permute-start.10 = (f32[16,8,128]{2,1,0:T(8,128)S(1)}, f32[16,8,128]{2,1,0:T(8,128)S(1)}, u32[]{:S(2)}, u32[]{:S(2)}) collective-permute-start(f32[16,8,128]{2,1,0:T(8,128)S(1)} %get-tuple-element.48), channel_id=1, source_target_pairs={{1,64},{2,65},{3,66},{4,67},{5,68},{6,69},{7,70},{8,71},{9,72},{10... | collective-permute-start | bytes 196616 | tf_op jit(solution)/shard_map/ppermute | solution.py:366
  50.1 2.2 %collective-permute-start.9 = (f32[16,8,128]{2,1,0:T(8,128)S(1)}, f32[16,8,128]{2,1,0:T(8,128)S(1)}, u32[]{:S(2)}, u32[]{:S(2)}) collective-permute-start(f32[16,8,128]{2,1,0:T(8,128)S(1)} %get-tuple-element.48), channel_id=1, source_target_pairs={{0,65},{1,66},{2,67},{3,68},{4,69},{5,70},{6,71},{7,72},{8,73},{9,... | collective-permute-start | bytes 196616 | tf_op jit(solution)/shard_map/ppermute | solution.py:366
  50.8 1.5 %collective-permute-start.8 = (f32[16,8,128]{2,1,0:T(8,128)S(1)}, f32[16,8,128]{2,1,0:T(8,128)S(1)}, u32[]{:S(2)}, u32[]{:S(2)}) collective-permute-start(f32[16,8,128]{2,1,0:T(8,128)S(1)} %get-tuple-element.48), channel_id=1, source_target_pairs={{0,64},{1,65},{2,66},{3,67},{4,68},{5,69},{6,70},{7,71},{8,72},{9,... | collective-permute-start | bytes 196616 | tf_op jit(solution)/shard_map/ppermute | solution.py:366
  52.4 2.0 %collective-permute-start.13 = (f32[16,8,128]{2,1,0:T(8,128)S(1)}, f32[16,8,128]{2,1,0:T(8,128)S(1)}, u32[]{:S(2)}, u32[]{:S(2)}) collective-permute-start(f32[16,8,128]{2,1,0:T(8,128)S(1)} %get-tuple-element.50), channel_id=1, source_target_pairs={{65,128},{66,129},{67,130},{68,131},{69,132},{70,133},{71,134},{72... | collective-permute-start | bytes 196616 | tf_op jit(solution)/shard_map/ppermute | solution.py:366
  53.1 1.4 %collective-permute-start.12 = (f32[16,8,128]{2,1,0:T(8,128)S(1)}, f32[16,8,128]{2,1,0:T(8,128)S(1)}, u32[]{:S(2)}, u32[]{:S(2)}) collective-permute-start(f32[16,8,128]{2,1,0:T(8,128)S(1)} %get-tuple-element.50), channel_id=1, source_target_pairs={{64,129},{65,130},{66,131},{67,132},{68,133},{69,134},{70,135},{71... | collective-permute-start | bytes 196616 | tf_op jit(solution)/shard_map/ppermute | solution.py:366
  54.5 2.0 %collective-permute-start.16 = (f32[16,8,128]{2,1,0:T(8,128)S(1)}, f32[16,8,128]{2,1,0:T(8,128)S(1)}, u32[]{:S(2)}, u32[]{:S(2)}) collective-permute-start(f32[16,8,128]{2,1,0:T(8,128)S(1)} %get-tuple-element.52), channel_id=1, source_target_pairs={{129,192},{130,193},{131,194},{132,195},{133,196},{134,197},{135,1... | collective-permute-start | bytes 196616 | tf_op jit(solution)/shard_map/ppermute | solution.py:366
  55.1 1.4 %collective-permute-start.15 = (f32[16,8,128]{2,1,0:T(8,128)S(1)}, f32[16,8,128]{2,1,0:T(8,128)S(1)}, u32[]{:S(2)}, u32[]{:S(2)}) collective-permute-start(f32[16,8,128]{2,1,0:T(8,128)S(1)} %get-tuple-element.52), channel_id=1, source_target_pairs={{128,193},{129,194},{130,195},{131,196},{132,197},{133,198},{134,1... | collective-permute-start | bytes 196616 | tf_op jit(solution)/shard_map/ppermute | solution.py:366
  56.7 2.0 %collective-permute-start.19 = (f32[16,8,128]{2,1,0:T(8,128)S(1)}, f32[16,8,128]{2,1,0:T(8,128)S(1)}, u32[]{:S(2)}, u32[]{:S(2)}) collective-permute-start(f32[16,8,128]{2,1,0:T(8,128)S(1)} %get-tuple-element.54), channel_id=1, source_target_pairs={{193,256},{194,257},{195,258},{196,259},{197,260},{198,261},{199,2... | collective-permute-start | bytes 196616 | tf_op jit(solution)/shard_map/ppermute | solution.py:366
  57.4 1.4 %collective-permute-start.18 = (f32[16,8,128]{2,1,0:T(8,128)S(1)}, f32[16,8,128]{2,1,0:T(8,128)S(1)}, u32[]{:S(2)}, u32[]{:S(2)}) collective-permute-start(f32[16,8,128]{2,1,0:T(8,128)S(1)} %get-tuple-element.54), channel_id=1, source_target_pairs={{192,257},{193,258},{194,259},{195,260},{196,261},{197,262},{198,2... | collective-permute-start | bytes 196616 | tf_op jit(solution)/shard_map/ppermute | solution.py:366
  58.8 2.0 %collective-permute-start.22 = (f32[16,8,128]{2,1,0:T(8,128)S(1)}, f32[16,8,128]{2,1,0:T(8,128)S(1)}, u32[]{:S(2)}, u32[]{:S(2)}) collective-permute-start(f32[16,8,128]{2,1,0:T(8,128)S(1)} %get-tuple-element.56), channel_id=1, source_target_pairs={{257,320},{258,321},{259,322},{260,323},{261,324},{262,325},{263,3... | collective-permute-start | bytes 196616 | tf_op jit(solution)/shard_map/ppermute | solution.py:366
  59.5 1.4 %collective-permute-start.21 = (f32[16,8,128]{2,1,0:T(8,128)S(1)}, f32[16,8,128]{2,1,0:T(8,128)S(1)}, u32[]{:S(2)}, u32[]{:S(2)}) collective-permute-start(f32[16,8,128]{2,1,0:T(8,128)S(1)} %get-tuple-element.56), channel_id=1, source_target_pairs={{256,321},{257,322},{258,323},{259,324},{260,325},{261,326},{262,3... | collective-permute-start | bytes 196616 | tf_op jit(solution)/shard_map/ppermute | solution.py:366
  60.9 2.0 %collective-permute-start.25 = (f32[16,8,128]{2,1,0:T(8,128)S(1)}, f32[16,8,128]{2,1,0:T(8,128)S(1)}, u32[]{:S(2)}, u32[]{:S(2)}) collective-permute-start(f32[16,8,128]{2,1,0:T(8,128)S(1)} %get-tuple-element.58), channel_id=1, source_target_pairs={{321,384},{322,385},{323,386},{324,387},{325,388},{326,389},{327,3... | collective-permute-start | bytes 196616 | tf_op jit(solution)/shard_map/ppermute | solution.py:366
  63.0 53.1 %collective-permute-start.28 = (f32[16,8,128]{2,1,0:T(8,128)S(1)}, f32[16,8,128]{2,1,0:T(8,128)S(1)}, u32[]{:S(2)}, u32[]{:S(2)}) collective-permute-start(f32[16,8,128]{2,1,0:T(8,128)S(1)} %get-tuple-element.60), channel_id=1, source_target_pairs={{385,448},{386,449},{387,450},{388,451},{389,452},{390,453},{391,4... | collective-permute-start | bytes 196616 | tf_op jit(solution)/shard_map/ppermute | solution.py:366
  64.3 56.7 %collective-permute-start.27 = (f32[16,8,128]{2,1,0:T(8,128)S(1)}, f32[16,8,128]{2,1,0:T(8,128)S(1)}, u32[]{:S(2)}, u32[]{:S(2)}) collective-permute-start(f32[16,8,128]{2,1,0:T(8,128)S(1)} %get-tuple-element.60), channel_id=1, source_target_pairs={{384,449},{385,450},{386,451},{387,452},{388,453},{389,454},{390,4... | collective-permute-start | bytes 196616 | tf_op jit(solution)/shard_map/ppermute | solution.py:366
  65.6 55.4 %collective-permute-start.26 = (f32[16,8,128]{2,1,0:T(8,128)S(1)}, f32[16,8,128]{2,1,0:T(8,128)S(1)}, u32[]{:S(2)}, u32[]{:S(2)}) collective-permute-start(f32[16,8,128]{2,1,0:T(8,128)S(1)} %get-tuple-element.60), channel_id=1, source_target_pairs={{384,448},{385,449},{386,450},{387,451},{388,452},{389,453},{390,4... | collective-permute-start | bytes 196616 | tf_op jit(solution)/shard_map/ppermute | solution.py:366
  123.6 4.7 %collective-permute-start.29 = (f32[8,16,512]{2,1,0:T(8,128)S(1)}, f32[8,16,512]{2,1,0:T(8,128)S(1)}, u32[]{:S(2)}, u32[]{:S(2)}) collective-permute-start(f32[8,16,512]{2,1,0:T(8,128)S(1)} %get-tuple-element.63), channel_id=1, source_target_pairs={{0,32},{32,0},{64,96},{96,64},{128,160},{160,128},{192,224},{224,1... | collective-permute-start | bytes 786440 | tf_op jit(solution)/shard_map/ppermute | solution.py:297
  (7 other events, 8.7 us)

commit v6 on v5

--- a/solution.py
+++ b/solution.py
@@ -44,6 +44,23 @@
     fold = lax.broadcasted_iota(jnp.int32, (FOLDS, LANES), 0)
     column = 384 * core + STRIDE * fold + lane_of() - HALO
     return (column >= 0) & (column < 1024)
+
+
+def fetch_kernel(design, own, partner, near, far, done):
+    unused, core, unused = place()
+    here = pl.ds(pl.multiple_of(256 * core, LANES), PART)
+    there = pl.ds(pl.multiple_of(256 * (1 - core), LANES), PART)
+    rim = pl.ds((8 - REACH) * core, REACH)
+    copies = [
+        pltpu.make_async_copy(design.at[rim, :, here], far, done.at[0]),
+        pltpu.make_async_copy(design.at[rim, :, there], near, done.at[1]),
+        pltpu.make_async_copy(design.at[:, :, there], partner, done.at[2]),
+        pltpu.make_async_copy(design.at[:, :, here], own, done.at[3]),
+    ]
+    for copy in copies:
+        copy.start()
+    for copy in copies:
+        copy.wait()
 
 
 def fold_rows(tiles, lane, store):
@@ -75,12 +92,12 @@
     unused, core, unused = place()
     lane = lane_of()
 
-    def fold(source, start, base, count):
+    def fold(source, base, count):
         def layer(i, carry):
             for group in range(2):
                 tiles = []
                 for a in range(7):
-                    at = jnp.clip(a - 1 + core, 0, 5) * LANES + start
+                    at = jnp.clip(a - 1 + core, 0, 5) * LANES
                     tile = source[i, pl.ds(8 * group, 8), pl.ds(pl.multiple_of(at, LANES), LANES)]
                     if a == 0:
                         tile = jnp.where(core == 0, 0.0, tile)
@@ -97,10 +114,10 @@
 
         lax.fori_loop(0, count, layer, 0, unroll=count)
 
-    fold(own, 256 * core, REACH + 8 * core, 8)
-    fold(partner, 0, REACH + 8 * (1 - core), 8)
-    fold(near, 0, 19 * core, REACH)
-    fold(far, 0, 19 * (1 - core), REACH)
+    fold(own, REACH + 8 * core, 8)
+    fold(partner, REACH + 8 * (1 - core), 8)
+    fold(near, 19 * core, REACH)
+    fold(far, 19 * (1 - core), REACH)
     at = 0
     for away in range(REACH):
         for i in range(1 + away, 21 - away):
@@ -302,20 +319,27 @@
     def from_down(block):
         return lax.ppermute(block, "xy", [(i + 1, i) for i in range(tiles - 1)])
 
-    rim = jnp.where(core == 0, design[:REACH], design[8 - REACH :])
-    left, right = design[:, :, :PART], design[:, :, 1024 - PART :]
-    rim_left, rim_right = rim[:, :, :PART], rim[:, :, 1024 - PART :]
     crossing = [(i, j) for k in range(1, chips) for i, j in ((2 * k - 1, 2 * k), (2 * k, 2 * k - 1))]
     straight = [(i, j) for k in range(1, chips) for i, j in ((2 * k - 1, 2 * k + 1), (2 * k, 2 * k - 2))]
-    partner = swap(jnp.where(core == 0, right, left))
-    near = lax.ppermute(jnp.where(core == 0, rim_right, rim_left), "gz", crossing)
-    far = lax.ppermute(jnp.where(core == 0, rim_left, rim_right), "gz", straight)
+    vmem = pl.BlockSpec(memory_space=pltpu.VMEM)
+    whole, rim = (8, ROWS, PART), (REACH, ROWS, PART)
+    own, partner, near, far = pl.pallas_call(
+        fetch_kernel,
+        name="fetch",
+        out_shape=[pltpu.VMEM(shape, jnp.float32) for shape in (whole, whole, rim, rim)],
+        in_specs=[pl.BlockSpec(memory_space=pltpu.HBM)],
+        out_specs=[vmem] * 4,
+        scratch_shapes=[pltpu.SemaphoreType.DMA((4,))],
+    )(pltpu.with_memory_space_constraint(design, pltpu.HBM))
+    far = lax.ppermute(far, "gz", straight)
+    near = lax.ppermute(near, "gz", crossing)
+    partner = swap(partner)
     block = (FOLDS, LANES)
     folded, to_down, to_up = call(
         fold_kernel,
         "fold",
         [(22 * ROWS * FOLDS, LANES), (SIDE, *block), (SIDE, *block)],
-        [design, partner, near, far],
+        [own, partner, near, far],
     )
     height, to_down, to_up = call(
         functools.partial(filter_kernel, chips, tiles),
@@ -346,8 +370,7 @@
             core == 0, jnp.concatenate([own, other], axis=2), jnp.concatenate([other, own], axis=2)
         )
 
-    shown, height_up = lax.optimization_barrier((height, height_up))
-    shown = spread(shown, 1.0 / HALF, "blueprint")
+    shown = spread(height, 1.0 / HALF, "blueprint")
     height, shown = lax.optimization_barrier((height, shown))
     printed = jnp.zeros((LAYERS, ROWS, *block), jnp.float32)
     received = []

time: 130 us -> 127 us (0.977)
  waiting for transfers between devices: 65.2 us -> 61.2 us
  Pallas kernels: 7.37 us -> 8.84 us
    ppermute x21, waiting for transfers between devices: 54.2 us -> 50.1 us  [local(): lax.ppermute(top[0], AXES, [(at(2 * turn + c, t), at(2 * turn + 2 + c, t...]
    ppermute x2, waiting for transfers between devices: 3.91 us -> 5.73 us  [the longest x1 5.72 us: local(): far = lax.ppermute(far, 'gz', straight)]
    ppermute x2, waiting for transfers between devices: 3.68 us -> 2.21 us  [from_up(): return lax.ppermute(block, 'xy', [(i, i + 1) for i in range(tiles - 1)])]
    pallas_call x0 -> x1, Pallas kernels: none -> 1.32 us  [local(): pl.pallas_call(fetch_kernel, name='fetch', out_shape=[pltpu.VMEM(shape, j...]
where the time goes in v6:
time: 127 us; the launch traced here: 126 us
  waiting for transfers between devices  61.2 us (48%)
  starting transfers between devices  53.5 us (42%)
  Pallas kernels  8.84 us (7%)
  other arithmetic  1.69 us (1%)
    ppermute x21, waiting for transfers between devices, local(): lax.ppermute(top[0], AXES, [(at(2 * turn + c, t), at(2 * turn + 2 + c, t...  50.1 us
    ppermute x21, starting transfers between devices, local(): lax.ppermute(top[0], AXES, [(at(2 * turn + c, t), at(2 * turn + 2 + c, t...  15.8 us
    ppermute x2, starting transfers between devices, from_down(): return lax.ppermute(block, 'xy', [(i + 1, i) for i in range(tiles - 1)])  15.1 us
    ppermute x3, starting transfers between devices, swap(): return lax.ppermute(block, 'gz', [(i, i ^ 1) for i in range(slabs)])  14.7 us
    pallas_call x14, Pallas kernels, call(): pl.pallas_call(kernel, name=name, out_shape=[pltpu.VMEM(shape, jnp.float3...  7.52 us
    ppermute x2, starting transfers between devices, from_up(): return lax.ppermute(block, 'xy', [(i, i + 1) for i in range(tiles - 1)])  5.92 us
    ppermute x1, waiting for transfers between devices, local(): far = lax.ppermute(far, 'gz', straight)  5.72 us
  transfers between devices with their start and end apart: 30, of which 8 were waited for; matrix products, arithmetic and copies ran while one was open for 1% of the time, Pallas kernels for 1%

profile of v6, /device:TPU:63, one launch (start us, length us, event | category | flops | bytes accessed | tf_op | source)
XLA Modules:
  0.0 126.5 jit_solution(397701735499866298)
XLA Ops:
  0.6 1.3 %fetch.1 = (f32[8,16,768]{2,1,0:T(8,128)S(1)}, f32[8,16,768]{2,1,0:T(8,128)S(1)}, f32[3,16,768]{2,1,0:T(8,128)S(1)}, f32[3,16,768]{2,1,0:T(8,128)S(1)}) custom-call(f32[8,16,1024]{2,1,0:T(8,128)} %design.1), custom_call_target="tpu_custom_call" | custom-call | tf_op jit(solution)/shard_map/fetch/pallas_call | solution.py:326
  2.0 2.6 %collective-permute-start = (f32[8,16,768]{2,1,0:T(8,128)S(1)}, f32[8,16,768]{2,1,0:T(8,128)S(1)}, u32[]{:S(2)}, u32[]{:S(2)}) collective-permute-start(f32[8,16,768]{2,1,0:T(8,128)S(1)} %get-tuple-element.36), channel_id=1, source_target_pairs={{0,32},{32,0},{64,96},{96,64},{128,160},{160,128},{192,224},{224,1... | collective-permute-start | bytes 1179656 | tf_op jit(solution)/shard_map/ppermute | solution.py:314
  5.2 1.3 %collective-permute-start.2 = (f32[3,16,768]{2,1,0:T(8,128)S(1)}, f32[3,16,768]{2,1,0:T(8,128)S(1)}, u32[]{:S(2)}, u32[]{:S(2)}) collective-permute-start(f32[3,16,768]{2,1,0:T(8,128)S(1)} %get-tuple-element.38), channel_id=1, source_target_pairs={{32,96},{64,0},{96,160},{128,64},{160,224},{192,128},{224,288},{25... | collective-permute-start | bytes 442376 | tf_op jit(solution)/shard_map/ppermute | solution.py:334
  6.5 5.7 %collective-permute-done.2.far = f32[3,16,768]{2,1,0:T(8,128)S(1)} collective-permute-done((f32[3,16,768]{2,1,0:T(8,128)S(1)}, f32[3,16,768]{2,1,0:T(8,128)S(1)}, u32[]{:S(2)}, u32[]{:S(2)}) %collective-permute-start.2) | collective-permute-done | bytes 147488 | tf_op jit(solution)/shard_map/ppermute | solution.py:334
  13.1 4.0 %collective-permute-start.3 = (f32[54,8,128]{2,1,0:T(8,128)S(1)}, f32[54,8,128]{2,1,0:T(8,128)S(1)}, u32[]{:S(2)}, u32[]{:S(2)}) collective-permute-start(f32[54,8,128]{2,1,0:T(8,128)S(1)} %get-tuple-element.40), channel_id=1, source_target_pairs={{0,1},{1,2},{2,3},{3,4},{4,5},{5,6},{6,7},{7,8},{8,9},{9,10},{10,1... | collective-permute-start | bytes 663560 | tf_op jit(solution)/shard_map/ppermute | solution.py:317
  17.1 8.9 %collective-permute-start.4 = (f32[54,8,128]{2,1,0:T(8,128)S(1)}, f32[54,8,128]{2,1,0:T(8,128)S(1)}, u32[]{:S(2)}, u32[]{:S(2)}) collective-permute-start(f32[54,8,128]{2,1,0:T(8,128)S(1)} %get-tuple-element.41), channel_id=1, source_target_pairs={{1,0},{2,1},{3,2},{4,3},{5,4},{6,5},{7,6},{8,7},{9,8},{10,9},{11,1... | collective-permute-start | bytes 663560 | tf_op jit(solution)/shard_map/ppermute | solution.py:320
  25.9 2.2 %collective-permute-done.3.up = f32[54,8,128]{2,1,0:T(8,128)S(1)} collective-permute-done((f32[54,8,128]{2,1,0:T(8,128)S(1)}, f32[54,8,128]{2,1,0:T(8,128)S(1)}, u32[]{:S(2)}, u32[]{:S(2)}) %collective-permute-start.3) | collective-permute-done | bytes 221216 | tf_op jit(solution)/shard_map/ppermute | solution.py:317
  28.2 0.9 collective-permute-done.4.down
  29.1 2.8 %filter.1 = (f32[16,16,8,128]{3,2,1,0:T(8,128)S(1)}, f32[120,640]{1,0:T(8,128)S(1)}, f32[120,640]{1,0:T(8,128)S(1)}) custom-call(f32[22,16,8,128]{3,2,1,0:T(8,128)S(1)} %bitcast.23, f32[54,8,128]{2,1,0:T(8,128)S(1)} %collective-permute-done.3.up, f32[54,8,128]{2,1,0:T(8,128)S(1)} %collective-permute-done.4.down), custom_call_target="tpu_custom_call" | custom-call | tf_op jit(solution)/shard_map/filter/pallas_call | solution.py:292
  31.8 1.9 %collective-permute-start.6 = (f32[120,640]{1,0:T(8,128)S(1)}, f32[120,640]{1,0:T(8,128)S(1)}, u32[]{:S(2)}, u32[]{:S(2)}) collective-permute-start(f32[120,640]{1,0:T(8,128)S(1)} %get-tuple-element.46), channel_id=1, source_target_pairs={{0,1},{1,2},{2,3},{3,4},{4,5},{5,6},{6,7},{7,8},{8,9},{9,10},{10,1... | collective-permute-start | bytes 921608 | tf_op jit(solution)/shard_map/ppermute | solution.py:317
  33.8 6.2 %collective-permute-start.7 = (f32[120,640]{1,0:T(8,128)S(1)}, f32[120,640]{1,0:T(8,128)S(1)}, u32[]{:S(2)}, u32[]{:S(2)}) collective-permute-start(f32[120,640]{1,0:T(8,128)S(1)} %get-tuple-element.47), channel_id=1, source_target_pairs={{1,0},{2,1},{3,2},{4,3},{5,4},{6,5},{7,6},{8,7},{9,8},{10,9},{11,1... | collective-permute-start | bytes 921608 | tf_op jit(solution)/shard_map/ppermute | solution.py:320
  40.3 4.7 %collective-permute-start.5 = (f32[8,16,512]{2,1,0:T(8,128)S(1)}, f32[8,16,512]{2,1,0:T(8,128)S(1)}, u32[]{:S(2)}, u32[]{:S(2)}) collective-permute-start(f32[8,16,512]{2,1,0:T(8,128)S(1)} %get-tuple-element.44), channel_id=1, source_target_pairs={{0,32},{32,0},{64,96},{96,64},{128,160},{160,128},{192,224},{224,1... | collective-permute-start | bytes 786440 | tf_op jit(solution)/shard_map/ppermute | solution.py:314
  45.1 1.1 collective-permute-done.5
  49.0 0.8 maximum_select_fusion
  60.4 1.3 %collective-permute-start.28 = (f32[16,8,128]{2,1,0:T(8,128)S(1)}, f32[16,8,128]{2,1,0:T(8,128)S(1)}, u32[]{:S(2)}, u32[]{:S(2)}) collective-permute-start(f32[16,8,128]{2,1,0:T(8,128)S(1)} %get-tuple-element.64), channel_id=1, source_target_pairs={{385,448},{386,449},{387,450},{388,451},{389,452},{390,453},{391,4... | collective-permute-start | bytes 196616 | tf_op jit(solution)/shard_map/ppermute | solution.py:389
  61.7 1.3 %collective-permute-start.27 = (f32[16,8,128]{2,1,0:T(8,128)S(1)}, f32[16,8,128]{2,1,0:T(8,128)S(1)}, u32[]{:S(2)}, u32[]{:S(2)}) collective-permute-start(f32[16,8,128]{2,1,0:T(8,128)S(1)} %get-tuple-element.64), channel_id=1, source_target_pairs={{384,449},{385,450},{386,451},{387,452},{388,453},{389,454},{390,4... | collective-permute-start | bytes 196616 | tf_op jit(solution)/shard_map/ppermute | solution.py:389
  63.0 1.3 %collective-permute-start.26 = (f32[16,8,128]{2,1,0:T(8,128)S(1)}, f32[16,8,128]{2,1,0:T(8,128)S(1)}, u32[]{:S(2)}, u32[]{:S(2)}) collective-permute-start(f32[16,8,128]{2,1,0:T(8,128)S(1)} %get-tuple-element.64), channel_id=1, source_target_pairs={{384,448},{385,449},{386,450},{387,451},{388,452},{389,453},{390,4... | collective-permute-start | bytes 196616 | tf_op jit(solution)/shard_map/ppermute | solution.py:389
  64.3 47.0 %collective-permute-done.28.refs_2_ = f32[16,8,128]{2,1,0:T(8,128)S(1)} collective-permute-done((f32[16,8,128]{2,1,0:T(8,128)S(1)}, f32[16,8,128]{2,1,0:T(8,128)S(1)}, u32[]{:S(2)}, u32[]{:S(2)}) %collective-permute-start.28) | collective-permute-done | bytes 65568 | tf_op jit(solution)/shard_map/ppermute | solution.py:389
  111.4 2.1 %collective-permute-done.27.refs_1_ = f32[16,8,128]{2,1,0:T(8,128)S(1)} collective-permute-done((f32[16,8,128]{2,1,0:T(8,128)S(1)}, f32[16,8,128]{2,1,0:T(8,128)S(1)}, u32[]{:S(2)}, u32[]{:S(2)}) %collective-permute-start.27) | collective-permute-done | bytes 65568 | tf_op jit(solution)/shard_map/ppermute | solution.py:389
  113.5 0.9 collective-permute-done.26.refs_0_
  114.4 2.3 %chain.15 = f32[16,16,8,128]{3,2,1,0:T(8,128)S(1)} custom-call(f32[16,8,128]{2,1,0:T(8,128)S(1)} %collective-permute-done.26.refs_0_, f32[16,8,128]{2,1,0:T(8,128)S(1)} %collective-permute-done.27.refs_1_, f32[16,8,128]{2,1,0:T(8,128)S(1)} %collective-permute-done.28.refs_2_, ...), custom_call_target="tpu_custom_call", output_to_operand_aliasing={{}: (6, {})} | custom-call | tf_op jit(solution)/shard_map/chain/pallas_call | solution.py:292
  117.0 7.4 %collective-permute-start.29 = (f32[8,16,512]{2,1,0:T(8,128)S(1)}, f32[8,16,512]{2,1,0:T(8,128)S(1)}, u32[]{:S(2)}, u32[]{:S(2)}) collective-permute-start(f32[8,16,512]{2,1,0:T(8,128)S(1)} %get-tuple-element.67), channel_id=1, source_target_pairs={{0,32},{32,0},{64,96},{96,64},{128,160},{160,128},{192,224},{224,1... | collective-permute-start | bytes 786440 | tf_op jit(solution)/shard_map/ppermute | solution.py:314
  124.5 1.1 collective-permute-done.29
  125.6 0.8 maximum_select_fusion.1
  (54 shorter events, 15.3 us)
Async XLA Ops:
  2.0 10.3 %collective-permute-start = (f32[8,16,768]{2,1,0:T(8,128)S(1)}, f32[8,16,768]{2,1,0:T(8,128)S(1)}, u32[]{:S(2)}, u32[]{:S(2)}) collective-permute-start(f32[8,16,768]{2,1,0:T(8,128)S(1)} %get-tuple-element.36), channel_id=1, source_target_pairs={{0,32},{32,0},{64,96},{96,64},{128,160},{160,128},{192,224},{224,1... | collective-permute-start | bytes 1179656 | tf_op jit(solution)/shard_map/ppermute | solution.py:314
  4.5 2.0 %collective-permute-start.1 = (f32[3,16,768]{2,1,0:T(8,128)S(1)}, f32[3,16,768]{2,1,0:T(8,128)S(1)}, u32[]{:S(2)}, u32[]{:S(2)}) collective-permute-start(f32[3,16,768]{2,1,0:T(8,128)S(1)} %get-tuple-element.37), channel_id=1, source_target_pairs={{32,64},{64,32},{96,128},{128,96},{160,192},{192,160},{224,256},{2... | collective-permute-start | bytes 442376 | tf_op jit(solution)/shard_map/ppermute | solution.py:335
  5.2 7.0 %collective-permute-start.2 = (f32[3,16,768]{2,1,0:T(8,128)S(1)}, f32[3,16,768]{2,1,0:T(8,128)S(1)}, u32[]{:S(2)}, u32[]{:S(2)}) collective-permute-start(f32[3,16,768]{2,1,0:T(8,128)S(1)} %get-tuple-element.38), channel_id=1, source_target_pairs={{32,96},{64,0},{96,160},{128,64},{160,224},{192,128},{224,288},{25... | collective-permute-start | bytes 442376 | tf_op jit(solution)/shard_map/ppermute | solution.py:334
  13.1 15.1 %collective-permute-start.3 = (f32[54,8,128]{2,1,0:T(8,128)S(1)}, f32[54,8,128]{2,1,0:T(8,128)S(1)}, u32[]{:S(2)}, u32[]{:S(2)}) collective-permute-start(f32[54,8,128]{2,1,0:T(8,128)S(1)} %get-tuple-element.40), channel_id=1, source_target_pairs={{0,1},{1,2},{2,3},{3,4},{4,5},{5,6},{6,7},{7,8},{8,9},{9,10},{10,1... | collective-permute-start | bytes 663560 | tf_op jit(solution)/shard_map/ppermute | solution.py:317
  17.1 12.0 %collective-permute-start.4 = (f32[54,8,128]{2,1,0:T(8,128)S(1)}, f32[54,8,128]{2,1,0:T(8,128)S(1)}, u32[]{:S(2)}, u32[]{:S(2)}) collective-permute-start(f32[54,8,128]{2,1,0:T(8,128)S(1)} %get-tuple-element.41), channel_id=1, source_target_pairs={{1,0},{2,1},{3,2},{4,3},{5,4},{6,5},{7,6},{8,7},{9,8},{10,9},{11,1... | collective-permute-start | bytes 663560 | tf_op jit(solution)/shard_map/ppermute | solution.py:320
  31.8 14.4 %collective-permute-start.6 = (f32[120,640]{1,0:T(8,128)S(1)}, f32[120,640]{1,0:T(8,128)S(1)}, u32[]{:S(2)}, u32[]{:S(2)}) collective-permute-start(f32[120,640]{1,0:T(8,128)S(1)} %get-tuple-element.46), channel_id=1, source_target_pairs={{0,1},{1,2},{2,3},{3,4},{4,5},{5,6},{6,7},{7,8},{8,9},{9,10},{10,1... | collective-permute-start | bytes 921608 | tf_op jit(solution)/shard_map/ppermute | solution.py:317
  33.8 12.8 %collective-permute-start.7 = (f32[120,640]{1,0:T(8,128)S(1)}, f32[120,640]{1,0:T(8,128)S(1)}, u32[]{:S(2)}, u32[]{:S(2)}) collective-permute-start(f32[120,640]{1,0:T(8,128)S(1)} %get-tuple-element.47), channel_id=1, source_target_pairs={{1,0},{2,1},{3,2},{4,3},{5,4},{6,5},{7,6},{8,7},{9,8},{10,9},{11,1... | collective-permute-start | bytes 921608 | tf_op jit(solution)/shard_map/ppermute | solution.py:320
  40.3 5.8 %collective-permute-start.5 = (f32[8,16,512]{2,1,0:T(8,128)S(1)}, f32[8,16,512]{2,1,0:T(8,128)S(1)}, u32[]{:S(2)}, u32[]{:S(2)}) collective-permute-start(f32[8,16,512]{2,1,0:T(8,128)S(1)} %get-tuple-element.44), channel_id=1, source_target_pairs={{0,32},{32,0},{64,96},{96,64},{128,160},{160,128},{192,224},{224,1... | collective-permute-start | bytes 786440 | tf_op jit(solution)/shard_map/ppermute | solution.py:314
  47.0 2.9 %collective-permute-start.10 = (f32[16,8,128]{2,1,0:T(8,128)S(1)}, f32[16,8,128]{2,1,0:T(8,128)S(1)}, u32[]{:S(2)}, u32[]{:S(2)}) collective-permute-start(f32[16,8,128]{2,1,0:T(8,128)S(1)} %get-tuple-element.52), channel_id=1, source_target_pairs={{1,64},{2,65},{3,66},{4,67},{5,68},{6,69},{7,70},{8,71},{9,72},{10... | collective-permute-start | bytes 196616 | tf_op jit(solution)/shard_map/ppermute | solution.py:389
  47.6 2.2 %collective-permute-start.9 = (f32[16,8,128]{2,1,0:T(8,128)S(1)}, f32[16,8,128]{2,1,0:T(8,128)S(1)}, u32[]{:S(2)}, u32[]{:S(2)}) collective-permute-start(f32[16,8,128]{2,1,0:T(8,128)S(1)} %get-tuple-element.52), channel_id=1, source_target_pairs={{0,65},{1,66},{2,67},{3,68},{4,69},{5,70},{6,71},{7,72},{8,73},{9,... | collective-permute-start | bytes 196616 | tf_op jit(solution)/shard_map/ppermute | solution.py:389
  48.3 1.5 %collective-permute-start.8 = (f32[16,8,128]{2,1,0:T(8,128)S(1)}, f32[16,8,128]{2,1,0:T(8,128)S(1)}, u32[]{:S(2)}, u32[]{:S(2)}) collective-permute-start(f32[16,8,128]{2,1,0:T(8,128)S(1)} %get-tuple-element.52), channel_id=1, source_target_pairs={{0,64},{1,65},{2,66},{3,67},{4,68},{5,69},{6,70},{7,71},{8,72},{9,... | collective-permute-start | bytes 196616 | tf_op jit(solution)/shard_map/ppermute | solution.py:389
  49.9 2.0 %collective-permute-start.13 = (f32[16,8,128]{2,1,0:T(8,128)S(1)}, f32[16,8,128]{2,1,0:T(8,128)S(1)}, u32[]{:S(2)}, u32[]{:S(2)}) collective-permute-start(f32[16,8,128]{2,1,0:T(8,128)S(1)} %get-tuple-element.54), channel_id=1, source_target_pairs={{65,128},{66,129},{67,130},{68,131},{69,132},{70,133},{71,134},{72... | collective-permute-start | bytes 196616 | tf_op jit(solution)/shard_map/ppermute | solution.py:389
  50.5 1.4 %collective-permute-start.12 = (f32[16,8,128]{2,1,0:T(8,128)S(1)}, f32[16,8,128]{2,1,0:T(8,128)S(1)}, u32[]{:S(2)}, u32[]{:S(2)}) collective-permute-start(f32[16,8,128]{2,1,0:T(8,128)S(1)} %get-tuple-element.54), channel_id=1, source_target_pairs={{64,129},{65,130},{66,131},{67,132},{68,133},{69,134},{70,135},{71... | collective-permute-start | bytes 196616 | tf_op jit(solution)/shard_map/ppermute | solution.py:389
  52.0 2.0 %collective-permute-start.16 = (f32[16,8,128]{2,1,0:T(8,128)S(1)}, f32[16,8,128]{2,1,0:T(8,128)S(1)}, u32[]{:S(2)}, u32[]{:S(2)}) collective-permute-start(f32[16,8,128]{2,1,0:T(8,128)S(1)} %get-tuple-element.56), channel_id=1, source_target_pairs={{129,192},{130,193},{131,194},{132,195},{133,196},{134,197},{135,1... | collective-permute-start | bytes 196616 | tf_op jit(solution)/shard_map/ppermute | solution.py:389
  52.6 1.4 %collective-permute-start.15 = (f32[16,8,128]{2,1,0:T(8,128)S(1)}, f32[16,8,128]{2,1,0:T(8,128)S(1)}, u32[]{:S(2)}, u32[]{:S(2)}) collective-permute-start(f32[16,8,128]{2,1,0:T(8,128)S(1)} %get-tuple-element.56), channel_id=1, source_target_pairs={{128,193},{129,194},{130,195},{131,196},{132,197},{133,198},{134,1... | collective-permute-start | bytes 196616 | tf_op jit(solution)/shard_map/ppermute | solution.py:389
  54.2 2.0 %collective-permute-start.19 = (f32[16,8,128]{2,1,0:T(8,128)S(1)}, f32[16,8,128]{2,1,0:T(8,128)S(1)}, u32[]{:S(2)}, u32[]{:S(2)}) collective-permute-start(f32[16,8,128]{2,1,0:T(8,128)S(1)} %get-tuple-element.58), channel_id=1, source_target_pairs={{193,256},{194,257},{195,258},{196,259},{197,260},{198,261},{199,2... | collective-permute-start | bytes 196616 | tf_op jit(solution)/shard_map/ppermute | solution.py:389
  54.9 1.4 %collective-permute-start.18 = (f32[16,8,128]{2,1,0:T(8,128)S(1)}, f32[16,8,128]{2,1,0:T(8,128)S(1)}, u32[]{:S(2)}, u32[]{:S(2)}) collective-permute-start(f32[16,8,128]{2,1,0:T(8,128)S(1)} %get-tuple-element.58), channel_id=1, source_target_pairs={{192,257},{193,258},{194,259},{195,260},{196,261},{197,262},{198,2... | collective-permute-start | bytes 196616 | tf_op jit(solution)/shard_map/ppermute | solution.py:389
  56.3 2.0 %collective-permute-start.22 = (f32[16,8,128]{2,1,0:T(8,128)S(1)}, f32[16,8,128]{2,1,0:T(8,128)S(1)}, u32[]{:S(2)}, u32[]{:S(2)}) collective-permute-start(f32[16,8,128]{2,1,0:T(8,128)S(1)} %get-tuple-element.60), channel_id=1, source_target_pairs={{257,320},{258,321},{259,322},{260,323},{261,324},{262,325},{263,3... | collective-permute-start | bytes 196616 | tf_op jit(solution)/shard_map/ppermute | solution.py:389
  58.4 2.0 %collective-permute-start.25 = (f32[16,8,128]{2,1,0:T(8,128)S(1)}, f32[16,8,128]{2,1,0:T(8,128)S(1)}, u32[]{:S(2)}, u32[]{:S(2)}) collective-permute-start(f32[16,8,128]{2,1,0:T(8,128)S(1)} %get-tuple-element.62), channel_id=1, source_target_pairs={{321,384},{322,385},{323,386},{324,387},{325,388},{326,389},{327,3... | collective-permute-start | bytes 196616 | tf_op jit(solution)/shard_map/ppermute | solution.py:389
  59.0 1.4 %collective-permute-start.24 = (f32[16,8,128]{2,1,0:T(8,128)S(1)}, f32[16,8,128]{2,1,0:T(8,128)S(1)}, u32[]{:S(2)}, u32[]{:S(2)}) collective-permute-start(f32[16,8,128]{2,1,0:T(8,128)S(1)} %get-tuple-element.62), channel_id=1, source_target_pairs={{320,385},{321,386},{322,387},{323,388},{324,389},{325,390},{326,3... | collective-permute-start | bytes 196616 | tf_op jit(solution)/shard_map/ppermute | solution.py:389
  60.4 50.9 %collective-permute-start.28 = (f32[16,8,128]{2,1,0:T(8,128)S(1)}, f32[16,8,128]{2,1,0:T(8,128)S(1)}, u32[]{:S(2)}, u32[]{:S(2)}) collective-permute-start(f32[16,8,128]{2,1,0:T(8,128)S(1)} %get-tuple-element.64), channel_id=1, source_target_pairs={{385,448},{386,449},{387,450},{388,451},{389,452},{390,453},{391,4... | collective-permute-start | bytes 196616 | tf_op jit(solution)/shard_map/ppermute | solution.py:389
  61.7 51.7 %collective-permute-start.27 = (f32[16,8,128]{2,1,0:T(8,128)S(1)}, f32[16,8,128]{2,1,0:T(8,128)S(1)}, u32[]{:S(2)}, u32[]{:S(2)}) collective-permute-start(f32[16,8,128]{2,1,0:T(8,128)S(1)} %get-tuple-element.64), channel_id=1, source_target_pairs={{384,449},{385,450},{386,451},{387,452},{388,453},{389,454},{390,4... | collective-permute-start | bytes 196616 | tf_op jit(solution)/shard_map/ppermute | solution.py:389
  63.0 51.3 %collective-permute-start.26 = (f32[16,8,128]{2,1,0:T(8,128)S(1)}, f32[16,8,128]{2,1,0:T(8,128)S(1)}, u32[]{:S(2)}, u32[]{:S(2)}) collective-permute-start(f32[16,8,128]{2,1,0:T(8,128)S(1)} %get-tuple-element.64), channel_id=1, source_target_pairs={{384,448},{385,449},{386,450},{387,451},{388,452},{389,453},{390,4... | collective-permute-start | bytes 196616 | tf_op jit(solution)/shard_map/ppermute | solution.py:389
  117.0 8.6 %collective-permute-start.29 = (f32[8,16,512]{2,1,0:T(8,128)S(1)}, f32[8,16,512]{2,1,0:T(8,128)S(1)}, u32[]{:S(2)}, u32[]{:S(2)}) collective-permute-start(f32[8,16,512]{2,1,0:T(8,128)S(1)} %get-tuple-element.67), channel_id=1, source_target_pairs={{0,32},{32,0},{64,96},{96,64},{128,160},{160,128},{192,224},{224,1... | collective-permute-start | bytes 786440 | tf_op jit(solution)/shard_map/ppermute | solution.py:314
  (6 other events, 4.8 us)

commit v7 on v6

--- a/solution.py
+++ b/solution.py
@@ -219,29 +219,37 @@
     height, height_up, height_down, unused, printed, *top, even, odd = refs
     chip, core, tile = place()
 
+    def row(j):
+        return pl.ds(j * FOLDS, FOLDS)
+
     @pl.when(chip == turn)
     def run():
         inside = column_mask(core)
         lane = lane_of()
         if turn:
             middle, up, down = received
-            for r in range(ROWS):
-                even[r] = up[r] + TINY
-                even[ROWS + r] = middle[r] + TINY
-                even[2 * ROWS + r] = down[r] + TINY
+            zero = jnp.zeros((8, LANES), jnp.float32)
+            for source, first in ((up, 0), (middle, ROWS), (down, 2 * ROWS)):
+                for group in range(2):
+                    tiles = [source[pl.ds(8 * group, 8), pl.ds(LANES * a, LANES)] for a in range(5)]
+
+                    def store(s, block):
+                        even[pl.ds((first + 8 * group) * FOLDS + s, 8, stride=FOLDS), :] = block + TINY
+
+                    fold_rows([zero, *tiles, zero], lane, store)
         else:
             ones = jnp.where(inside, math.exp(SHARPNESS), TINY)
             ones_up = jnp.where(tile > 0, ones, TINY)
             ones_down = jnp.where(tile < count_tiles - 1, ones, TINY)
             for r in range(ROWS):
-                even[r] = ones_up
-                even[ROWS + r] = ones
-                even[2 * ROWS + r] = ones_down
+                even[row(r), :] = ones_up
+                even[row(ROWS + r), :] = ones
+                even[row(2 * ROWS + r), :] = ones_down
         level = HALF * math.sqrt(SMOOTH_EPS)
         for k in range(LAYERS):
             source, target = (even, odd) if k % 2 == 0 else (odd, even)
             for j in range(k + 1, 47 - k):
-                total = source[j - 1] + source[j] + source[j + 1]
+                total = source[row(j - 1), :] + source[row(j), :] + source[row(j + 1), :]
                 total = total + pltpu.roll(total, 1, 1) + pltpu.roll(total, LANES - 1, 1)
                 support = jnp.log(total) * (0.5 / math.log(2.0)) - 0.5 * math.log2(9.0)
                 if j < ROWS:
@@ -256,14 +264,13 @@
                 weight = jnp.exp2(value)
                 if ROWS <= j < 2 * ROWS:
                     printed[k, j - ROWS] = value
-                if k < LAYERS - 1:
-                    target[j] = weight
-                elif top:
-                    before = pltpu.roll(pltpu.roll(weight, 1, 0), LANES - STRIDE, 1)
-                    after = pltpu.roll(pltpu.roll(weight, FOLDS - 1, 0), STRIDE, 1)
-                    weight = jnp.where(lane < HALO, before, weight)
-                    weight = jnp.where(lane >= HALO + STRIDE, after, weight)
-                    top[0][j - ROWS] = jnp.where(inside, weight, 0.0)
+                if k < LAYERS - 1 or top:
+                    target[row(j), :] = weight
+        for group in range(2 if top else 0):
+            first = (ROWS + 8 * group) * FOLDS
+            blocks = [even[pl.ds(first + s, 8, stride=FOLDS), :] for s in range(FOLDS)]
+            for a, piece in enumerate(unfold_rows(blocks, lane)):
+                top[0][pl.ds(8 * group, 8), pl.ds(LANES * a, LANES)] = piece
 
 
 def unfold_kernel(scale, folded, own, partner):
@@ -379,9 +386,9 @@
         printed, *top = call(
             functools.partial(chain_kernel, turn, tiles),
             "chain",
-            [(LAYERS, ROWS, *block), (ROWS, *block)][: 2 if turn < chips - 1 else 1],
+            [(LAYERS, ROWS, *block), (ROWS, 640)][: 2 if turn < chips - 1 else 1],
             operands,
-            scratch=[(48, *block)] * 2,
+            scratch=[(48 * FOLDS, LANES)] * 2,
             aliases={len(operands) - 1: 0},
         )
         if turn < chips - 1:

time: 127 us -> 126 us (level)
  waiting for transfers between devices: 61.2 us -> 58.5 us
  starting transfers between devices: 53.5 us -> 55.2 us
    ppermute x21, waiting for transfers between devices: 50.1 us -> 47.4 us  [local(): lax.ppermute(top[0], AXES, [(at(2 * turn + c, t), at(2 * turn + 2 + c, t...]
    ppermute x3, starting transfers between devices: 14.7 us -> 16.4 us  [swap(): return lax.ppermute(block, 'gz', [(i, i ^ 1) for i in range(slabs)])]
where the time goes in v7:
time: 126 us
  waiting for transfers between devices  58.5 us (46%)
  starting transfers between devices  55.2 us (44%)
  Pallas kernels  9 us (7%)
  other arithmetic  1.69 us (1%)
    ppermute x21, waiting for transfers between devices, local(): lax.ppermute(top[0], AXES, [(at(2 * turn + c, t), at(2 * turn + 2 + c, t...  47.4 us
    ppermute x3, starting transfers between devices, swap(): return lax.ppermute(block, 'gz', [(i, i ^ 1) for i in range(slabs)])  16.4 us
    ppermute x21, starting transfers between devices, local(): lax.ppermute(top[0], AXES, [(at(2 * turn + c, t), at(2 * turn + 2 + c, t...  15.8 us
    ppermute x2, starting transfers between devices, from_down(): return lax.ppermute(block, 'xy', [(i + 1, i) for i in range(tiles - 1)])  15.1 us
    pallas_call x14, Pallas kernels, call(): pl.pallas_call(kernel, name=name, out_shape=[pltpu.VMEM(shape, jnp.float3...  7.69 us
    ppermute x2, starting transfers between devices, from_up(): return lax.ppermute(block, 'xy', [(i, i + 1) for i in range(tiles - 1)])  5.92 us
    ppermute x1, waiting for transfers between devices, local(): far = lax.ppermute(far, 'gz', straight)  5.72 us
  transfers between devices with their start and end apart: 30, of which 8 were waited for; matrix products, arithmetic and copies ran while one was open for 1% of the time, Pallas kernels for 1%

profile of v7, /device:TPU:63, one launch (start us, length us, event | category | flops | bytes accessed | tf_op | source)
XLA Modules:
  0.0 125.6 jit_solution(1024011896992729512)
XLA Ops:
  0.6 1.3 %fetch.1 = (f32[8,16,768]{2,1,0:T(8,128)S(1)}, f32[8,16,768]{2,1,0:T(8,128)S(1)}, f32[3,16,768]{2,1,0:T(8,128)S(1)}, f32[3,16,768]{2,1,0:T(8,128)S(1)}) custom-call(f32[8,16,1024]{2,1,0:T(8,128)} %design.1), custom_call_target="tpu_custom_call" | custom-call | tf_op jit(solution)/shard_map/fetch/pallas_call | solution.py:333
  2.0 2.6 %collective-permute-start = (f32[8,16,768]{2,1,0:T(8,128)S(1)}, f32[8,16,768]{2,1,0:T(8,128)S(1)}, u32[]{:S(2)}, u32[]{:S(2)}) collective-permute-start(f32[8,16,768]{2,1,0:T(8,128)S(1)} %get-tuple-element.36), channel_id=1, source_target_pairs={{0,32},{32,0},{64,96},{96,64},{128,160},{160,128},{192,224},{224,1... | collective-permute-start | bytes 1179656 | tf_op jit(solution)/shard_map/ppermute | solution.py:321
  5.2 1.3 %collective-permute-start.2 = (f32[3,16,768]{2,1,0:T(8,128)S(1)}, f32[3,16,768]{2,1,0:T(8,128)S(1)}, u32[]{:S(2)}, u32[]{:S(2)}) collective-permute-start(f32[3,16,768]{2,1,0:T(8,128)S(1)} %get-tuple-element.38), channel_id=1, source_target_pairs={{32,96},{64,0},{96,160},{128,64},{160,224},{192,128},{224,288},{25... | collective-permute-start | bytes 442376 | tf_op jit(solution)/shard_map/ppermute | solution.py:341
  6.5 5.7 %collective-permute-done.2.far = f32[3,16,768]{2,1,0:T(8,128)S(1)} collective-permute-done((f32[3,16,768]{2,1,0:T(8,128)S(1)}, f32[3,16,768]{2,1,0:T(8,128)S(1)}, u32[]{:S(2)}, u32[]{:S(2)}) %collective-permute-start.2) | collective-permute-done | bytes 147488 | tf_op jit(solution)/shard_map/ppermute | solution.py:341
  13.1 4.0 %collective-permute-start.3 = (f32[54,8,128]{2,1,0:T(8,128)S(1)}, f32[54,8,128]{2,1,0:T(8,128)S(1)}, u32[]{:S(2)}, u32[]{:S(2)}) collective-permute-start(f32[54,8,128]{2,1,0:T(8,128)S(1)} %get-tuple-element.40), channel_id=1, source_target_pairs={{0,1},{1,2},{2,3},{3,4},{4,5},{5,6},{6,7},{7,8},{8,9},{9,10},{10,1... | collective-permute-start | bytes 663560 | tf_op jit(solution)/shard_map/ppermute | solution.py:324
  17.1 8.9 %collective-permute-start.4 = (f32[54,8,128]{2,1,0:T(8,128)S(1)}, f32[54,8,128]{2,1,0:T(8,128)S(1)}, u32[]{:S(2)}, u32[]{:S(2)}) collective-permute-start(f32[54,8,128]{2,1,0:T(8,128)S(1)} %get-tuple-element.41), channel_id=1, source_target_pairs={{1,0},{2,1},{3,2},{4,3},{5,4},{6,5},{7,6},{8,7},{9,8},{10,9},{11,1... | collective-permute-start | bytes 663560 | tf_op jit(solution)/shard_map/ppermute | solution.py:327
  25.9 2.2 %collective-permute-done.3.up = f32[54,8,128]{2,1,0:T(8,128)S(1)} collective-permute-done((f32[54,8,128]{2,1,0:T(8,128)S(1)}, f32[54,8,128]{2,1,0:T(8,128)S(1)}, u32[]{:S(2)}, u32[]{:S(2)}) %collective-permute-start.3) | collective-permute-done | bytes 221216 | tf_op jit(solution)/shard_map/ppermute | solution.py:324
  28.2 0.9 collective-permute-done.4.down
  29.1 2.8 %filter.1 = (f32[16,16,8,128]{3,2,1,0:T(8,128)S(1)}, f32[120,640]{1,0:T(8,128)S(1)}, f32[120,640]{1,0:T(8,128)S(1)}) custom-call(f32[22,16,8,128]{3,2,1,0:T(8,128)S(1)} %bitcast.23, f32[54,8,128]{2,1,0:T(8,128)S(1)} %collective-permute-done.3.up, f32[54,8,128]{2,1,0:T(8,128)S(1)} %collective-permute-done.4.down), custom_call_target="tpu_custom_call" | custom-call | tf_op jit(solution)/shard_map/filter/pallas_call | solution.py:299
  31.8 1.9 %collective-permute-start.6 = (f32[120,640]{1,0:T(8,128)S(1)}, f32[120,640]{1,0:T(8,128)S(1)}, u32[]{:S(2)}, u32[]{:S(2)}) collective-permute-start(f32[120,640]{1,0:T(8,128)S(1)} %get-tuple-element.46), channel_id=1, source_target_pairs={{0,1},{1,2},{2,3},{3,4},{4,5},{5,6},{6,7},{7,8},{8,9},{9,10},{10,1... | collective-permute-start | bytes 921608 | tf_op jit(solution)/shard_map/ppermute | solution.py:324
  33.8 6.2 %collective-permute-start.7 = (f32[120,640]{1,0:T(8,128)S(1)}, f32[120,640]{1,0:T(8,128)S(1)}, u32[]{:S(2)}, u32[]{:S(2)}) collective-permute-start(f32[120,640]{1,0:T(8,128)S(1)} %get-tuple-element.47), channel_id=1, source_target_pairs={{1,0},{2,1},{3,2},{4,3},{5,4},{6,5},{7,6},{8,7},{9,8},{10,9},{11,1... | collective-permute-start | bytes 921608 | tf_op jit(solution)/shard_map/ppermute | solution.py:327
  40.3 4.7 %collective-permute-start.5 = (f32[8,16,512]{2,1,0:T(8,128)S(1)}, f32[8,16,512]{2,1,0:T(8,128)S(1)}, u32[]{:S(2)}, u32[]{:S(2)}) collective-permute-start(f32[8,16,512]{2,1,0:T(8,128)S(1)} %get-tuple-element.44), channel_id=1, source_target_pairs={{0,32},{32,0},{64,96},{96,64},{128,160},{160,128},{192,224},{224,1... | collective-permute-start | bytes 786440 | tf_op jit(solution)/shard_map/ppermute | solution.py:321
  45.1 1.1 collective-permute-done.5
  49.0 0.8 maximum_select_fusion
  60.4 1.3 %collective-permute-start.28 = (f32[16,640]{1,0:T(8,128)S(1)}, f32[16,640]{1,0:T(8,128)S(1)}, u32[]{:S(2)}, u32[]{:S(2)}) collective-permute-start(f32[16,640]{1,0:T(8,128)S(1)} %get-tuple-element.64), channel_id=1, source_target_pairs={{385,448},{386,449},{387,450},{388,451},{389,452},{390,453},{391,4... | collective-permute-start | bytes 122888 | tf_op jit(solution)/shard_map/ppermute | solution.py:396
  61.7 1.3 %collective-permute-start.27 = (f32[16,640]{1,0:T(8,128)S(1)}, f32[16,640]{1,0:T(8,128)S(1)}, u32[]{:S(2)}, u32[]{:S(2)}) collective-permute-start(f32[16,640]{1,0:T(8,128)S(1)} %get-tuple-element.64), channel_id=1, source_target_pairs={{384,449},{385,450},{386,451},{387,452},{388,453},{389,454},{390,4... | collective-permute-start | bytes 122888 | tf_op jit(solution)/shard_map/ppermute | solution.py:396
  63.0 1.3 %collective-permute-start.26 = (f32[16,640]{1,0:T(8,128)S(1)}, f32[16,640]{1,0:T(8,128)S(1)}, u32[]{:S(2)}, u32[]{:S(2)}) collective-permute-start(f32[16,640]{1,0:T(8,128)S(1)} %get-tuple-element.64), channel_id=1, source_target_pairs={{384,448},{385,449},{386,450},{387,451},{388,452},{389,453},{390,4... | collective-permute-start | bytes 122888 | tf_op jit(solution)/shard_map/ppermute | solution.py:396
  64.3 44.4 %collective-permute-done.28.refs_2_ = f32[16,640]{1,0:T(8,128)S(1)} collective-permute-done((f32[16,640]{1,0:T(8,128)S(1)}, f32[16,640]{1,0:T(8,128)S(1)}, u32[]{:S(2)}, u32[]{:S(2)}) %collective-permute-start.28) | collective-permute-done | bytes 40992 | tf_op jit(solution)/shard_map/ppermute | solution.py:396
  108.7 2.1 %collective-permute-done.27.refs_1_ = f32[16,640]{1,0:T(8,128)S(1)} collective-permute-done((f32[16,640]{1,0:T(8,128)S(1)}, f32[16,640]{1,0:T(8,128)S(1)}, u32[]{:S(2)}, u32[]{:S(2)}) %collective-permute-start.27) | collective-permute-done | bytes 40992 | tf_op jit(solution)/shard_map/ppermute | solution.py:396
  110.8 0.9 collective-permute-done.26.refs_0_
  111.7 2.4 %chain.15 = f32[16,16,8,128]{3,2,1,0:T(8,128)S(1)} custom-call(f32[16,640]{1,0:T(8,128)S(1)} %collective-permute-done.26.refs_0_, f32[16,640]{1,0:T(8,128)S(1)} %collective-permute-done.27.refs_1_, f32[16,640]{1,0:T(8,128)S(1)} %collective-permute-done.28.refs_2_, ...), custom_call_target="tpu_custom_call", output_to_operand_aliasing={{}: (6, {})} | custom-call | tf_op jit(solution)/shard_map/chain/pallas_call | solution.py:299
  114.5 9.1 %collective-permute-start.29 = (f32[8,16,512]{2,1,0:T(8,128)S(1)}, f32[8,16,512]{2,1,0:T(8,128)S(1)}, u32[]{:S(2)}, u32[]{:S(2)}) collective-permute-start(f32[8,16,512]{2,1,0:T(8,128)S(1)} %get-tuple-element.67), channel_id=1, source_target_pairs={{0,32},{32,0},{64,96},{96,64},{128,160},{160,128},{192,224},{224,1... | collective-permute-start | bytes 786440 | tf_op jit(solution)/shard_map/ppermute | solution.py:321
  123.7 1.1 collective-permute-done.29
  124.8 0.8 maximum_select_fusion.1
  (54 shorter events, 15.2 us)
Async XLA Ops:
  2.0 10.3 %collective-permute-start = (f32[8,16,768]{2,1,0:T(8,128)S(1)}, f32[8,16,768]{2,1,0:T(8,128)S(1)}, u32[]{:S(2)}, u32[]{:S(2)}) collective-permute-start(f32[8,16,768]{2,1,0:T(8,128)S(1)} %get-tuple-element.36), channel_id=1, source_target_pairs={{0,32},{32,0},{64,96},{96,64},{128,160},{160,128},{192,224},{224,1... | collective-permute-start | bytes 1179656 | tf_op jit(solution)/shard_map/ppermute | solution.py:321
  4.5 2.0 %collective-permute-start.1 = (f32[3,16,768]{2,1,0:T(8,128)S(1)}, f32[3,16,768]{2,1,0:T(8,128)S(1)}, u32[]{:S(2)}, u32[]{:S(2)}) collective-permute-start(f32[3,16,768]{2,1,0:T(8,128)S(1)} %get-tuple-element.37), channel_id=1, source_target_pairs={{32,64},{64,32},{96,128},{128,96},{160,192},{192,160},{224,256},{2... | collective-permute-start | bytes 442376 | tf_op jit(solution)/shard_map/ppermute | solution.py:342
  5.2 7.0 %collective-permute-start.2 = (f32[3,16,768]{2,1,0:T(8,128)S(1)}, f32[3,16,768]{2,1,0:T(8,128)S(1)}, u32[]{:S(2)}, u32[]{:S(2)}) collective-permute-start(f32[3,16,768]{2,1,0:T(8,128)S(1)} %get-tuple-element.38), channel_id=1, source_target_pairs={{32,96},{64,0},{96,160},{128,64},{160,224},{192,128},{224,288},{25... | collective-permute-start | bytes 442376 | tf_op jit(solution)/shard_map/ppermute | solution.py:341
  13.1 15.1 %collective-permute-start.3 = (f32[54,8,128]{2,1,0:T(8,128)S(1)}, f32[54,8,128]{2,1,0:T(8,128)S(1)}, u32[]{:S(2)}, u32[]{:S(2)}) collective-permute-start(f32[54,8,128]{2,1,0:T(8,128)S(1)} %get-tuple-element.40), channel_id=1, source_target_pairs={{0,1},{1,2},{2,3},{3,4},{4,5},{5,6},{6,7},{7,8},{8,9},{9,10},{10,1... | collective-permute-start | bytes 663560 | tf_op jit(solution)/shard_map/ppermute | solution.py:324
  17.1 12.0 %collective-permute-start.4 = (f32[54,8,128]{2,1,0:T(8,128)S(1)}, f32[54,8,128]{2,1,0:T(8,128)S(1)}, u32[]{:S(2)}, u32[]{:S(2)}) collective-permute-start(f32[54,8,128]{2,1,0:T(8,128)S(1)} %get-tuple-element.41), channel_id=1, source_target_pairs={{1,0},{2,1},{3,2},{4,3},{5,4},{6,5},{7,6},{8,7},{9,8},{10,9},{11,1... | collective-permute-start | bytes 663560 | tf_op jit(solution)/shard_map/ppermute | solution.py:327
  31.8 14.4 %collective-permute-start.6 = (f32[120,640]{1,0:T(8,128)S(1)}, f32[120,640]{1,0:T(8,128)S(1)}, u32[]{:S(2)}, u32[]{:S(2)}) collective-permute-start(f32[120,640]{1,0:T(8,128)S(1)} %get-tuple-element.46), channel_id=1, source_target_pairs={{0,1},{1,2},{2,3},{3,4},{4,5},{5,6},{6,7},{7,8},{8,9},{9,10},{10,1... | collective-permute-start | bytes 921608 | tf_op jit(solution)/shard_map/ppermute | solution.py:324
  33.8 12.8 %collective-permute-start.7 = (f32[120,640]{1,0:T(8,128)S(1)}, f32[120,640]{1,0:T(8,128)S(1)}, u32[]{:S(2)}, u32[]{:S(2)}) collective-permute-start(f32[120,640]{1,0:T(8,128)S(1)} %get-tuple-element.47), channel_id=1, source_target_pairs={{1,0},{2,1},{3,2},{4,3},{5,4},{6,5},{7,6},{8,7},{9,8},{10,9},{11,1... | collective-permute-start | bytes 921608 | tf_op jit(solution)/shard_map/ppermute | solution.py:327
  40.3 5.8 %collective-permute-start.5 = (f32[8,16,512]{2,1,0:T(8,128)S(1)}, f32[8,16,512]{2,1,0:T(8,128)S(1)}, u32[]{:S(2)}, u32[]{:S(2)}) collective-permute-start(f32[8,16,512]{2,1,0:T(8,128)S(1)} %get-tuple-element.44), channel_id=1, source_target_pairs={{0,32},{32,0},{64,96},{96,64},{128,160},{160,128},{192,224},{224,1... | collective-permute-start | bytes 786440 | tf_op jit(solution)/shard_map/ppermute | solution.py:321
  47.0 2.9 %collective-permute-start.10 = (f32[16,640]{1,0:T(8,128)S(1)}, f32[16,640]{1,0:T(8,128)S(1)}, u32[]{:S(2)}, u32[]{:S(2)}) collective-permute-start(f32[16,640]{1,0:T(8,128)S(1)} %get-tuple-element.52), channel_id=1, source_target_pairs={{1,64},{2,65},{3,66},{4,67},{5,68},{6,69},{7,70},{8,71},{9,72},{10... | collective-permute-start | bytes 122888 | tf_op jit(solution)/shard_map/ppermute | solution.py:396
  47.6 2.2 %collective-permute-start.9 = (f32[16,640]{1,0:T(8,128)S(1)}, f32[16,640]{1,0:T(8,128)S(1)}, u32[]{:S(2)}, u32[]{:S(2)}) collective-permute-start(f32[16,640]{1,0:T(8,128)S(1)} %get-tuple-element.52), channel_id=1, source_target_pairs={{0,65},{1,66},{2,67},{3,68},{4,69},{5,70},{6,71},{7,72},{8,73},{9,... | collective-permute-start | bytes 122888 | tf_op jit(solution)/shard_map/ppermute | solution.py:396
  48.3 1.5 %collective-permute-start.8 = (f32[16,640]{1,0:T(8,128)S(1)}, f32[16,640]{1,0:T(8,128)S(1)}, u32[]{:S(2)}, u32[]{:S(2)}) collective-permute-start(f32[16,640]{1,0:T(8,128)S(1)} %get-tuple-element.52), channel_id=1, source_target_pairs={{0,64},{1,65},{2,66},{3,67},{4,68},{5,69},{6,70},{7,71},{8,72},{9,... | collective-permute-start | bytes 122888 | tf_op jit(solution)/shard_map/ppermute | solution.py:396
  49.9 2.0 %collective-permute-start.13 = (f32[16,640]{1,0:T(8,128)S(1)}, f32[16,640]{1,0:T(8,128)S(1)}, u32[]{:S(2)}, u32[]{:S(2)}) collective-permute-start(f32[16,640]{1,0:T(8,128)S(1)} %get-tuple-element.54), channel_id=1, source_target_pairs={{65,128},{66,129},{67,130},{68,131},{69,132},{70,133},{71,134},{72... | collective-permute-start | bytes 122888 | tf_op jit(solution)/shard_map/ppermute | solution.py:396
  50.5 1.4 %collective-permute-start.12 = (f32[16,640]{1,0:T(8,128)S(1)}, f32[16,640]{1,0:T(8,128)S(1)}, u32[]{:S(2)}, u32[]{:S(2)}) collective-permute-start(f32[16,640]{1,0:T(8,128)S(1)} %get-tuple-element.54), channel_id=1, source_target_pairs={{64,129},{65,130},{66,131},{67,132},{68,133},{69,134},{70,135},{71... | collective-permute-start | bytes 122888 | tf_op jit(solution)/shard_map/ppermute | solution.py:396
  51.9 2.0 %collective-permute-start.16 = (f32[16,640]{1,0:T(8,128)S(1)}, f32[16,640]{1,0:T(8,128)S(1)}, u32[]{:S(2)}, u32[]{:S(2)}) collective-permute-start(f32[16,640]{1,0:T(8,128)S(1)} %get-tuple-element.56), channel_id=1, source_target_pairs={{129,192},{130,193},{131,194},{132,195},{133,196},{134,197},{135,1... | collective-permute-start | bytes 122888 | tf_op jit(solution)/shard_map/ppermute | solution.py:396
  52.6 1.4 %collective-permute-start.15 = (f32[16,640]{1,0:T(8,128)S(1)}, f32[16,640]{1,0:T(8,128)S(1)}, u32[]{:S(2)}, u32[]{:S(2)}) collective-permute-start(f32[16,640]{1,0:T(8,128)S(1)} %get-tuple-element.56), channel_id=1, source_target_pairs={{128,193},{129,194},{130,195},{131,196},{132,197},{133,198},{134,1... | collective-permute-start | bytes 122888 | tf_op jit(solution)/shard_map/ppermute | solution.py:396
  54.2 2.0 %collective-permute-start.19 = (f32[16,640]{1,0:T(8,128)S(1)}, f32[16,640]{1,0:T(8,128)S(1)}, u32[]{:S(2)}, u32[]{:S(2)}) collective-permute-start(f32[16,640]{1,0:T(8,128)S(1)} %get-tuple-element.58), channel_id=1, source_target_pairs={{193,256},{194,257},{195,258},{196,259},{197,260},{198,261},{199,2... | collective-permute-start | bytes 122888 | tf_op jit(solution)/shard_map/ppermute | solution.py:396
  54.9 1.4 %collective-permute-start.18 = (f32[16,640]{1,0:T(8,128)S(1)}, f32[16,640]{1,0:T(8,128)S(1)}, u32[]{:S(2)}, u32[]{:S(2)}) collective-permute-start(f32[16,640]{1,0:T(8,128)S(1)} %get-tuple-element.58), channel_id=1, source_target_pairs={{192,257},{193,258},{194,259},{195,260},{196,261},{197,262},{198,2... | collective-permute-start | bytes 122888 | tf_op jit(solution)/shard_map/ppermute | solution.py:396
  56.3 2.0 %collective-permute-start.22 = (f32[16,640]{1,0:T(8,128)S(1)}, f32[16,640]{1,0:T(8,128)S(1)}, u32[]{:S(2)}, u32[]{:S(2)}) collective-permute-start(f32[16,640]{1,0:T(8,128)S(1)} %get-tuple-element.60), channel_id=1, source_target_pairs={{257,320},{258,321},{259,322},{260,323},{261,324},{262,325},{263,3... | collective-permute-start | bytes 122888 | tf_op jit(solution)/shard_map/ppermute | solution.py:396
  58.3 2.0 %collective-permute-start.25 = (f32[16,640]{1,0:T(8,128)S(1)}, f32[16,640]{1,0:T(8,128)S(1)}, u32[]{:S(2)}, u32[]{:S(2)}) collective-permute-start(f32[16,640]{1,0:T(8,128)S(1)} %get-tuple-element.62), channel_id=1, source_target_pairs={{321,384},{322,385},{323,386},{324,387},{325,388},{326,389},{327,3... | collective-permute-start | bytes 122888 | tf_op jit(solution)/shard_map/ppermute | solution.py:396
  59.0 1.4 %collective-permute-start.24 = (f32[16,640]{1,0:T(8,128)S(1)}, f32[16,640]{1,0:T(8,128)S(1)}, u32[]{:S(2)}, u32[]{:S(2)}) collective-permute-start(f32[16,640]{1,0:T(8,128)S(1)} %get-tuple-element.62), channel_id=1, source_target_pairs={{320,385},{321,386},{322,387},{323,388},{324,389},{325,390},{326,3... | collective-permute-start | bytes 122888 | tf_op jit(solution)/shard_map/ppermute | solution.py:396
  60.4 48.3 %collective-permute-start.28 = (f32[16,640]{1,0:T(8,128)S(1)}, f32[16,640]{1,0:T(8,128)S(1)}, u32[]{:S(2)}, u32[]{:S(2)}) collective-permute-start(f32[16,640]{1,0:T(8,128)S(1)} %get-tuple-element.64), channel_id=1, source_target_pairs={{385,448},{386,449},{387,450},{388,451},{389,452},{390,453},{391,4... | collective-permute-start | bytes 122888 | tf_op jit(solution)/shard_map/ppermute | solution.py:396
  61.7 49.1 %collective-permute-start.27 = (f32[16,640]{1,0:T(8,128)S(1)}, f32[16,640]{1,0:T(8,128)S(1)}, u32[]{:S(2)}, u32[]{:S(2)}) collective-permute-start(f32[16,640]{1,0:T(8,128)S(1)} %get-tuple-element.64), channel_id=1, source_target_pairs={{384,449},{385,450},{386,451},{387,452},{388,453},{389,454},{390,4... | collective-permute-start | bytes 122888 | tf_op jit(solution)/shard_map/ppermute | solution.py:396
  63.0 48.7 %collective-permute-start.26 = (f32[16,640]{1,0:T(8,128)S(1)}, f32[16,640]{1,0:T(8,128)S(1)}, u32[]{:S(2)}, u32[]{:S(2)}) collective-permute-start(f32[16,640]{1,0:T(8,128)S(1)} %get-tuple-element.64), channel_id=1, source_target_pairs={{384,448},{385,449},{386,450},{387,451},{388,452},{389,453},{390,4... | collective-permute-start | bytes 122888 | tf_op jit(solution)/shard_map/ppermute | solution.py:396
  114.5 10.3 %collective-permute-start.29 = (f32[8,16,512]{2,1,0:T(8,128)S(1)}, f32[8,16,512]{2,1,0:T(8,128)S(1)}, u32[]{:S(2)}, u32[]{:S(2)}) collective-permute-start(f32[8,16,512]{2,1,0:T(8,128)S(1)} %get-tuple-element.67), channel_id=1, source_target_pairs={{0,32},{32,0},{64,96},{96,64},{128,160},{160,128},{192,224},{224,1... | collective-permute-start | bytes 786440 | tf_op jit(solution)/shard_map/ppermute | solution.py:321
  (6 other events, 4.8 us)

commit v8 on v7

--- a/solution.py
+++ b/solution.py
@@ -46,17 +46,20 @@
     return (column >= 0) & (column < 1024)
 
 
-def fetch_kernel(design, own, partner, near, far, done):
+def fetch_kernel(design, own, near, far, *refs):
     unused, core, unused = place()
     here = pl.ds(pl.multiple_of(256 * core, LANES), PART)
     there = pl.ds(pl.multiple_of(256 * (1 - core), LANES), PART)
     rim = pl.ds((8 - REACH) * core, REACH)
+    *parts, done = refs
     copies = [
         pltpu.make_async_copy(design.at[rim, :, here], far, done.at[0]),
         pltpu.make_async_copy(design.at[rim, :, there], near, done.at[1]),
-        pltpu.make_async_copy(design.at[:, :, there], partner, done.at[2]),
-        pltpu.make_async_copy(design.at[:, :, here], own, done.at[3]),
+        pltpu.make_async_copy(design.at[:, :, here], own, done.at[2]),
     ]
+    for i, part in enumerate(parts):
+        side = pl.ds(pl.multiple_of(256 * (1 - core) + 256 * i, LANES), 256)
+        copies.append(pltpu.make_async_copy(design.at[:, :, side], part, done.at[3 + i]))
     for copy in copies:
         copy.start()
     for copy in copies:
@@ -88,7 +91,7 @@
     return tiles
 
 
-def fold_kernel(own, partner, near, far, out, to_down, to_up):
+def fold_kernel(own, near, far, first, second, third, out, to_down, to_up):
     unused, core, unused = place()
     lane = lane_of()
 
@@ -97,8 +100,15 @@
             for group in range(2):
                 tiles = []
                 for a in range(7):
-                    at = jnp.clip(a - 1 + core, 0, 5) * LANES
-                    tile = source[i, pl.ds(8 * group, 8), pl.ds(pl.multiple_of(at, LANES), LANES)]
+                    if isinstance(source, tuple):
+                        sides = [
+                            source[b // 2][i, pl.ds(8 * group, 8), pl.ds(b % 2 * LANES, LANES)]
+                            for b in (max(a - 1, 0), min(a, 5))
+                        ]
+                        tile = jnp.where(core == 0, *sides)
+                    else:
+                        at = jnp.clip(a - 1 + core, 0, 5) * LANES
+                        tile = source[i, pl.ds(8 * group, 8), pl.ds(pl.multiple_of(at, LANES), LANES)]
                     if a == 0:
                         tile = jnp.where(core == 0, 0.0, tile)
                     if a == 6:
@@ -115,7 +125,7 @@
         lax.fori_loop(0, count, layer, 0, unroll=count)
 
     fold(own, REACH + 8 * core, 8)
-    fold(partner, REACH + 8 * (1 - core), 8)
+    fold((first, second, third), REACH + 8 * (1 - core), 8)
     fold(near, 19 * core, REACH)
     fold(far, 19 * (1 - core), REACH)
     at = 0
@@ -330,23 +340,24 @@
     straight = [(i, j) for k in range(1, chips) for i, j in ((2 * k - 1, 2 * k + 1), (2 * k, 2 * k - 2))]
     vmem = pl.BlockSpec(memory_space=pltpu.VMEM)
     whole, rim = (8, ROWS, PART), (REACH, ROWS, PART)
-    own, partner, near, far = pl.pallas_call(
+    part = (8, ROWS, 256)
+    own, near, far, *parts = pl.pallas_call(
         fetch_kernel,
         name="fetch",
-        out_shape=[pltpu.VMEM(shape, jnp.float32) for shape in (whole, whole, rim, rim)],
+        out_shape=[pltpu.VMEM(shape, jnp.float32) for shape in (whole, rim, rim, part, part, part)],
         in_specs=[pl.BlockSpec(memory_space=pltpu.HBM)],
-        out_specs=[vmem] * 4,
-        scratch_shapes=[pltpu.SemaphoreType.DMA((4,))],
+        out_specs=[vmem] * 6,
+        scratch_shapes=[pltpu.SemaphoreType.DMA((6,))],
     )(pltpu.with_memory_space_constraint(design, pltpu.HBM))
     far = lax.ppermute(far, "gz", straight)
     near = lax.ppermute(near, "gz", crossing)
-    partner = swap(partner)
+    parts = [swap(part) for part in parts]
     block = (FOLDS, LANES)
     folded, to_down, to_up = call(
         fold_kernel,
         "fold",
         [(22 * ROWS * FOLDS, LANES), (SIDE, *block), (SIDE, *block)],
-        [own, partner, near, far],
+        [own, near, far, *parts],
     )
     height, to_down, to_up = call(
         functools.partial(filter_kernel, chips, tiles),

time: 126 us -> 129 us (1.024)
  starting transfers between devices: 55.2 us -> 62.1 us
  waiting for transfers between devices: 58.5 us -> 54.7 us
    ppermute x3 -> x5, starting transfers between devices: 16.4 us -> 23.4 us  [swap(): return lax.ppermute(block, 'gz', [(i, i ^ 1) for i in range(slabs)])]
    ppermute x1, waiting for transfers between devices: 5.72 us -> 0.01 us  [local(): far = lax.ppermute(far, 'gz', straight)]
    ppermute x2, waiting for transfers between devices: 2.21 us -> 3.57 us  [from_up(): return lax.ppermute(block, 'xy', [(i, i + 1) for i in range(tiles - 1)])]
    ppermute x3 -> x5, waiting for transfers between devices: 2.28 us -> 3.22 us  [swap(): return lax.ppermute(block, 'gz', [(i, i ^ 1) for i in range(slabs)])]
  transfers between devices with their start and end apart: 30 -> 32, of which waited for: 8 -> 9; matrix products, arithmetic and copies ran while one was open for 1% -> 1% of each run, Pallas kernels for 1% -> 1%
where the time goes in v8:
time: 129 us
  starting transfers between devices  62.1 us (48%)
  waiting for transfers between devices  54.7 us (42%)
  Pallas kernels  9.01 us (7%)
  other arithmetic  1.69 us (1%)
    ppermute x21, waiting for transfers between devices, local(): lax.ppermute(top[0], AXES, [(at(2 * turn + c, t), at(2 * turn + 2 + c, t...  46.9 us
    ppermute x5, starting transfers between devices, swap(): return lax.ppermute(block, 'gz', [(i, i ^ 1) for i in range(slabs)])  23.4 us
    ppermute x21, starting transfers between devices, local(): lax.ppermute(top[0], AXES, [(at(2 * turn + c, t), at(2 * turn + 2 + c, t...  15.8 us
    ppermute x2, starting transfers between devices, from_down(): return lax.ppermute(block, 'xy', [(i + 1, i) for i in range(tiles - 1)])  15.1 us
    pallas_call x14, Pallas kernels, call(): pl.pallas_call(kernel, name=name, out_shape=[pltpu.VMEM(shape, jnp.float3...  7.69 us
    ppermute x2, starting transfers between devices, from_up(): return lax.ppermute(block, 'xy', [(i, i + 1) for i in range(tiles - 1)])  5.92 us
    ppermute x2, waiting for transfers between devices, from_up(): return lax.ppermute(block, 'xy', [(i, i + 1) for i in range(tiles - 1)])  3.57 us
    ppermute x5, waiting for transfers between devices, swap(): return lax.ppermute(block, 'gz', [(i, i ^ 1) for i in range(slabs)])  3.22 us
  transfers between devices with their start and end apart: 32, of which 9 were waited for; matrix products, arithmetic and copies ran while one was open for 1% of the time, Pallas kernels for 1%

profile of v8, /device:TPU:63, one launch (start us, length us, event | category | flops | bytes accessed | tf_op | source)
XLA Modules:
  0.0 128.8 jit_solution(13617476845090847465)
XLA Ops:
  0.6 1.3 %fetch.1 = (f32[8,16,768]{2,1,0:T(8,128)S(1)}, f32[3,16,768]{2,1,0:T(8,128)S(1)}, f32[3,16,768]{2,1,0:T(8,128)S(1)}, f32[8,16,256]{2,1,0:T(8,128)S(1)}, f32[8,16...) custom-call(f32[8,16,1024]{2,1,0:T(8,128)} %design.1), custom_call_target="tpu_custom_call" | custom-call | tf_op jit(solution)/shard_map/fetch/pallas_call | solution.py:344
  2.6 1.3 %collective-permute-start.1 = (f32[3,16,768]{2,1,0:T(8,128)S(1)}, f32[3,16,768]{2,1,0:T(8,128)S(1)}, u32[]{:S(2)}, u32[]{:S(2)}) collective-permute-start(f32[3,16,768]{2,1,0:T(8,128)S(1)} %get-tuple-element.39), channel_id=1, source_target_pairs={{32,96},{64,0},{96,160},{128,64},{160,224},{192,128},{224,288},{25... | collective-permute-start | bytes 442376 | tf_op jit(solution)/shard_map/ppermute | solution.py:352
  3.9 6.6 %collective-permute-start.2 = (f32[8,16,256]{2,1,0:T(8,128)S(1)}, f32[8,16,256]{2,1,0:T(8,128)S(1)}, u32[]{:S(2)}, u32[]{:S(2)}) collective-permute-start(f32[8,16,256]{2,1,0:T(8,128)S(1)} %get-tuple-element.40), channel_id=1, source_target_pairs={{0,32},{32,0},{64,96},{96,64},{128,160},{160,128},{192,224},{224,1... | collective-permute-start | bytes 393224 | tf_op jit(solution)/shard_map/ppermute | solution.py:331
  10.5 1.9 %collective-permute-start.3 = (f32[8,16,256]{2,1,0:T(8,128)S(1)}, f32[8,16,256]{2,1,0:T(8,128)S(1)}, u32[]{:S(2)}, u32[]{:S(2)}) collective-permute-start(f32[8,16,256]{2,1,0:T(8,128)S(1)} %get-tuple-element.41), channel_id=1, source_target_pairs={{0,32},{32,0},{64,96},{96,64},{128,160},{160,128},{192,224},{224,1... | collective-permute-start | bytes 393224 | tf_op jit(solution)/shard_map/ppermute | solution.py:331
  12.4 2.4 %collective-permute-start.4 = (f32[8,16,256]{2,1,0:T(8,128)S(1)}, f32[8,16,256]{2,1,0:T(8,128)S(1)}, u32[]{:S(2)}, u32[]{:S(2)}) collective-permute-start(f32[8,16,256]{2,1,0:T(8,128)S(1)} %get-tuple-element.42), channel_id=1, source_target_pairs={{0,32},{32,0},{64,96},{96,64},{128,160},{160,128},{192,224},{224,1... | collective-permute-start | bytes 393224 | tf_op jit(solution)/shard_map/ppermute | solution.py:331
  14.9 0.9 collective-permute-done.4.third
  16.7 4.0 %collective-permute-start.5 = (f32[54,8,128]{2,1,0:T(8,128)S(1)}, f32[54,8,128]{2,1,0:T(8,128)S(1)}, u32[]{:S(2)}, u32[]{:S(2)}) collective-permute-start(f32[54,8,128]{2,1,0:T(8,128)S(1)} %get-tuple-element.44), channel_id=1, source_target_pairs={{0,1},{1,2},{2,3},{3,4},{4,5},{5,6},{6,7},{7,8},{8,9},{9,10},{10,1... | collective-permute-start | bytes 663560 | tf_op jit(solution)/shard_map/ppermute | solution.py:334
  20.7 8.9 %collective-permute-start.6 = (f32[54,8,128]{2,1,0:T(8,128)S(1)}, f32[54,8,128]{2,1,0:T(8,128)S(1)}, u32[]{:S(2)}, u32[]{:S(2)}) collective-permute-start(f32[54,8,128]{2,1,0:T(8,128)S(1)} %get-tuple-element.45), channel_id=1, source_target_pairs={{1,0},{2,1},{3,2},{4,3},{5,4},{6,5},{7,6},{8,7},{9,8},{10,9},{11,1... | collective-permute-start | bytes 663560 | tf_op jit(solution)/shard_map/ppermute | solution.py:337
  29.5 3.6 %collective-permute-done.5.up = f32[54,8,128]{2,1,0:T(8,128)S(1)} collective-permute-done((f32[54,8,128]{2,1,0:T(8,128)S(1)}, f32[54,8,128]{2,1,0:T(8,128)S(1)}, u32[]{:S(2)}, u32[]{:S(2)}) %collective-permute-start.5) | collective-permute-done | bytes 221216 | tf_op jit(solution)/shard_map/ppermute | solution.py:334
  33.1 0.9 collective-permute-done.6.down
  34.0 2.8 %filter.1 = (f32[16,16,8,128]{3,2,1,0:T(8,128)S(1)}, f32[120,640]{1,0:T(8,128)S(1)}, f32[120,640]{1,0:T(8,128)S(1)}) custom-call(f32[22,16,8,128]{3,2,1,0:T(8,128)S(1)} %bitcast.23, f32[54,8,128]{2,1,0:T(8,128)S(1)} %collective-permute-done.5.up, f32[54,8,128]{2,1,0:T(8,128)S(1)} %collective-permute-done.6.down), custom_call_target="tpu_custom_call" | custom-call | tf_op jit(solution)/shard_map/filter/pallas_call | solution.py:309
  36.7 1.9 %collective-permute-start.8 = (f32[120,640]{1,0:T(8,128)S(1)}, f32[120,640]{1,0:T(8,128)S(1)}, u32[]{:S(2)}, u32[]{:S(2)}) collective-permute-start(f32[120,640]{1,0:T(8,128)S(1)} %get-tuple-element.50), channel_id=1, source_target_pairs={{0,1},{1,2},{2,3},{3,4},{4,5},{5,6},{6,7},{7,8},{8,9},{9,10},{10,1... | collective-permute-start | bytes 921608 | tf_op jit(solution)/shard_map/ppermute | solution.py:334
  38.7 6.2 %collective-permute-start.9 = (f32[120,640]{1,0:T(8,128)S(1)}, f32[120,640]{1,0:T(8,128)S(1)}, u32[]{:S(2)}, u32[]{:S(2)}) collective-permute-start(f32[120,640]{1,0:T(8,128)S(1)} %get-tuple-element.51), channel_id=1, source_target_pairs={{1,0},{2,1},{3,2},{4,3},{5,4},{6,5},{7,6},{8,7},{9,8},{10,9},{11,1... | collective-permute-start | bytes 921608 | tf_op jit(solution)/shard_map/ppermute | solution.py:337
  45.2 3.4 %collective-permute-start.7 = (f32[8,16,512]{2,1,0:T(8,128)S(1)}, f32[8,16,512]{2,1,0:T(8,128)S(1)}, u32[]{:S(2)}, u32[]{:S(2)}) collective-permute-start(f32[8,16,512]{2,1,0:T(8,128)S(1)} %get-tuple-element.48), channel_id=1, source_target_pairs={{0,32},{32,0},{64,96},{96,64},{128,160},{160,128},{192,224},{224,1... | collective-permute-start | bytes 786440 | tf_op jit(solution)/shard_map/ppermute | solution.py:331
  48.6 1.1 collective-permute-done.7
  64.1 1.3 %collective-permute-start.30 = (f32[16,640]{1,0:T(8,128)S(1)}, f32[16,640]{1,0:T(8,128)S(1)}, u32[]{:S(2)}, u32[]{:S(2)}) collective-permute-start(f32[16,640]{1,0:T(8,128)S(1)} %get-tuple-element.68), channel_id=1, source_target_pairs={{385,448},{386,449},{387,450},{388,451},{389,452},{390,453},{391,4... | collective-permute-start | bytes 122888 | tf_op jit(solution)/shard_map/ppermute | solution.py:407
  65.4 1.3 %collective-permute-start.29 = (f32[16,640]{1,0:T(8,128)S(1)}, f32[16,640]{1,0:T(8,128)S(1)}, u32[]{:S(2)}, u32[]{:S(2)}) collective-permute-start(f32[16,640]{1,0:T(8,128)S(1)} %get-tuple-element.68), channel_id=1, source_target_pairs={{384,449},{385,450},{386,451},{387,452},{388,453},{389,454},{390,4... | collective-permute-start | bytes 122888 | tf_op jit(solution)/shard_map/ppermute | solution.py:407
  66.7 1.3 %collective-permute-start.28 = (f32[16,640]{1,0:T(8,128)S(1)}, f32[16,640]{1,0:T(8,128)S(1)}, u32[]{:S(2)}, u32[]{:S(2)}) collective-permute-start(f32[16,640]{1,0:T(8,128)S(1)} %get-tuple-element.68), channel_id=1, source_target_pairs={{384,448},{385,449},{386,450},{387,451},{388,452},{389,453},{390,4... | collective-permute-start | bytes 122888 | tf_op jit(solution)/shard_map/ppermute | solution.py:407
  68.0 43.8 %collective-permute-done.30.refs_2_ = f32[16,640]{1,0:T(8,128)S(1)} collective-permute-done((f32[16,640]{1,0:T(8,128)S(1)}, f32[16,640]{1,0:T(8,128)S(1)}, u32[]{:S(2)}, u32[]{:S(2)}) %collective-permute-start.30) | collective-permute-done | bytes 40992 | tf_op jit(solution)/shard_map/ppermute | solution.py:407
  111.9 2.1 %collective-permute-done.29.refs_1_ = f32[16,640]{1,0:T(8,128)S(1)} collective-permute-done((f32[16,640]{1,0:T(8,128)S(1)}, f32[16,640]{1,0:T(8,128)S(1)}, u32[]{:S(2)}, u32[]{:S(2)}) %collective-permute-start.29) | collective-permute-done | bytes 40992 | tf_op jit(solution)/shard_map/ppermute | solution.py:407
  114.0 0.9 collective-permute-done.28.refs_0_
  114.9 2.4 %chain.15 = f32[16,16,8,128]{3,2,1,0:T(8,128)S(1)} custom-call(f32[16,640]{1,0:T(8,128)S(1)} %collective-permute-done.28.refs_0_, f32[16,640]{1,0:T(8,128)S(1)} %collective-permute-done.29.refs_1_, f32[16,640]{1,0:T(8,128)S(1)} %collective-permute-done.30.refs_2_, ...), custom_call_target="tpu_custom_call", output_to_operand_aliasing={{}: (6, {})} | custom-call | tf_op jit(solution)/shard_map/chain/pallas_call | solution.py:309
  117.7 9.1 %collective-permute-start.31 = (f32[8,16,512]{2,1,0:T(8,128)S(1)}, f32[8,16,512]{2,1,0:T(8,128)S(1)}, u32[]{:S(2)}, u32[]{:S(2)}) collective-permute-start(f32[8,16,512]{2,1,0:T(8,128)S(1)} %get-tuple-element.71), channel_id=1, source_target_pairs={{0,32},{32,0},{64,96},{96,64},{128,160},{160,128},{192,224},{224,1... | collective-permute-start | bytes 786440 | tf_op jit(solution)/shard_map/ppermute | solution.py:331
  126.8 1.1 collective-permute-done.31
  (58 shorter events, 17.1 us)
Async XLA Ops:
  2.0 13.9 %collective-permute-start = (f32[3,16,768]{2,1,0:T(8,128)S(1)}, f32[3,16,768]{2,1,0:T(8,128)S(1)}, u32[]{:S(2)}, u32[]{:S(2)}) collective-permute-start(f32[3,16,768]{2,1,0:T(8,128)S(1)} %get-tuple-element.38), channel_id=1, source_target_pairs={{32,64},{64,32},{96,128},{128,96},{160,192},{192,160},{224,256},{2... | collective-permute-start | bytes 442376 | tf_op jit(solution)/shard_map/ppermute | solution.py:353
  2.6 13.2 %collective-permute-start.1 = (f32[3,16,768]{2,1,0:T(8,128)S(1)}, f32[3,16,768]{2,1,0:T(8,128)S(1)}, u32[]{:S(2)}, u32[]{:S(2)}) collective-permute-start(f32[3,16,768]{2,1,0:T(8,128)S(1)} %get-tuple-element.39), channel_id=1, source_target_pairs={{32,96},{64,0},{96,160},{128,64},{160,224},{192,128},{224,288},{25... | collective-permute-start | bytes 442376 | tf_op jit(solution)/shard_map/ppermute | solution.py:352
  3.9 10.9 %collective-permute-start.2 = (f32[8,16,256]{2,1,0:T(8,128)S(1)}, f32[8,16,256]{2,1,0:T(8,128)S(1)}, u32[]{:S(2)}, u32[]{:S(2)}) collective-permute-start(f32[8,16,256]{2,1,0:T(8,128)S(1)} %get-tuple-element.40), channel_id=1, source_target_pairs={{0,32},{32,0},{64,96},{96,64},{128,160},{160,128},{192,224},{224,1... | collective-permute-start | bytes 393224 | tf_op jit(solution)/shard_map/ppermute | solution.py:331
  10.5 4.4 %collective-permute-start.3 = (f32[8,16,256]{2,1,0:T(8,128)S(1)}, f32[8,16,256]{2,1,0:T(8,128)S(1)}, u32[]{:S(2)}, u32[]{:S(2)}) collective-permute-start(f32[8,16,256]{2,1,0:T(8,128)S(1)} %get-tuple-element.41), channel_id=1, source_target_pairs={{0,32},{32,0},{64,96},{96,64},{128,160},{160,128},{192,224},{224,1... | collective-permute-start | bytes 393224 | tf_op jit(solution)/shard_map/ppermute | solution.py:331
  12.4 3.4 %collective-permute-start.4 = (f32[8,16,256]{2,1,0:T(8,128)S(1)}, f32[8,16,256]{2,1,0:T(8,128)S(1)}, u32[]{:S(2)}, u32[]{:S(2)}) collective-permute-start(f32[8,16,256]{2,1,0:T(8,128)S(1)} %get-tuple-element.42), channel_id=1, source_target_pairs={{0,32},{32,0},{64,96},{96,64},{128,160},{160,128},{192,224},{224,1... | collective-permute-start | bytes 393224 | tf_op jit(solution)/shard_map/ppermute | solution.py:331
  16.7 16.4 %collective-permute-start.5 = (f32[54,8,128]{2,1,0:T(8,128)S(1)}, f32[54,8,128]{2,1,0:T(8,128)S(1)}, u32[]{:S(2)}, u32[]{:S(2)}) collective-permute-start(f32[54,8,128]{2,1,0:T(8,128)S(1)} %get-tuple-element.44), channel_id=1, source_target_pairs={{0,1},{1,2},{2,3},{3,4},{4,5},{5,6},{6,7},{7,8},{8,9},{9,10},{10,1... | collective-permute-start | bytes 663560 | tf_op jit(solution)/shard_map/ppermute | solution.py:334
  20.7 13.3 %collective-permute-start.6 = (f32[54,8,128]{2,1,0:T(8,128)S(1)}, f32[54,8,128]{2,1,0:T(8,128)S(1)}, u32[]{:S(2)}, u32[]{:S(2)}) collective-permute-start(f32[54,8,128]{2,1,0:T(8,128)S(1)} %get-tuple-element.45), channel_id=1, source_target_pairs={{1,0},{2,1},{3,2},{4,3},{5,4},{6,5},{7,6},{8,7},{9,8},{10,9},{11,1... | collective-permute-start | bytes 663560 | tf_op jit(solution)/shard_map/ppermute | solution.py:337
  36.7 13.0 %collective-permute-start.8 = (f32[120,640]{1,0:T(8,128)S(1)}, f32[120,640]{1,0:T(8,128)S(1)}, u32[]{:S(2)}, u32[]{:S(2)}) collective-permute-start(f32[120,640]{1,0:T(8,128)S(1)} %get-tuple-element.50), channel_id=1, source_target_pairs={{0,1},{1,2},{2,3},{3,4},{4,5},{5,6},{6,7},{7,8},{8,9},{9,10},{10,1... | collective-permute-start | bytes 921608 | tf_op jit(solution)/shard_map/ppermute | solution.py:334
  38.7 11.6 %collective-permute-start.9 = (f32[120,640]{1,0:T(8,128)S(1)}, f32[120,640]{1,0:T(8,128)S(1)}, u32[]{:S(2)}, u32[]{:S(2)}) collective-permute-start(f32[120,640]{1,0:T(8,128)S(1)} %get-tuple-element.51), channel_id=1, source_target_pairs={{1,0},{2,1},{3,2},{4,3},{5,4},{6,5},{7,6},{8,7},{9,8},{10,9},{11,1... | collective-permute-start | bytes 921608 | tf_op jit(solution)/shard_map/ppermute | solution.py:337
  45.2 4.5 %collective-permute-start.7 = (f32[8,16,512]{2,1,0:T(8,128)S(1)}, f32[8,16,512]{2,1,0:T(8,128)S(1)}, u32[]{:S(2)}, u32[]{:S(2)}) collective-permute-start(f32[8,16,512]{2,1,0:T(8,128)S(1)} %get-tuple-element.48), channel_id=1, source_target_pairs={{0,32},{32,0},{64,96},{96,64},{128,160},{160,128},{192,224},{224,1... | collective-permute-start | bytes 786440 | tf_op jit(solution)/shard_map/ppermute | solution.py:331
  50.7 2.9 %collective-permute-start.12 = (f32[16,640]{1,0:T(8,128)S(1)}, f32[16,640]{1,0:T(8,128)S(1)}, u32[]{:S(2)}, u32[]{:S(2)}) collective-permute-start(f32[16,640]{1,0:T(8,128)S(1)} %get-tuple-element.56), channel_id=1, source_target_pairs={{1,64},{2,65},{3,66},{4,67},{5,68},{6,69},{7,70},{8,71},{9,72},{10... | collective-permute-start | bytes 122888 | tf_op jit(solution)/shard_map/ppermute | solution.py:407
  51.4 2.2 %collective-permute-start.11 = (f32[16,640]{1,0:T(8,128)S(1)}, f32[16,640]{1,0:T(8,128)S(1)}, u32[]{:S(2)}, u32[]{:S(2)}) collective-permute-start(f32[16,640]{1,0:T(8,128)S(1)} %get-tuple-element.56), channel_id=1, source_target_pairs={{0,65},{1,66},{2,67},{3,68},{4,69},{5,70},{6,71},{7,72},{8,73},{9,... | collective-permute-start | bytes 122888 | tf_op jit(solution)/shard_map/ppermute | solution.py:407
  52.0 1.5 %collective-permute-start.10 = (f32[16,640]{1,0:T(8,128)S(1)}, f32[16,640]{1,0:T(8,128)S(1)}, u32[]{:S(2)}, u32[]{:S(2)}) collective-permute-start(f32[16,640]{1,0:T(8,128)S(1)} %get-tuple-element.56), channel_id=1, source_target_pairs={{0,64},{1,65},{2,66},{3,67},{4,68},{5,69},{6,70},{7,71},{8,72},{9,... | collective-permute-start | bytes 122888 | tf_op jit(solution)/shard_map/ppermute | solution.py:407
  53.6 2.0 %collective-permute-start.15 = (f32[16,640]{1,0:T(8,128)S(1)}, f32[16,640]{1,0:T(8,128)S(1)}, u32[]{:S(2)}, u32[]{:S(2)}) collective-permute-start(f32[16,640]{1,0:T(8,128)S(1)} %get-tuple-element.58), channel_id=1, source_target_pairs={{65,128},{66,129},{67,130},{68,131},{69,132},{70,133},{71,134},{72... | collective-permute-start | bytes 122888 | tf_op jit(solution)/shard_map/ppermute | solution.py:407
  54.3 1.4 %collective-permute-start.14 = (f32[16,640]{1,0:T(8,128)S(1)}, f32[16,640]{1,0:T(8,128)S(1)}, u32[]{:S(2)}, u32[]{:S(2)}) collective-permute-start(f32[16,640]{1,0:T(8,128)S(1)} %get-tuple-element.58), channel_id=1, source_target_pairs={{64,129},{65,130},{66,131},{67,132},{68,133},{69,134},{70,135},{71... | collective-permute-start | bytes 122888 | tf_op jit(solution)/shard_map/ppermute | solution.py:407
  55.7 2.0 %collective-permute-start.18 = (f32[16,640]{1,0:T(8,128)S(1)}, f32[16,640]{1,0:T(8,128)S(1)}, u32[]{:S(2)}, u32[]{:S(2)}) collective-permute-start(f32[16,640]{1,0:T(8,128)S(1)} %get-tuple-element.60), channel_id=1, source_target_pairs={{129,192},{130,193},{131,194},{132,195},{133,196},{134,197},{135,1... | collective-permute-start | bytes 122888 | tf_op jit(solution)/shard_map/ppermute | solution.py:407
  56.3 1.4 %collective-permute-start.17 = (f32[16,640]{1,0:T(8,128)S(1)}, f32[16,640]{1,0:T(8,128)S(1)}, u32[]{:S(2)}, u32[]{:S(2)}) collective-permute-start(f32[16,640]{1,0:T(8,128)S(1)} %get-tuple-element.60), channel_id=1, source_target_pairs={{128,193},{129,194},{130,195},{131,196},{132,197},{133,198},{134,1... | collective-permute-start | bytes 122888 | tf_op jit(solution)/shard_map/ppermute | solution.py:407
  57.9 2.0 %collective-permute-start.21 = (f32[16,640]{1,0:T(8,128)S(1)}, f32[16,640]{1,0:T(8,128)S(1)}, u32[]{:S(2)}, u32[]{:S(2)}) collective-permute-start(f32[16,640]{1,0:T(8,128)S(1)} %get-tuple-element.62), channel_id=1, source_target_pairs={{193,256},{194,257},{195,258},{196,259},{197,260},{198,261},{199,2... | collective-permute-start | bytes 122888 | tf_op jit(solution)/shard_map/ppermute | solution.py:407
  60.0 2.0 %collective-permute-start.24 = (f32[16,640]{1,0:T(8,128)S(1)}, f32[16,640]{1,0:T(8,128)S(1)}, u32[]{:S(2)}, u32[]{:S(2)}) collective-permute-start(f32[16,640]{1,0:T(8,128)S(1)} %get-tuple-element.64), channel_id=1, source_target_pairs={{257,320},{258,321},{259,322},{260,323},{261,324},{262,325},{263,3... | collective-permute-start | bytes 122888 | tf_op jit(solution)/shard_map/ppermute | solution.py:407
  62.1 2.0 %collective-permute-start.27 = (f32[16,640]{1,0:T(8,128)S(1)}, f32[16,640]{1,0:T(8,128)S(1)}, u32[]{:S(2)}, u32[]{:S(2)}) collective-permute-start(f32[16,640]{1,0:T(8,128)S(1)} %get-tuple-element.66), channel_id=1, source_target_pairs={{321,384},{322,385},{323,386},{324,387},{325,388},{326,389},{327,3... | collective-permute-start | bytes 122888 | tf_op jit(solution)/shard_map/ppermute | solution.py:407
  64.1 47.7 %collective-permute-start.30 = (f32[16,640]{1,0:T(8,128)S(1)}, f32[16,640]{1,0:T(8,128)S(1)}, u32[]{:S(2)}, u32[]{:S(2)}) collective-permute-start(f32[16,640]{1,0:T(8,128)S(1)} %get-tuple-element.68), channel_id=1, source_target_pairs={{385,448},{386,449},{387,450},{388,451},{389,452},{390,453},{391,4... | collective-permute-start | bytes 122888 | tf_op jit(solution)/shard_map/ppermute | solution.py:407
  65.4 48.6 %collective-permute-start.29 = (f32[16,640]{1,0:T(8,128)S(1)}, f32[16,640]{1,0:T(8,128)S(1)}, u32[]{:S(2)}, u32[]{:S(2)}) collective-permute-start(f32[16,640]{1,0:T(8,128)S(1)} %get-tuple-element.68), channel_id=1, source_target_pairs={{384,449},{385,450},{386,451},{387,452},{388,453},{389,454},{390,4... | collective-permute-start | bytes 122888 | tf_op jit(solution)/shard_map/ppermute | solution.py:407
  66.7 48.1 %collective-permute-start.28 = (f32[16,640]{1,0:T(8,128)S(1)}, f32[16,640]{1,0:T(8,128)S(1)}, u32[]{:S(2)}, u32[]{:S(2)}) collective-permute-start(f32[16,640]{1,0:T(8,128)S(1)} %get-tuple-element.68), channel_id=1, source_target_pairs={{384,448},{385,449},{386,450},{387,451},{388,452},{389,453},{390,4... | collective-permute-start | bytes 122888 | tf_op jit(solution)/shard_map/ppermute | solution.py:407
  117.7 10.2 %collective-permute-start.31 = (f32[8,16,512]{2,1,0:T(8,128)S(1)}, f32[8,16,512]{2,1,0:T(8,128)S(1)}, u32[]{:S(2)}, u32[]{:S(2)}) collective-permute-start(f32[8,16,512]{2,1,0:T(8,128)S(1)} %get-tuple-element.71), channel_id=1, source_target_pairs={{0,32},{32,0},{64,96},{96,64},{128,160},{160,128},{192,224},{224,1... | collective-permute-start | bytes 786440 | tf_op jit(solution)/shard_map/ppermute | solution.py:331
  (8 other events, 7.5 us)

commit v9 on v7

--- a/solution.py
+++ b/solution.py
@@ -36,24 +36,29 @@
     return lax.div(slab, 2), lax.rem(slab, 2), lax.axis_index("xy")
 
 
+def window_of(chip, core):
+    return lax.rem(chip + core, 2)
+
+
 def lane_of(shape=(FOLDS, LANES)):
     return lax.broadcasted_iota(jnp.int32, shape, len(shape) - 1)
 
 
-def column_mask(core):
+def column_mask(window):
     fold = lax.broadcasted_iota(jnp.int32, (FOLDS, LANES), 0)
-    column = 384 * core + STRIDE * fold + lane_of() - HALO
+    column = 384 * window + STRIDE * fold + lane_of() - HALO
     return (column >= 0) & (column < 1024)
 
 
 def fetch_kernel(design, own, partner, near, far, done):
-    unused, core, unused = place()
-    here = pl.ds(pl.multiple_of(256 * core, LANES), PART)
-    there = pl.ds(pl.multiple_of(256 * (1 - core), LANES), PART)
+    chip, core, unused = place()
+    window = window_of(chip, core)
+    here = pl.ds(pl.multiple_of(256 * window, LANES), PART)
+    there = pl.ds(pl.multiple_of(256 * (1 - window), LANES), PART)
     rim = pl.ds((8 - REACH) * core, REACH)
     copies = [
-        pltpu.make_async_copy(design.at[rim, :, here], far, done.at[0]),
-        pltpu.make_async_copy(design.at[rim, :, there], near, done.at[1]),
+        pltpu.make_async_copy(design.at[rim, :, there], far, done.at[0]),
+        pltpu.make_async_copy(design.at[rim, :, here], near, done.at[1]),
         pltpu.make_async_copy(design.at[:, :, there], partner, done.at[2]),
         pltpu.make_async_copy(design.at[:, :, here], own, done.at[3]),
     ]
@@ -89,7 +94,8 @@
 
 
 def fold_kernel(own, partner, near, far, out, to_down, to_up):
-    unused, core, unused = place()
+    chip, core, unused = place()
+    window = window_of(chip, core)
     lane = lane_of()
 
     def fold(source, base, count):
@@ -97,12 +103,12 @@
             for group in range(2):
                 tiles = []
                 for a in range(7):
-                    at = jnp.clip(a - 1 + core, 0, 5) * LANES
+                    at = jnp.clip(a - 1 + window, 0, 5) * LANES
                     tile = source[i, pl.ds(8 * group, 8), pl.ds(pl.multiple_of(at, LANES), LANES)]
                     if a == 0:
-                        tile = jnp.where(core == 0, 0.0, tile)
+                        tile = jnp.where(window == 0, 0.0, tile)
                     if a == 6:
-                        tile = jnp.where(core == 1, 0.0, tile)
+                        tile = jnp.where(window == 1, 0.0, tile)
                     tiles.append(tile)
                 row = ((base + i) * ROWS + 8 * group) * FOLDS
 
@@ -128,7 +134,7 @@
 
 def filter_kernel(count_chips, count_tiles, own, up, down, height, to_down, to_up, cells, first, second, packed):
     chip, core, tile = place()
-    inside = column_mask(core)
+    inside = column_mask(window_of(chip, core))
     scale = jnp.where(inside, 1.0 / (1.0 + 6.0 * FILTER_R2), 0.0)
     above = jnp.where(tile > 0, 1.0, 0.0)
     below = jnp.where(tile < count_tiles - 1, 1.0, 0.0)
@@ -198,7 +204,7 @@
 
 
 def widen_kernel(edge, rows, out):
-    unused, core, tile = place()
+    chip, core, tile = place()
     lane = lane_of()
     zero = jnp.zeros((8, LANES), jnp.float32)
     for group in range(MARGIN // 8):
@@ -208,7 +214,7 @@
             out[pl.ds(8 * group * FOLDS + s, 8, stride=FOLDS), :] = block
 
         fold_rows([zero, *tiles, zero], lane, store)
-    inside = column_mask(core) & (tile != edge)
+    inside = column_mask(window_of(chip, core)) & (tile != edge)
     for r in range(MARGIN):
         at = pl.ds(r * FOLDS, FOLDS)
         out[at, :] = jnp.where(inside, out[at, :], OUTSIDE)
@@ -224,7 +230,7 @@
 
     @pl.when(chip == turn)
     def run():
-        inside = column_mask(core)
+        inside = column_mask(window_of(chip, core))
         lane = lane_of()
         if turn:
             middle, up, down = received
@@ -274,7 +280,8 @@
 
 
 def unfold_kernel(scale, folded, own, partner):
-    unused, core, unused = place()
+    chip, core, unused = place()
+    window = window_of(chip, core)
     lane = lane_of()
 
     def unfold(target, base):
@@ -284,7 +291,7 @@
                 blocks = [folded[pl.ds(row + s, 8, stride=FOLDS), :] * scale for s in range(FOLDS)]
                 tiles = unfold_rows(blocks, lane)
                 for a in range(4):
-                    target[i, pl.ds(8 * group, 8), pl.ds(LANES * a, LANES)] = jnp.where(core == 0, tiles[a], tiles[a + 1])
+                    target[i, pl.ds(8 * group, 8), pl.ds(LANES * a, LANES)] = jnp.where(window == 0, tiles[a], tiles[a + 1])
             return carry
 
         lax.fori_loop(0, 8, layer, 0, unroll=8)
@@ -312,7 +319,8 @@
     slabs = lax.axis_size("gz")
     tiles = lax.axis_size("xy")
     chips = slabs // 2
-    unused, core, unused = place()
+    chip, core, unused = place()
+    window = window_of(chip, core)
 
     def at(slab, tile):
         return slab * tiles + tile
@@ -374,7 +382,7 @@
 
     def assemble(own, other):
         return jnp.where(
-            core == 0, jnp.concatenate([own, other], axis=2), jnp.concatenate([other, own], axis=2)
+            window == 0, jnp.concatenate([own, other], axis=2), jnp.concatenate([other, own], axis=2)
         )
 
     shown = spread(height, 1.0 / HALF, "blueprint")
@@ -397,7 +405,7 @@
                     top[0],
                     AXES,
                     [
-                        (at(2 * turn + c, t), at(2 * turn + 2 + c, t + away))
+                        (at(2 * turn + c, t), at(2 * turn + 3 - c, t + away))
                         for c in range(2)
                         for t in range(tiles)
                         if 0 <= t + away < tiles

time: 126 us -> 124 us (0.984)
  starting transfers between devices: 55.2 us -> 48.4 us
  waiting for transfers between devices: 58.5 us -> 62.6 us
    ppermute x3, starting transfers between devices: 16.4 us -> 9.58 us  [swap(): return lax.ppermute(block, 'gz', [(i, i ^ 1) for i in range(slabs)])]
    ppermute x21, waiting for transfers between devices: 47.4 us -> 51.5 us  [local(): lax.ppermute(top[0], AXES, [(at(2 * turn + c, t), at(2 * turn + 3 - c, t...]
where the time goes in v9:
time: 124 us; the launch traced here: 123 us
  waiting for transfers between devices  62.6 us (50%)
  starting transfers between devices  48.4 us (39%)
  Pallas kernels  9.01 us (7%)
  other arithmetic  1.69 us (1%)
    ppermute x21, waiting for transfers between devices, local(): lax.ppermute(top[0], AXES, [(at(2 * turn + c, t), at(2 * turn + 3 - c, t...  51.5 us
    ppermute x21, starting transfers between devices, local(): lax.ppermute(top[0], AXES, [(at(2 * turn + c, t), at(2 * turn + 3 - c, t...  15.8 us
    ppermute x2, starting transfers between devices, from_down(): return lax.ppermute(block, 'xy', [(i + 1, i) for i in range(tiles - 1)])  15.1 us
    ppermute x3, starting transfers between devices, swap(): return lax.ppermute(block, 'gz', [(i, i ^ 1) for i in range(slabs)])  9.58 us
    pallas_call x14, Pallas kernels, call(): pl.pallas_call(kernel, name=name, out_shape=[pltpu.VMEM(shape, jnp.float3...  7.69 us
    ppermute x2, starting transfers between devices, from_up(): return lax.ppermute(block, 'xy', [(i, i + 1) for i in range(tiles - 1)])  5.92 us
    ppermute x1, waiting for transfers between devices, local(): far = lax.ppermute(far, 'gz', straight)  5.72 us
  transfers between devices with their start and end apart: 30, of which 8 were waited for; matrix products, arithmetic and copies ran while one was open for 1% of the time, Pallas kernels for 1%

profile of v9, /device:TPU:63, one launch (start us, length us, event | category | flops | bytes accessed | tf_op | source)
XLA Modules:
  0.0 122.9 jit_solution(17765299034061132140)
XLA Ops:
  0.6 1.3 %fetch.1 = (f32[8,16,768]{2,1,0:T(8,128)S(1)}, f32[8,16,768]{2,1,0:T(8,128)S(1)}, f32[3,16,768]{2,1,0:T(8,128)S(1)}, f32[3,16,768]{2,1,0:T(8,128)S(1)}) custom-call(f32[8,16,1024]{2,1,0:T(8,128)} %design.1), custom_call_target="tpu_custom_call" | custom-call | tf_op jit(solution)/shard_map/fetch/pallas_call | solution.py:341
  2.0 2.6 %collective-permute-start = (f32[8,16,768]{2,1,0:T(8,128)S(1)}, f32[8,16,768]{2,1,0:T(8,128)S(1)}, u32[]{:S(2)}, u32[]{:S(2)}) collective-permute-start(f32[8,16,768]{2,1,0:T(8,128)S(1)} %get-tuple-element.36), channel_id=1, source_target_pairs={{0,32},{32,0},{64,96},{96,64},{128,160},{160,128},{192,224},{224,1... | collective-permute-start | bytes 1179656 | tf_op jit(solution)/shard_map/ppermute | solution.py:329
  5.2 1.3 %collective-permute-start.2 = (f32[3,16,768]{2,1,0:T(8,128)S(1)}, f32[3,16,768]{2,1,0:T(8,128)S(1)}, u32[]{:S(2)}, u32[]{:S(2)}) collective-permute-start(f32[3,16,768]{2,1,0:T(8,128)S(1)} %get-tuple-element.38), channel_id=1, source_target_pairs={{32,96},{64,0},{96,160},{128,64},{160,224},{192,128},{224,288},{25... | collective-permute-start | bytes 442376 | tf_op jit(solution)/shard_map/ppermute | solution.py:349
  6.5 5.7 %collective-permute-done.2.far = f32[3,16,768]{2,1,0:T(8,128)S(1)} collective-permute-done((f32[3,16,768]{2,1,0:T(8,128)S(1)}, f32[3,16,768]{2,1,0:T(8,128)S(1)}, u32[]{:S(2)}, u32[]{:S(2)}) %collective-permute-start.2) | collective-permute-done | bytes 147488 | tf_op jit(solution)/shard_map/ppermute | solution.py:349
  12.3 0.8 fold.1
  13.1 4.0 %collective-permute-start.3 = (f32[54,8,128]{2,1,0:T(8,128)S(1)}, f32[54,8,128]{2,1,0:T(8,128)S(1)}, u32[]{:S(2)}, u32[]{:S(2)}) collective-permute-start(f32[54,8,128]{2,1,0:T(8,128)S(1)} %get-tuple-element.40), channel_id=1, source_target_pairs={{0,1},{1,2},{2,3},{3,4},{4,5},{5,6},{6,7},{7,8},{8,9},{9,10},{10,1... | collective-permute-start | bytes 663560 | tf_op jit(solution)/shard_map/ppermute | solution.py:332
  17.1 8.9 %collective-permute-start.4 = (f32[54,8,128]{2,1,0:T(8,128)S(1)}, f32[54,8,128]{2,1,0:T(8,128)S(1)}, u32[]{:S(2)}, u32[]{:S(2)}) collective-permute-start(f32[54,8,128]{2,1,0:T(8,128)S(1)} %get-tuple-element.41), channel_id=1, source_target_pairs={{1,0},{2,1},{3,2},{4,3},{5,4},{6,5},{7,6},{8,7},{9,8},{10,9},{11,1... | collective-permute-start | bytes 663560 | tf_op jit(solution)/shard_map/ppermute | solution.py:335
  26.0 2.2 %collective-permute-done.3.up = f32[54,8,128]{2,1,0:T(8,128)S(1)} collective-permute-done((f32[54,8,128]{2,1,0:T(8,128)S(1)}, f32[54,8,128]{2,1,0:T(8,128)S(1)}, u32[]{:S(2)}, u32[]{:S(2)}) %collective-permute-start.3) | collective-permute-done | bytes 221216 | tf_op jit(solution)/shard_map/ppermute | solution.py:332
  28.2 0.9 collective-permute-done.4.down
  29.1 2.8 %filter.1 = (f32[16,16,8,128]{3,2,1,0:T(8,128)S(1)}, f32[120,640]{1,0:T(8,128)S(1)}, f32[120,640]{1,0:T(8,128)S(1)}) custom-call(f32[22,16,8,128]{3,2,1,0:T(8,128)S(1)} %bitcast.23, f32[54,8,128]{2,1,0:T(8,128)S(1)} %collective-permute-done.3.up, f32[54,8,128]{2,1,0:T(8,128)S(1)} %collective-permute-done.4.down), custom_call_target="tpu_custom_call" | custom-call | tf_op jit(solution)/shard_map/filter/pallas_call | solution.py:306
  31.8 1.9 %collective-permute-start.6 = (f32[120,640]{1,0:T(8,128)S(1)}, f32[120,640]{1,0:T(8,128)S(1)}, u32[]{:S(2)}, u32[]{:S(2)}) collective-permute-start(f32[120,640]{1,0:T(8,128)S(1)} %get-tuple-element.46), channel_id=1, source_target_pairs={{0,1},{1,2},{2,3},{3,4},{4,5},{5,6},{6,7},{7,8},{8,9},{9,10},{10,1... | collective-permute-start | bytes 921608 | tf_op jit(solution)/shard_map/ppermute | solution.py:332
  33.8 6.2 %collective-permute-start.7 = (f32[120,640]{1,0:T(8,128)S(1)}, f32[120,640]{1,0:T(8,128)S(1)}, u32[]{:S(2)}, u32[]{:S(2)}) collective-permute-start(f32[120,640]{1,0:T(8,128)S(1)} %get-tuple-element.47), channel_id=1, source_target_pairs={{1,0},{2,1},{3,2},{4,3},{5,4},{6,5},{7,6},{8,7},{9,8},{10,9},{11,1... | collective-permute-start | bytes 921608 | tf_op jit(solution)/shard_map/ppermute | solution.py:335
  40.3 4.7 %collective-permute-start.5 = (f32[8,16,512]{2,1,0:T(8,128)S(1)}, f32[8,16,512]{2,1,0:T(8,128)S(1)}, u32[]{:S(2)}, u32[]{:S(2)}) collective-permute-start(f32[8,16,512]{2,1,0:T(8,128)S(1)} %get-tuple-element.44), channel_id=1, source_target_pairs={{0,32},{32,0},{64,96},{96,64},{128,160},{160,128},{192,224},{224,1... | collective-permute-start | bytes 786440 | tf_op jit(solution)/shard_map/ppermute | solution.py:329
  45.1 1.1 collective-permute-done.5
  49.0 0.8 maximum_select_fusion
  60.4 1.3 %collective-permute-start.28 = (f32[16,640]{1,0:T(8,128)S(1)}, f32[16,640]{1,0:T(8,128)S(1)}, u32[]{:S(2)}, u32[]{:S(2)}) collective-permute-start(f32[16,640]{1,0:T(8,128)S(1)} %get-tuple-element.64), channel_id=1, source_target_pairs={{385,480},{386,481},{387,482},{388,483},{389,484},{390,485},{391,4... | collective-permute-start | bytes 122888 | tf_op jit(solution)/shard_map/ppermute | solution.py:404
  61.7 1.3 %collective-permute-start.27 = (f32[16,640]{1,0:T(8,128)S(1)}, f32[16,640]{1,0:T(8,128)S(1)}, u32[]{:S(2)}, u32[]{:S(2)}) collective-permute-start(f32[16,640]{1,0:T(8,128)S(1)} %get-tuple-element.64), channel_id=1, source_target_pairs={{384,481},{385,482},{386,483},{387,484},{388,485},{389,486},{390,4... | collective-permute-start | bytes 122888 | tf_op jit(solution)/shard_map/ppermute | solution.py:404
  63.0 1.3 %collective-permute-start.26 = (f32[16,640]{1,0:T(8,128)S(1)}, f32[16,640]{1,0:T(8,128)S(1)}, u32[]{:S(2)}, u32[]{:S(2)}) collective-permute-start(f32[16,640]{1,0:T(8,128)S(1)} %get-tuple-element.64), channel_id=1, source_target_pairs={{384,480},{385,481},{386,482},{387,483},{388,484},{389,485},{390,4... | collective-permute-start | bytes 122888 | tf_op jit(solution)/shard_map/ppermute | solution.py:404
  64.3 48.9 %collective-permute-done.28.refs_2_ = f32[16,640]{1,0:T(8,128)S(1)} collective-permute-done((f32[16,640]{1,0:T(8,128)S(1)}, f32[16,640]{1,0:T(8,128)S(1)}, u32[]{:S(2)}, u32[]{:S(2)}) %collective-permute-start.28) | collective-permute-done | bytes 40992 | tf_op jit(solution)/shard_map/ppermute | solution.py:404
  113.2 2.2 %collective-permute-done.27.refs_1_ = f32[16,640]{1,0:T(8,128)S(1)} collective-permute-done((f32[16,640]{1,0:T(8,128)S(1)}, f32[16,640]{1,0:T(8,128)S(1)}, u32[]{:S(2)}, u32[]{:S(2)}) %collective-permute-start.27) | collective-permute-done | bytes 40992 | tf_op jit(solution)/shard_map/ppermute | solution.py:404
  115.8 2.4 %chain.15 = f32[16,16,8,128]{3,2,1,0:T(8,128)S(1)} custom-call(f32[16,640]{1,0:T(8,128)S(1)} %collective-permute-done.26.refs_0_, f32[16,640]{1,0:T(8,128)S(1)} %collective-permute-done.27.refs_1_, f32[16,640]{1,0:T(8,128)S(1)} %collective-permute-done.28.refs_2_, ...), custom_call_target="tpu_custom_call", output_to_operand_aliasing={{}: (6, {})} | custom-call | tf_op jit(solution)/shard_map/chain/pallas_call | solution.py:306
  118.6 2.3 %collective-permute-start.29 = (f32[8,16,512]{2,1,0:T(8,128)S(1)}, f32[8,16,512]{2,1,0:T(8,128)S(1)}, u32[]{:S(2)}, u32[]{:S(2)}) collective-permute-start(f32[8,16,512]{2,1,0:T(8,128)S(1)} %get-tuple-element.67), channel_id=1, source_target_pairs={{0,32},{32,0},{64,96},{96,64},{128,160},{160,128},{192,224},{224,1... | collective-permute-start | bytes 786440 | tf_op jit(solution)/shard_map/ppermute | solution.py:329
  120.9 1.1 collective-permute-done.29
  122.1 0.8 maximum_select_fusion.1
  (54 shorter events, 14.8 us)
Async XLA Ops:
  2.0 10.3 %collective-permute-start = (f32[8,16,768]{2,1,0:T(8,128)S(1)}, f32[8,16,768]{2,1,0:T(8,128)S(1)}, u32[]{:S(2)}, u32[]{:S(2)}) collective-permute-start(f32[8,16,768]{2,1,0:T(8,128)S(1)} %get-tuple-element.36), channel_id=1, source_target_pairs={{0,32},{32,0},{64,96},{96,64},{128,160},{160,128},{192,224},{224,1... | collective-permute-start | bytes 1179656 | tf_op jit(solution)/shard_map/ppermute | solution.py:329
  4.5 2.0 %collective-permute-start.1 = (f32[3,16,768]{2,1,0:T(8,128)S(1)}, f32[3,16,768]{2,1,0:T(8,128)S(1)}, u32[]{:S(2)}, u32[]{:S(2)}) collective-permute-start(f32[3,16,768]{2,1,0:T(8,128)S(1)} %get-tuple-element.37), channel_id=1, source_target_pairs={{32,64},{64,32},{96,128},{128,96},{160,192},{192,160},{224,256},{2... | collective-permute-start | bytes 442376 | tf_op jit(solution)/shard_map/ppermute | solution.py:350
  5.2 7.0 %collective-permute-start.2 = (f32[3,16,768]{2,1,0:T(8,128)S(1)}, f32[3,16,768]{2,1,0:T(8,128)S(1)}, u32[]{:S(2)}, u32[]{:S(2)}) collective-permute-start(f32[3,16,768]{2,1,0:T(8,128)S(1)} %get-tuple-element.38), channel_id=1, source_target_pairs={{32,96},{64,0},{96,160},{128,64},{160,224},{192,128},{224,288},{25... | collective-permute-start | bytes 442376 | tf_op jit(solution)/shard_map/ppermute | solution.py:349
  13.1 15.1 %collective-permute-start.3 = (f32[54,8,128]{2,1,0:T(8,128)S(1)}, f32[54,8,128]{2,1,0:T(8,128)S(1)}, u32[]{:S(2)}, u32[]{:S(2)}) collective-permute-start(f32[54,8,128]{2,1,0:T(8,128)S(1)} %get-tuple-element.40), channel_id=1, source_target_pairs={{0,1},{1,2},{2,3},{3,4},{4,5},{5,6},{6,7},{7,8},{8,9},{9,10},{10,1... | collective-permute-start | bytes 663560 | tf_op jit(solution)/shard_map/ppermute | solution.py:332
  17.1 12.0 %collective-permute-start.4 = (f32[54,8,128]{2,1,0:T(8,128)S(1)}, f32[54,8,128]{2,1,0:T(8,128)S(1)}, u32[]{:S(2)}, u32[]{:S(2)}) collective-permute-start(f32[54,8,128]{2,1,0:T(8,128)S(1)} %get-tuple-element.41), channel_id=1, source_target_pairs={{1,0},{2,1},{3,2},{4,3},{5,4},{6,5},{7,6},{8,7},{9,8},{10,9},{11,1... | collective-permute-start | bytes 663560 | tf_op jit(solution)/shard_map/ppermute | solution.py:335
  31.8 14.4 %collective-permute-start.6 = (f32[120,640]{1,0:T(8,128)S(1)}, f32[120,640]{1,0:T(8,128)S(1)}, u32[]{:S(2)}, u32[]{:S(2)}) collective-permute-start(f32[120,640]{1,0:T(8,128)S(1)} %get-tuple-element.46), channel_id=1, source_target_pairs={{0,1},{1,2},{2,3},{3,4},{4,5},{5,6},{6,7},{7,8},{8,9},{9,10},{10,1... | collective-permute-start | bytes 921608 | tf_op jit(solution)/shard_map/ppermute | solution.py:332
  33.8 12.8 %collective-permute-start.7 = (f32[120,640]{1,0:T(8,128)S(1)}, f32[120,640]{1,0:T(8,128)S(1)}, u32[]{:S(2)}, u32[]{:S(2)}) collective-permute-start(f32[120,640]{1,0:T(8,128)S(1)} %get-tuple-element.47), channel_id=1, source_target_pairs={{1,0},{2,1},{3,2},{4,3},{5,4},{6,5},{7,6},{8,7},{9,8},{10,9},{11,1... | collective-permute-start | bytes 921608 | tf_op jit(solution)/shard_map/ppermute | solution.py:335
  40.3 5.8 %collective-permute-start.5 = (f32[8,16,512]{2,1,0:T(8,128)S(1)}, f32[8,16,512]{2,1,0:T(8,128)S(1)}, u32[]{:S(2)}, u32[]{:S(2)}) collective-permute-start(f32[8,16,512]{2,1,0:T(8,128)S(1)} %get-tuple-element.44), channel_id=1, source_target_pairs={{0,32},{32,0},{64,96},{96,64},{128,160},{160,128},{192,224},{224,1... | collective-permute-start | bytes 786440 | tf_op jit(solution)/shard_map/ppermute | solution.py:329
  47.0 2.9 %collective-permute-start.10 = (f32[16,640]{1,0:T(8,128)S(1)}, f32[16,640]{1,0:T(8,128)S(1)}, u32[]{:S(2)}, u32[]{:S(2)}) collective-permute-start(f32[16,640]{1,0:T(8,128)S(1)} %get-tuple-element.52), channel_id=1, source_target_pairs={{1,96},{2,97},{3,98},{4,99},{5,100},{6,101},{7,102},{8,103},{9,104... | collective-permute-start | bytes 122888 | tf_op jit(solution)/shard_map/ppermute | solution.py:404
  47.6 2.2 %collective-permute-start.9 = (f32[16,640]{1,0:T(8,128)S(1)}, f32[16,640]{1,0:T(8,128)S(1)}, u32[]{:S(2)}, u32[]{:S(2)}) collective-permute-start(f32[16,640]{1,0:T(8,128)S(1)} %get-tuple-element.52), channel_id=1, source_target_pairs={{0,97},{1,98},{2,99},{3,100},{4,101},{5,102},{6,103},{7,104},{8,10... | collective-permute-start | bytes 122888 | tf_op jit(solution)/shard_map/ppermute | solution.py:404
  48.3 1.5 %collective-permute-start.8 = (f32[16,640]{1,0:T(8,128)S(1)}, f32[16,640]{1,0:T(8,128)S(1)}, u32[]{:S(2)}, u32[]{:S(2)}) collective-permute-start(f32[16,640]{1,0:T(8,128)S(1)} %get-tuple-element.52), channel_id=1, source_target_pairs={{0,96},{1,97},{2,98},{3,99},{4,100},{5,101},{6,102},{7,103},{8,104... | collective-permute-start | bytes 122888 | tf_op jit(solution)/shard_map/ppermute | solution.py:404
  49.9 2.0 %collective-permute-start.13 = (f32[16,640]{1,0:T(8,128)S(1)}, f32[16,640]{1,0:T(8,128)S(1)}, u32[]{:S(2)}, u32[]{:S(2)}) collective-permute-start(f32[16,640]{1,0:T(8,128)S(1)} %get-tuple-element.54), channel_id=1, source_target_pairs={{65,160},{66,161},{67,162},{68,163},{69,164},{70,165},{71,166},{72... | collective-permute-start | bytes 122888 | tf_op jit(solution)/shard_map/ppermute | solution.py:404
  52.0 2.0 %collective-permute-start.16 = (f32[16,640]{1,0:T(8,128)S(1)}, f32[16,640]{1,0:T(8,128)S(1)}, u32[]{:S(2)}, u32[]{:S(2)}) collective-permute-start(f32[16,640]{1,0:T(8,128)S(1)} %get-tuple-element.56), channel_id=1, source_target_pairs={{129,224},{130,225},{131,226},{132,227},{133,228},{134,229},{135,2... | collective-permute-start | bytes 122888 | tf_op jit(solution)/shard_map/ppermute | solution.py:404
  52.6 1.4 %collective-permute-start.15 = (f32[16,640]{1,0:T(8,128)S(1)}, f32[16,640]{1,0:T(8,128)S(1)}, u32[]{:S(2)}, u32[]{:S(2)}) collective-permute-start(f32[16,640]{1,0:T(8,128)S(1)} %get-tuple-element.56), channel_id=1, source_target_pairs={{128,225},{129,226},{130,227},{131,228},{132,229},{133,230},{134,2... | collective-permute-start | bytes 122888 | tf_op jit(solution)/shard_map/ppermute | solution.py:404
  54.2 2.0 %collective-permute-start.19 = (f32[16,640]{1,0:T(8,128)S(1)}, f32[16,640]{1,0:T(8,128)S(1)}, u32[]{:S(2)}, u32[]{:S(2)}) collective-permute-start(f32[16,640]{1,0:T(8,128)S(1)} %get-tuple-element.58), channel_id=1, source_target_pairs={{193,288},{194,289},{195,290},{196,291},{197,292},{198,293},{199,2... | collective-permute-start | bytes 122888 | tf_op jit(solution)/shard_map/ppermute | solution.py:404
  54.9 1.4 %collective-permute-start.18 = (f32[16,640]{1,0:T(8,128)S(1)}, f32[16,640]{1,0:T(8,128)S(1)}, u32[]{:S(2)}, u32[]{:S(2)}) collective-permute-start(f32[16,640]{1,0:T(8,128)S(1)} %get-tuple-element.58), channel_id=1, source_target_pairs={{192,289},{193,290},{194,291},{195,292},{196,293},{197,294},{198,2... | collective-permute-start | bytes 122888 | tf_op jit(solution)/shard_map/ppermute | solution.py:404
  56.3 2.0 %collective-permute-start.22 = (f32[16,640]{1,0:T(8,128)S(1)}, f32[16,640]{1,0:T(8,128)S(1)}, u32[]{:S(2)}, u32[]{:S(2)}) collective-permute-start(f32[16,640]{1,0:T(8,128)S(1)} %get-tuple-element.60), channel_id=1, source_target_pairs={{257,352},{258,353},{259,354},{260,355},{261,356},{262,357},{263,3... | collective-permute-start | bytes 122888 | tf_op jit(solution)/shard_map/ppermute | solution.py:404
  57.0 1.4 %collective-permute-start.21 = (f32[16,640]{1,0:T(8,128)S(1)}, f32[16,640]{1,0:T(8,128)S(1)}, u32[]{:S(2)}, u32[]{:S(2)}) collective-permute-start(f32[16,640]{1,0:T(8,128)S(1)} %get-tuple-element.60), channel_id=1, source_target_pairs={{256,353},{257,354},{258,355},{259,356},{260,357},{261,358},{262,3... | collective-permute-start | bytes 122888 | tf_op jit(solution)/shard_map/ppermute | solution.py:404
  58.4 2.0 %collective-permute-start.25 = (f32[16,640]{1,0:T(8,128)S(1)}, f32[16,640]{1,0:T(8,128)S(1)}, u32[]{:S(2)}, u32[]{:S(2)}) collective-permute-start(f32[16,640]{1,0:T(8,128)S(1)} %get-tuple-element.62), channel_id=1, source_target_pairs={{321,416},{322,417},{323,418},{324,419},{325,420},{326,421},{327,4... | collective-permute-start | bytes 122888 | tf_op jit(solution)/shard_map/ppermute | solution.py:404
  59.0 1.4 %collective-permute-start.24 = (f32[16,640]{1,0:T(8,128)S(1)}, f32[16,640]{1,0:T(8,128)S(1)}, u32[]{:S(2)}, u32[]{:S(2)}) collective-permute-start(f32[16,640]{1,0:T(8,128)S(1)} %get-tuple-element.62), channel_id=1, source_target_pairs={{320,417},{321,418},{322,419},{323,420},{324,421},{325,422},{326,4... | collective-permute-start | bytes 122888 | tf_op jit(solution)/shard_map/ppermute | solution.py:404
  60.4 52.8 %collective-permute-start.28 = (f32[16,640]{1,0:T(8,128)S(1)}, f32[16,640]{1,0:T(8,128)S(1)}, u32[]{:S(2)}, u32[]{:S(2)}) collective-permute-start(f32[16,640]{1,0:T(8,128)S(1)} %get-tuple-element.64), channel_id=1, source_target_pairs={{385,480},{386,481},{387,482},{388,483},{389,484},{390,485},{391,4... | collective-permute-start | bytes 122888 | tf_op jit(solution)/shard_map/ppermute | solution.py:404
  61.7 53.7 %collective-permute-start.27 = (f32[16,640]{1,0:T(8,128)S(1)}, f32[16,640]{1,0:T(8,128)S(1)}, u32[]{:S(2)}, u32[]{:S(2)}) collective-permute-start(f32[16,640]{1,0:T(8,128)S(1)} %get-tuple-element.64), channel_id=1, source_target_pairs={{384,481},{385,482},{386,483},{387,484},{388,485},{389,486},{390,4... | collective-permute-start | bytes 122888 | tf_op jit(solution)/shard_map/ppermute | solution.py:404
  63.0 52.8 %collective-permute-start.26 = (f32[16,640]{1,0:T(8,128)S(1)}, f32[16,640]{1,0:T(8,128)S(1)}, u32[]{:S(2)}, u32[]{:S(2)}) collective-permute-start(f32[16,640]{1,0:T(8,128)S(1)} %get-tuple-element.64), channel_id=1, source_target_pairs={{384,480},{385,481},{386,482},{387,483},{388,484},{389,485},{390,4... | collective-permute-start | bytes 122888 | tf_op jit(solution)/shard_map/ppermute | solution.py:404
  118.6 3.4 %collective-permute-start.29 = (f32[8,16,512]{2,1,0:T(8,128)S(1)}, f32[8,16,512]{2,1,0:T(8,128)S(1)}, u32[]{:S(2)}, u32[]{:S(2)}) collective-permute-start(f32[8,16,512]{2,1,0:T(8,128)S(1)} %get-tuple-element.67), channel_id=1, source_target_pairs={{0,32},{32,0},{64,96},{96,64},{128,160},{160,128},{192,224},{224,1... | collective-permute-start | bytes 786440 | tf_op jit(solution)/shard_map/ppermute | solution.py:329
  (6 other events, 4.8 us)
